TPU v7x, 256 devices: a whole 4x4x8 slice. The times are simulated.
256 devices in a mesh: dp: 64 (over x, z, core), rep: 4 (over y).
Axes of the slice: x: 4, y: 4, z: 8, core: 2. Of those that a mesh axis runs over, the one named last changes fastest.
Arguments:
- embeddings: bfloat16 [262144, 768], P('dp'), as said below
- valid_rows: int32 [512], replicated, may hold values from 64 to 512, as said below
- pair_table: int32 [64, 64], replicated, may hold values from -1 to 63, as said below
Outputs:
- best_similarity: float32 [262144], P('dp')
Inputs may be any that keep to these rules, and one draw needn't show every extreme that they name: `embeddings`: embeddings are finite; rows need no particular norm. Block k holds valid_rows[k] valid rows, which come first in the block. `pair_table`: entry [a, b] is -1 or i * 8 + j, naming block i of device a and block j of device b; at most one of [a, b] and [b, a] is not -1, and the diagonal is -1.
All inputs are finite; a program needn't handle non-finite values.
Results may differ from a plain program's by a relative error of at most 0.00036.
Values may be sent and summed in bfloat16 or wider, within the bound.
No kernel may reach another device: no remote copies, remote signals or barrier semaphores. Data moves between devices by JAX's collectives and lax.ppermute only.
A program may use at most 128 MiB of HBM per device.

v0:
```python
import jax
import jax.numpy as jnp
from jax import lax
from jax.sharding import PartitionSpec as P

absent = -2.0
epsilon = 1e-06
per_round = 8


def similar(left, right):
    return lax.dot_general(
        left, right, (((1,), (1,)), ((), ())), preferred_element_type=jnp.float32
    )


def on_device(embeddings, valid_rows, pair_table):
    n_dp = lax.axis_size("dp")
    n_rep = lax.axis_size("rep")
    device = lax.axis_index("dp")
    quarter_id = lax.axis_index("rep")
    row_total, features = embeddings.shape
    blocks = valid_rows.shape[0] // n_dp
    block_rows = row_total // blocks
    quarter_len = block_rows // n_rep
    as_float = embeddings.astype(jnp.float32)
    unit_rows = (
        as_float * lax.rsqrt(jnp.sum(as_float * as_float, axis=1, keepdims=True) + epsilon)
    ).astype(jnp.bfloat16)
    unit_blocks = unit_rows.reshape(blocks, block_rows, features)
    own_counts = lax.dynamic_slice_in_dim(valid_rows, device * blocks, blocks)
    positions = jnp.arange(block_rows, dtype=jnp.int32)
    own_valid = positions[None, :] < own_counts[:, None]
    quarter_start = quarter_id * quarter_len
    quarter_units = lax.dynamic_slice_in_dim(unit_blocks, quarter_start, quarter_len, 1)
    quarter_valid = lax.dynamic_slice_in_dim(own_valid, quarter_start, quarter_len, 1)
    block_ids = jnp.arange(blocks, dtype=jnp.int32)
    peer_ids = jnp.arange(n_dp, dtype=jnp.int32)
    listed = lax.dynamic_index_in_dim(pair_table, device, 0, keepdims=False)
    listing = lax.dynamic_index_in_dim(pair_table, device, 1, keepdims=False)
    first_side = jnp.ones((n_dp,), jnp.bool_)
    take_listed = (listed >= 0) & first_side
    take_listing = (listing >= 0) & jnp.logical_not(first_side)
    recv_active = take_listed | take_listing
    recv_own = jnp.where(
        take_listed, listed // blocks, jnp.where(take_listing, listing % blocks, 0)
    )
    recv_partner = jnp.where(
        take_listed, listed % blocks, jnp.where(take_listing, listing // blocks, 0)
    )
    give_listing = (listing >= 0) & first_side
    give_listed = (listed >= 0) & jnp.logical_not(first_side)
    send_active = give_listing | give_listed
    send_block = jnp.where(
        give_listing, listing % blocks, jnp.where(give_listed, listed // blocks, 0)
    )
    outgoing = jnp.take(quarter_units, send_block, axis=0)
    outgoing = jnp.where(send_active[:, None, None], outgoing, jnp.zeros((), jnp.bfloat16))
    received = lax.all_to_all(outgoing, "dp", split_axis=0, concat_axis=0, tiled=True)
    partner_ids = peer_ids * blocks + recv_partner
    partner_counts = jnp.take(valid_rows, partner_ids)
    col_valid = (
        (quarter_start + jnp.arange(quarter_len, dtype=jnp.int32))[None, :]
        < partner_counts[:, None]
    ) & recv_active[:, None]
    ordered = jnp.argsort(jnp.where(recv_active, 0, 1).astype(jnp.int32), stable=True)
    live_count = jnp.sum(recv_active.astype(jnp.int32))
    rounds = (live_count + per_round - 1) // per_round

    def visit(round_id, running):
        row_best, col_best = running
        chosen = lax.dynamic_slice_in_dim(ordered, round_id * per_round, per_round)
        partner_units = jnp.take(received, chosen, axis=0)
        own_index = jnp.take(recv_own, chosen)
        own_units = jnp.take(unit_blocks, own_index, axis=0)
        scores = jnp.einsum(
            "grd,gcd->grc", own_units, partner_units, preferred_element_type=jnp.float32
        )
        active = jnp.take(recv_active, chosen)
        rows_ok = jnp.take(own_valid, own_index, axis=0) & active[:, None]
        cols_ok = jnp.take(col_valid, chosen, axis=0)
        row_max = jnp.max(jnp.where(cols_ok[:, None, :], scores, absent), axis=2)
        col_max = jnp.max(jnp.where(rows_ok[:, :, None], scores, absent), axis=1)
        own_hits = (own_index[:, None] == block_ids[None, :]) & active[:, None]
        row_best = jnp.maximum(
            row_best, jnp.max(jnp.where(own_hits[:, :, None], row_max[:, None, :], absent), axis=0)
        )
        slot_hits = chosen[:, None] == peer_ids[None, :]
        col_best = jnp.maximum(
            col_best, jnp.max(jnp.where(slot_hits[:, :, None], col_max[:, None, :], absent), axis=0)
        )
        return (row_best, col_best)

    row_init = jnp.full((blocks, block_rows), absent, jnp.float32)
    col_init = jnp.full((n_dp, quarter_len), absent, jnp.float32)
    row_best, col_best = lax.fori_loop(0, rounds, visit, (row_init, col_init))
    columns = quarter_units.reshape(blocks * quarter_len, features)
    columns_ok = quarter_valid.reshape(-1)
    column_rows = (
        block_ids[:, None] * block_rows
        + quarter_start
        + jnp.arange(quarter_len, dtype=jnp.int32)[None, :]
    ).reshape(-1)

    def one_block(block_item):
        rows_here, block_index = block_item
        scores = similar(rows_here, columns)
        row_index = block_index * block_rows + positions
        allowed = columns_ok[None, :] & (row_index[:, None] != column_rows[None, :])
        return jnp.max(jnp.where(allowed, scores, absent), axis=1)

    local_best = lax.map(one_block, (unit_blocks, block_ids))
    returned = lax.all_to_all(col_best, "dp", split_axis=0, concat_axis=0, tiled=True)
    owned = send_active[:, None] & (send_block[:, None] == block_ids[None, :])
    quarter_best = jnp.max(jnp.where(owned[:, :, None], returned[:, None, :], absent), axis=0)
    spread = lax.dynamic_update_slice_in_dim(row_init, quarter_best, quarter_start, 1)
    combined = jnp.maximum(jnp.maximum(row_best, local_best), spread)
    merged = lax.pmax(combined, "rep")
    return jnp.where(own_valid, merged, -1.0).reshape(-1)


def solution(mesh):
    return jax.shard_map(
        on_device,
        mesh=mesh,
        in_specs=(P("dp", None), P(), P()),
        out_specs=P("dp"),
        check_vma=False,
    )
```

profile of v0, /device:TPU:24, one launch (start us, length us, event | category | flops | bytes accessed | tf_op | source)
XLA Modules:
  0.0 493.5 jit_solution(11632760474741998687)
XLA Ops:
  0.0 4.1 fusion.24
  4.3 7.3 %fusion.25 = bf16[4096,768]{1,0:T(8,128)(2,1)} fusion(bf16[4096,768]{1,0:T(8,128)(2,1)} %param.7, f32[4096]{0:T(1024)S(1)} %add_rsqrt_fusion), kind=kLoop, calls=%fused_computation.50 | loop fusion | flops 9437184 | bytes 12599296 | tf_op jit(solution)/shard_map/convert_element_type | solution.py:29
  11.6 1.5 constant_dynamic-slice_fusion.1
  13.2 6.9 %gather_fusion.7 = bf16[64,128,768]{2,1,0:T(8,128)(2,1)} fusion(bf16[8,128,768]{2,1,0:T(8,128)(2,1)S(1)} %constant_dynamic-slice_fusion.1, s32[1024]{0:T(1024)S(1)} %pad_clamp_fusion.3), kind=kCustom, calls=%fused_computation.7 | custom fusion | bytes 25166080 | tf_op jit(solution)/shard_map/jit(_take)/gather | solution.py:57
  20.1 11.3 %select_select_fusion = bf16[64,128,768]{2,1,0:T(8,128)(2,1)} fusion(bf16[64,128,768]{2,1,0:T(8,128)(2,1)} %gather_fusion.7, pred[64]{0:T(512)(128)(4,1)S(1)} %get-tuple-element.255, pred[64]{0:T(512)(128)(4,1)S(1)} %get-tuple-element.261), kind=kLoop, calls=%fused_computation.51 | loop fusion | flops 12582912 | bytes 25165952 | tf_op jit(solution)/shard_map/jit(_where)/select_n | solution.py:58
  31.3 12.3 %all-to-all-start = ((bf16[64,128,768]{2,1,0:T(8,128)(2,1)}), bf16[64,128,768]{2,1,0:T(8,128)(2,1)}, u32[]{:S(2)}, u32[]{:S(2)}) async-start(bf16[64,128,768]{2,1,0:T(8,128)(2,1)} %select_select_fusion), calls=%async_computation | async-start | bytes 25165824 | tf_op jit(solution)/shard_map/all_to_all | solution.py:59
  43.7 0.8 gather_fusion.6
  44.5 0.7 and_select_fusion.2
  46.0 2.1 sort.17
  48.2 30.7 %while.25 = (s32[]{:T(128)}, f32[8,512]{1,0:T(8,128)S(1)}, pred[8,128]{1,0:T(8,128)(4,1)S(1)}, s32[8]{0:T(128)S(1)}, bf16[8,512,768]{2,1,0:T(8,128)(2,1)}, /*ind...) while((s32[]{:T(128)}, f32[8,512]{1,0:T(8,128)S(1)}, ...), condition=%wide.region_11.12_spmd.clone, body=%wide.region_9.11_spmd.clone.sunk | while | flops 807404544 | bytes 2378929 | solution.py:112
  48.3 0.7 dynamic_slice.51
  49.7 2.3 select_reduce_fusion.10
  52.1 0.7 dynamic_slice.51
  53.5 2.3 select_reduce_fusion.10
  55.9 0.7 dynamic_slice.51
  57.4 2.3 select_reduce_fusion.10
  59.8 0.7 dynamic_slice.51
  61.2 2.3 select_reduce_fusion.10
  63.6 0.7 dynamic_slice.51
  65.0 2.3 select_reduce_fusion.10
  67.4 0.7 dynamic_slice.51
  68.9 2.3 select_reduce_fusion.10
  71.3 0.7 dynamic_slice.51
  72.7 2.3 select_reduce_fusion.10
  75.1 0.7 dynamic_slice.51
  76.6 2.3 select_reduce_fusion.10
  78.9 239.5 %all-to-all-done = bf16[64,128,768]{2,1,0:T(8,128)(2,1)} async-done(((bf16[64,128,768]{2,1,0:T(8,128)(2,1)}), bf16[64,128,768]{2,1,0:T(8,128)(2,1)}, u32[]{:S(2)}, u32[]{:S(2)}) %all-to-all-start) | async-done | bytes 12582944 | tf_op jit(solution)/shard_map/all_to_all | solution.py:59
  319.1 122.9 %while.26 = (s32[]{:T(128)}, f32[8,512]{1,0:T(8,128)S(1)}, f32[64,128]{1,0:T(8,128)}, s32[]{:T(128)}, s32[64]{0:T(128)S(1)}, /*index=5*/s32[64]{0:T(128)S(1)}, p...) while((s32[]{:T(128)}, f32[8,512]{1,0:T(8,128)S(1)}, ...), condition=%wide.region_8.9_spmd.clone.clone, body=%wide.region_3.8_spmd.clone.clone.sunk | while | flops 811559744 | bytes 23879568 | solution.py:96
  319.2 0.6 gather_fusion.1
  319.9 0.6 gather_fusion
  322.1 5.2 %gather_fusion.4 = bf16[8,128,768]{2,1,0:T(8,128)(2,1)S(1)} fusion(bf16[64,128,768]{2,1,0:T(8,128)(2,1)} %get-tuple-element.435, s32[1024]{0:T(1024)S(1)} %pad_clamp_fusion.6), kind=kCustom, calls=%fused_computation.4.clone.clone.clone.1 | custom fusion | bytes 3145760 | tf_op jit(solution)/shard_map/while/body/jit(_take)/gather | solution.py:73
  327.3 6.3 %gather_fusion.5 = bf16[8,512,768]{2,1,0:T(8,128)(2,1)} fusion(bf16[8,512,768]{2,1,0:T(8,128)(2,1)} %get-tuple-element.434, s32[1024]{0:T(1024)S(1)} %pad_clamp_fusion.7), kind=kCustom, calls=%fused_computation.3.clone.clone.clone.1 | custom fusion | bytes 12582944 | tf_op jit(solution)/shard_map/while/body/jit(_take)/gather | solution.py:75
  333.7 4.3 select_reduce_fusion.11
  338.2 1.4 max.25
  339.7 0.6 gather_fusion.1
  340.3 0.6 gather_fusion
  342.6 5.2 %gather_fusion.4 = bf16[8,128,768]{2,1,0:T(8,128)(2,1)S(1)} fusion(bf16[64,128,768]{2,1,0:T(8,128)(2,1)} %get-tuple-element.435, s32[1024]{0:T(1024)S(1)} %pad_clamp_fusion.6), kind=kCustom, calls=%fused_computation.4.clone.clone.clone.1 | custom fusion | bytes 3145760 | tf_op jit(solution)/shard_map/while/body/jit(_take)/gather | solution.py:73
  347.8 6.3 %gather_fusion.5 = bf16[8,512,768]{2,1,0:T(8,128)(2,1)} fusion(bf16[8,512,768]{2,1,0:T(8,128)(2,1)} %get-tuple-element.434, s32[1024]{0:T(1024)S(1)} %pad_clamp_fusion.7), kind=kCustom, calls=%fused_computation.3.clone.clone.clone.1 | custom fusion | bytes 12582944 | tf_op jit(solution)/shard_map/while/body/jit(_take)/gather | solution.py:75
  354.2 4.3 select_reduce_fusion.11
  358.7 1.4 max.25
  360.8 0.6 gather_fusion
  363.1 5.2 %gather_fusion.4 = bf16[8,128,768]{2,1,0:T(8,128)(2,1)S(1)} fusion(bf16[64,128,768]{2,1,0:T(8,128)(2,1)} %get-tuple-element.435, s32[1024]{0:T(1024)S(1)} %pad_clamp_fusion.6), kind=kCustom, calls=%fused_computation.4.clone.clone.clone.1 | custom fusion | bytes 3145760 | tf_op jit(solution)/shard_map/while/body/jit(_take)/gather | solution.py:73
  368.3 6.3 %gather_fusion.5 = bf16[8,512,768]{2,1,0:T(8,128)(2,1)} fusion(bf16[8,512,768]{2,1,0:T(8,128)(2,1)} %get-tuple-element.434, s32[1024]{0:T(1024)S(1)} %pad_clamp_fusion.7), kind=kCustom, calls=%fused_computation.3.clone.clone.clone.1 | custom fusion | bytes 12582944 | tf_op jit(solution)/shard_map/while/body/jit(_take)/gather | solution.py:75
  374.6 4.3 select_reduce_fusion.11
  379.2 1.4 max.25
  380.7 0.6 gather_fusion.1
  381.3 0.6 gather_fusion
  383.6 5.2 %gather_fusion.4 = bf16[8,128,768]{2,1,0:T(8,128)(2,1)S(1)} fusion(bf16[64,128,768]{2,1,0:T(8,128)(2,1)} %get-tuple-element.435, s32[1024]{0:T(1024)S(1)} %pad_clamp_fusion.6), kind=kCustom, calls=%fused_computation.4.clone.clone.clone.1 | custom fusion | bytes 3145760 | tf_op jit(solution)/shard_map/while/body/jit(_take)/gather | solution.py:73
  388.8 6.3 %gather_fusion.5 = bf16[8,512,768]{2,1,0:T(8,128)(2,1)} fusion(bf16[8,512,768]{2,1,0:T(8,128)(2,1)} %get-tuple-element.434, s32[1024]{0:T(1024)S(1)} %pad_clamp_fusion.7), kind=kCustom, calls=%fused_computation.3.clone.clone.clone.1 | custom fusion | bytes 12582944 | tf_op jit(solution)/shard_map/while/body/jit(_take)/gather | solution.py:75
  395.1 4.3 select_reduce_fusion.11
  399.6 1.4 max.25
  401.8 0.6 gather_fusion
  404.0 5.2 %gather_fusion.4 = bf16[8,128,768]{2,1,0:T(8,128)(2,1)S(1)} fusion(bf16[64,128,768]{2,1,0:T(8,128)(2,1)} %get-tuple-element.435, s32[1024]{0:T(1024)S(1)} %pad_clamp_fusion.6), kind=kCustom, calls=%fused_computation.4.clone.clone.clone.1 | custom fusion | bytes 3145760 | tf_op jit(solution)/shard_map/while/body/jit(_take)/gather | solution.py:73
  409.3 6.3 %gather_fusion.5 = bf16[8,512,768]{2,1,0:T(8,128)(2,1)} fusion(bf16[8,512,768]{2,1,0:T(8,128)(2,1)} %get-tuple-element.434, s32[1024]{0:T(1024)S(1)} %pad_clamp_fusion.7), kind=kCustom, calls=%fused_computation.3.clone.clone.clone.1 | custom fusion | bytes 12582944 | tf_op jit(solution)/shard_map/while/body/jit(_take)/gather | solution.py:75
  415.6 4.3 select_reduce_fusion.11
  420.1 1.4 max.25
  422.3 0.6 gather_fusion
  424.5 5.2 %gather_fusion.4 = bf16[8,128,768]{2,1,0:T(8,128)(2,1)S(1)} fusion(bf16[64,128,768]{2,1,0:T(8,128)(2,1)} %get-tuple-element.435, s32[1024]{0:T(1024)S(1)} %pad_clamp_fusion.6), kind=kCustom, calls=%fused_computation.4.clone.clone.clone.1 | custom fusion | bytes 3145760 | tf_op jit(solution)/shard_map/while/body/jit(_take)/gather | solution.py:73
  429.8 6.3 %gather_fusion.5 = bf16[8,512,768]{2,1,0:T(8,128)(2,1)} fusion(bf16[8,512,768]{2,1,0:T(8,128)(2,1)} %get-tuple-element.434, s32[1024]{0:T(1024)S(1)} %pad_clamp_fusion.7), kind=kCustom, calls=%fused_computation.3.clone.clone.clone.1 | custom fusion | bytes 12582944 | tf_op jit(solution)/shard_map/while/body/jit(_take)/gather | solution.py:75
  436.1 4.3 select_reduce_fusion.11
  440.6 1.4 max.25
  442.0 27.3 %all-to-all-start.1 = ((f32[64,1,128]{2,1,0:T(1,128)}), f32[64,1,128]{2,1,0:T(1,128)S(1)}, u32[]{:S(2)}, u32[]{:S(2)}) async-start(f32[64,1,128]{2,1,0:T(1,128)} %bitcast.9), calls=%async_computation.1 | async-start | bytes 65536 | tf_op jit(solution)/shard_map/all_to_all | solution.py:113
  469.3 9.4 %all-to-all-done.1 = f32[64,1,128]{2,1,0:T(1,128)S(1)} async-done(((f32[64,1,128]{2,1,0:T(1,128)}), f32[64,1,128]{2,1,0:T(1,128)S(1)}, u32[]{:S(2)}, u32[]{:S(2)}) %all-to-all-start.1) | async-done | bytes 32800 | tf_op jit(solution)/shard_map/all_to_all | solution.py:113
  478.9 13.9 %pmax.7 = f32[8,512]{1,0:T(8,128)S(1)} all-reduce(f32[8,512]{1,0:T(8,128)S(1)} %maximum_maximum_fusion), channel_id=1, replica_groups=mesh['dp'=64,'rep'=4] {'rep'}, use_global_device_ids=true, to_apply=%region_13.14 | all-reduce | flops 4096 | bytes 32768 | tf_op jit(solution)/shard_map/pmax | solution.py:118
  (159 shorter events, 16.5 us)
Async XLA Ops:
  0.0 4.1 copy-start.1
  31.3 12.4 %copy-start = (s32[512]{0:T(512)S(1)}, s32[512]{0:T(512)}, u32[]{:S(2)}) copy-start(s32[512]{0:T(512)} %param.8) | copy-start | bytes 6148
  31.3 287.1 %all-to-all-start = ((bf16[64,128,768]{2,1,0:T(8,128)(2,1)}), bf16[64,128,768]{2,1,0:T(8,128)(2,1)}, u32[]{:S(2)}, u32[]{:S(2)}) async-start(bf16[64,128,768]{2,1,0:T(8,128)(2,1)} %select_select_fusion), calls=%async_computation | async-start | bytes 25165824 | tf_op jit(solution)/shard_map/all_to_all | solution.py:59
  442.0 36.8 %all-to-all-start.1 = ((f32[64,1,128]{2,1,0:T(1,128)}), f32[64,1,128]{2,1,0:T(1,128)S(1)}, u32[]{:S(2)}, u32[]{:S(2)}) async-start(f32[64,1,128]{2,1,0:T(1,128)} %bitcast.9), calls=%async_computation.1 | async-start | bytes 65536 | tf_op jit(solution)/shard_map/all_to_all | solution.py:113
where the time goes:
time: 498 us; the launch traced here: 494 us
  waiting for transfers between devices  249 us (50%)
  local copies, waits for them, and re-layouts  100 us (20%)
  matrix products  44.1 us (9%)
  starting transfers between devices  39.6 us (8%)
  other arithmetic  39.5 us (8%)
  blocking collectives  13.9 us (3%)
  loops' own time  6.21 us (1%)
    all_to_all x1, waiting for transfers between devices, on_device(): lax.all_to_all(outgoing, 'dp', split_axis=0, concat_axis=0, tiled=True)  240 us
    gather x6, local copies, waits for them, and re-layouts, visit(): own_units = jnp.take(unit_blocks, own_index, axis=0)  38.1 us
    gather x6, local copies, waits for them, and re-layouts, visit(): partner_units = jnp.take(received, chosen, axis=0)  31.3 us
    all_to_all x1, starting transfers between devices, on_device(): lax.all_to_all(col_best, 'dp', split_axis=0, concat_axis=0, tiled=True)  27.3 us
    dot_general x6, matrix products, visit(): jnp.einsum('grd,gcd->grc', own_units, partner_units, preferred_element_ty...  25.6 us
    dot_general x8, matrix products, similar(): lax.dot_general(left, right, (((1,), (1,)), ((), ())), preferred_element_...  18.5 us
    pmax x1, blocking collectives, on_device(): merged = lax.pmax(combined, 'rep')  13.9 us
    all_to_all x1, starting transfers between devices, on_device(): lax.all_to_all(outgoing, 'dp', split_axis=0, concat_axis=0, tiled=True)  12.3 us
  transfers between devices with their start and end apart: 2, of which 2 were waited for; matrix products, arithmetic and copies ran while one was open for 6% of the time, Pallas kernels for 0%

commit v1 on v0

v1 whole, which is shorter than its diff:
```python
import functools

import jax
import jax.numpy as jnp
from jax import lax
from jax.experimental import pallas as pl
from jax.experimental.pallas import tpu as pltpu
from jax.sharding import Mesh, PartitionSpec as P

absent = -2.0
epsilon = 1e-06
n_x, n_z, n_core, n_rep = 4, 8, 2, 4
chips = n_x * n_z
blocks = 8
rows = 512
quarter = rows // n_rep
width = 768
vmem_bytes = 60 << 20


def dot_t(left, right):
    return lax.dot_general(
        left, right, (((1,), (1,)), ((), ())), preferred_element_type=jnp.float32
    )


def normalise(raw):
    wide = raw.astype(jnp.float32)
    scale = lax.rsqrt(jnp.sum(wide * wide, axis=-1, keepdims=True) + epsilon)
    return (wide * scale).astype(jnp.bfloat16)


def place():
    return lax.axis_index("x"), lax.axis_index("z"), lax.axis_index("core"), lax.axis_index("rep")


def pair_info(table, source, target, core, many, which):
    side = which if many == 2 else jnp.where(source < target, core, 1 - core)
    forth = table[source * n_core + core, target * n_core + side]
    back = table[target * n_core + side, source * n_core + core]
    live = (forth >= 0) | (back >= 0)
    if many == 1:
        live = live & ((source != target) | (core == 0))
    source_block = jnp.where(forth >= 0, forth >> 3, back & 7)
    target_block = jnp.where(forth >= 0, forth & 7, (back >> 3) & 7)
    return live, side, source_block, target_block


def chip_at(x, z, dx, dz):
    return ((x + dx + n_x) & (n_x - 1)) * n_z + ((z + dz + n_z) & (n_z - 1))


first = [[(dx, 0, 1, 0), (dx, 1, 2, 0), (dx, 1, 2, 1)] for dx in range(n_x)]
second = [[(dx, 2, 2, 0), (dx, 2, 2, 1)] for dx in range(n_x)]
third = [[(dx, 3, 2, 0), (dx, 3, 2, 1)] for dx in range(n_x)]
far = [(dx, 4, 1, 0) for dx in range(n_x)]
stage_a = sum(first, [])
stage_b = sum(third + second, []) + far


def prep_kernel(table, emb, units, to0, to1, to2, to3, raw, unit, sem_in, sems):
    x, z, core, rep = place()
    load = pltpu.make_async_copy(emb.at[:, pl.ds(rep * quarter, quarter), :], raw, sem_in)
    load.start()
    load.wait()

    def one(b, carry):
        unit[b] = normalise(raw[b])
        return carry

    lax.fori_loop(0, blocks, one, 0)
    copies = [pltpu.make_async_copy(unit, units, sem_in)]
    copies[0].start()
    for dx, out in enumerate((to0, to1, to2, to3)):
        _, _, block, _ = pair_info(table, chip_at(x, z, 0, 0), chip_at(x, z, dx, 4), core, 1, 0)
        copies.append(pltpu.make_async_copy(unit.at[block], out.at[0], sems.at[dx]))
        copies[-1].start()
    for copy in copies:
        copy.wait()


def pick_kernel(wanted, sources, spread, table, *refs):
    held = dict(zip(sources, refs))
    parts, get_sems, put_sems = refs[-3:]
    x, z, core, rep = place()
    n = len(wanted)
    if spread:
        last = refs[-4]
        outs = list(refs[-n + n_x - 4 : -4]) + [last.at[(x + dx) & (n_x - 1)] for dx in range(n_x)]
    else:
        outs = refs[-n - 3 : -3]
    gone_of = max(sources)
    gets, puts = [], []
    for a, slots in enumerate(wanted):
        for place_in, (dx, dz, many, which) in enumerate(slots):
            gone = 0 if dz == 0 else gone_of
            source, target = chip_at(x, z, 0, -gone), chip_at(x, z, dx, dz - gone)
            _, _, block, _ = pair_info(table, source, target, core, many, which)
            come = held[gone].at[block]
            gets.append(
                pltpu.make_async_copy(come, parts.at[a, place_in], get_sems.at[3 * a + place_in])
            )
            gets[-1].start()
    left = list(gets)
    for a, (out, slots) in enumerate(zip(outs, wanted)):
        for _ in slots:
            left.pop(0).wait()
        puts.append(
            pltpu.make_async_copy(parts.at[a, pl.ds(0, len(slots))], out, put_sems.at[a])
        )
        puts[-1].start()
    for copy in puts:
        copy.wait()


def local_kernel(valid, own, sib, cols, unit_out, best):
    step = pl.program_id(0)
    x, z, core, rep = place()
    dev = chip_at(x, z, 0, 0) * n_core + core
    start = rep * quarter

    @pl.when(step >= blocks)
    def _():
        unit_out[0] = normalise(sib[0])

    @pl.when(step < blocks)
    def _():
        mine = normalise(own[0])
        unit_out[0] = mine
        part = lax.broadcasted_iota(jnp.int32, (quarter, rows), 0)
        gap = lax.broadcasted_iota(jnp.int32, (quarter, rows), 1) - part
        found = jnp.full((1, rows), absent, jnp.float32)
        for k in range(0, blocks, 2):
            pair = jnp.concatenate([cols[k], cols[k + 1]], axis=0)
            scores = dot_t(pair, mine)
            for half in range(2):
                count = valid[dev * blocks + k + half] - start
                own_gap = jnp.where(k + half == step, start, rows)
                allowed = (part < count) & (gap != own_gap)
                here = jnp.where(allowed, scores[half * quarter : (half + 1) * quarter], absent)
                found = jnp.maximum(found, jnp.max(here, axis=0, keepdims=True))
        best[pl.ds(step, 1), :] = found


def pair_kernel(stage, feeds, before, table, valid, own, *refs):
    past, refs = refs[: 2 * len(before)], refs[2 * len(before) :]
    arrays, scratch = refs, refs[-8:]
    units, held, cols, many, listed, owner, sem_u, sem_g = scratch
    outs = refs[-10:-8] if not before else refs[-11:-8]
    slots = len(stage)
    x, z, core, rep = place()
    chip = chip_at(x, z, 0, 0)
    start = rep * quarter
    gets = []
    for a, (array, dx, count, base) in enumerate(feeds):
        came = arrays[array] if dx is None else arrays[array].at[(x - dx + n_x) & (n_x - 1)]
        gets.append(pltpu.make_async_copy(came, held.at[pl.ds(base, count)], sem_g.at[a]))
        gets[-1].start()
    row_out = outs[0]
    row_out[...] = jnp.full((2 * blocks, rows), absent, jnp.float32)
    for ref in past[::2]:
        row_out[...] = jnp.maximum(row_out[...], ref[...])
    cols[...] = jnp.full(cols.shape, absent, jnp.float32)
    for o in range(2 * blocks):
        many[o] = 0
    for slot, (dx, dz, m, which) in enumerate(stage):
        source = chip_at(x, z, -dx, -dz)
        live, side, source_block, target_block = pair_info(table, source, chip, core, m, which)
        mine = jnp.where(side == core, 0, blocks) + target_block
        filled = many[mine]
        listed[mine, filled] = jnp.where(live, slot, slots)
        listed[mine, filled + 1] = slots
        many[mine] = filled + live.astype(jnp.int32)
        owner[slot] = valid[(source * n_core + core) * blocks + source_block] - start
    owner[slots] = 0
    loads = []
    for o in range(2 * blocks):
        loads.append(pltpu.make_async_copy(own.at[o], units.at[o], sem_u.at[o]))

        @pl.when(many[o] > 0)
        def _():
            loads[o].start()

    part = lax.broadcasted_iota(jnp.int32, (quarter, rows), 0)
    lane = lax.broadcasted_iota(jnp.int32, (2 * quarter, rows), 1)
    for copy in gets:
        copy.wait()
    for o in range(2 * blocks):
        own_dev = chip * n_core + (core if o < blocks else 1 - core)
        own_count = valid[own_dev * blocks + o % blocks]

        @pl.when(many[o] > 0)
        def _():
            loads[o].wait()

        def visit(turn, carry):
            pair = [listed[o, 2 * turn], listed[o, 2 * turn + 1]]
            here_slot = [pair[0], jnp.minimum(pair[1], slots - 1)]
            scores = dot_t(
                jnp.concatenate([held[here_slot[0]], held[here_slot[1]]], axis=0), units[o]
            )
            ok = jnp.where(lane < own_count, scores, absent)
            folded = jnp.maximum(
                jnp.maximum(ok[:, 0:128], ok[:, 128:256]), jnp.maximum(ok[:, 256:384], ok[:, 384:512])
            )
            top = row_out[o : o + 1, :]
            for half in range(2):
                span = slice(half * quarter, (half + 1) * quarter)
                here = jnp.where(part < owner[pair[half]], scores[span], absent)
                top = jnp.maximum(top, jnp.max(here, axis=0, keepdims=True))
                cols[pl.ds(pair[half], 1), :] = jnp.max(folded[span].T, axis=0, keepdims=True)
            row_out[o : o + 1, :] = top
            return carry

        lax.fori_loop(0, (many[o] + 1) >> 1, visit, 0)
    col_out = outs[1]
    if not before:
        col_out[...] = cols[0:slots]
    else:
        outs[2][...] = row_out[blocks:]
        col_out[...] = jnp.full(col_out.shape, absent, jnp.float32)
        for done, ref in zip(before + [stage], list(past[1::2]) + [cols]):
            for slot, (dx, dz, _, which) in enumerate(done):
                col_out[pl.ds(2 * chip_at(x, z, -dx, -dz) + which, 1), :] = ref[slot : slot + 1, :]


def spread_in(running, best, rep):
    wide = jnp.concatenate([best] * n_rep, axis=1)
    lane = lax.broadcasted_iota(jnp.int32, (blocks, rows), 1)
    mine = (lane >= rep * quarter) & (lane < (rep + 1) * quarter)
    return jnp.where(mine, jnp.maximum(running, wide), running)


def merge_kernel(table, local, row_best, sib_rows, back, out, best):
    x, z, core, rep = place()
    best[...] = jnp.full((blocks, quarter), absent, jnp.float32)
    for dx, dz, many, which in stage_a + stage_b:
        target = chip_at(x, z, dx, dz)
        _, _, block, _ = pair_info(table, chip_at(x, z, 0, 0), target, core, many, which)
        best[pl.ds(block, 1), :] = jnp.maximum(
            best[pl.ds(block, 1), :], back[pl.ds(2 * target + which, 1), :]
        )
    merged = jnp.maximum(jnp.maximum(local[...], row_best[0:blocks]), sib_rows[...])
    mine = spread_in(merged, best[...], rep)
    for y in range(n_rep):
        out[y] = mine


def finish_kernel(valid, got, out):
    x, z, core, _ = place()
    dev = chip_at(x, z, 0, 0) * n_core + core
    best = jnp.max(got[...], axis=0)
    lane = lax.broadcasted_iota(jnp.int32, (1, quarter), 1)
    for b in range(blocks):
        count = valid[dev * blocks + b]
        for q in range(n_rep):
            span = best[b : b + 1, q * quarter : (q + 1) * quarter]
            out[n_rep * b + q : n_rep * b + q + 1, :] = jnp.where(
                lane + q * quarter < count, span, -1.0
            )


def move(value, dx, dz):
    if dx % n_x == 0 and dz % n_z == 0:
        return value
    steps = [
        (x * n_z + z, (x + dx) % n_x * n_z + (z + dz) % n_z) for x in range(n_x) for z in range(n_z)
    ]
    return lax.ppermute(value, ("x", "z"), steps)


def on_device(embeddings, valid_rows, pair_table):
    smem = pl.BlockSpec(memory_space=pltpu.SMEM)
    vmem = pl.BlockSpec(memory_space=pltpu.VMEM)
    hbm = pl.BlockSpec(memory_space=pl.ANY)
    params = pltpu.CompilerParams(vmem_limit_bytes=vmem_bytes)
    cost = pl.CostEstimate(flops=0, bytes_accessed=1 << 16, transcendentals=0)
    f32, bf16 = jnp.float32, jnp.bfloat16
    part = (quarter, width)
    raw = embeddings.reshape(blocks, rows, width)

    def pick(wanted, sources, spread, held, after, name):
        n = len(wanted)
        shapes = [(len(slots),) + part for slots in wanted]
        if spread:
            shapes = shapes[:-n_x] + [(n_x,) + shapes[-1]]
        return pl.pallas_call(
            functools.partial(pick_kernel, wanted, sources, spread),
            out_shape=[jax.ShapeDtypeStruct(shape, bf16) for shape in shapes],
            in_specs=[smem] + [hbm] * len(held + after),
            out_specs=[hbm] * len(shapes),
            scratch_shapes=[
                pltpu.VMEM((n, 3) + part, bf16),
                pltpu.SemaphoreType.DMA((3 * n,)),
                pltpu.SemaphoreType.DMA((n,)),
            ],
            compiler_params=params,
            cost_estimate=cost,
            name=name,
        )(pair_table, *held, *after)

    def compare(stage, feeds, arrays, before, past, after, name):
        slots = len(stage)
        shapes = [(2 * blocks, rows), (slots, quarter)]
        if before:
            shapes = [(2 * blocks, rows), (2 * chips, quarter), (blocks, rows)]
        return pl.pallas_call(
            functools.partial(pair_kernel, stage, feeds, before),
            out_shape=[jax.ShapeDtypeStruct(shape, f32) for shape in shapes],
            in_specs=[smem, smem, hbm] + [vmem] * len(past) + [hbm] * len(arrays + after),
            out_specs=[vmem] * len(shapes),
            scratch_shapes=[
                pltpu.VMEM((2 * blocks, rows, width), bf16),
                pltpu.VMEM((slots,) + part, bf16),
                pltpu.VMEM((slots // 8 * 8 + 8, quarter), f32),
                pltpu.SMEM((2 * blocks,), jnp.int32),
                pltpu.SMEM((2 * blocks, slots + 2), jnp.int32),
                pltpu.SMEM((slots + 1,), jnp.int32),
                pltpu.SemaphoreType.DMA((2 * blocks,)),
                pltpu.SemaphoreType.DMA((len(feeds),)),
            ],
            compiler_params=params,
            cost_estimate=cost,
            name=name,
        )(pair_table, valid_rows, units, *past, *arrays, *after)

    cols, *away = pl.pallas_call(
        prep_kernel,
        out_shape=[
            jax.ShapeDtypeStruct((blocks,) + part, bf16),
        ]
        + [jax.ShapeDtypeStruct((1,) + part, bf16)] * n_x,
        in_specs=[smem, hbm],
        out_specs=[hbm] * (1 + n_x),
        scratch_shapes=[
            pltpu.VMEM((blocks,) + part, bf16),
            pltpu.VMEM((blocks,) + part, bf16),
            pltpu.SemaphoreType.DMA,
            pltpu.SemaphoreType.DMA((n_x,)),
        ],
        compiler_params=params,
        cost_estimate=cost,
        name="prep",
    )(pair_table, raw)
    swap = [(0, 1), (1, 0)]
    sib_raw = lax.ppermute(raw, "core", swap)
    hop1 = move(cols, 0, 1)
    away = jnp.concatenate([move(a, dx, 0) for dx, a in enumerate(away)], axis=0)
    units, local_best = pl.pallas_call(
        local_kernel,
        grid=(2 * blocks,),
        out_shape=(
            jax.ShapeDtypeStruct((2 * blocks, rows, width), bf16),
            jax.ShapeDtypeStruct((blocks, rows), f32),
        ),
        in_specs=[
            smem,
            pl.BlockSpec((1, rows, width), lambda i: (jnp.minimum(i, blocks - 1), 0, 0)),
            pl.BlockSpec((1, rows, width), lambda i: (jnp.maximum(i - blocks, 0), 0, 0)),
            pl.BlockSpec((blocks,) + part, lambda i: (0, 0, 0)),
        ],
        out_specs=(
            pl.BlockSpec((1, rows, width), lambda i: (i, 0, 0)),
            pl.BlockSpec((blocks, rows), lambda i: (0, 0)),
        ),
        compiler_params=params,
        cost_estimate=cost,
        name="local",
    )(valid_rows, raw, sib_raw, cols)
    hop1, away, local_best = lax.optimization_barrier((hop1, away, local_best))
    hop2 = move(hop1, 0, 1)
    away = move(away, 0, -2)
    picked = pick(first, (0, 1), False, [cols, hop1], [], "pick_a")
    first_in = [move(a, dx, 0) for dx, a in enumerate(picked)]
    hop2, away = lax.optimization_barrier((hop2, away))
    picked = pick(third + second, (2,), True, [hop2], first_in, "pick_b")
    away = move(away, 0, -2)
    third_in = [move(a, dx, 1) for dx, a in enumerate(picked[:n_x])]
    second_in = lax.all_to_all(picked[n_x], "x", split_axis=0, concat_axis=0, tiled=True)

    past_a = compare(
        stage_a,
        [(dx, None, 3, 3 * dx) for dx in range(n_x)],
        first_in,
        [],
        [],
        [picked[0]],
        "pairs_a",
    )
    row_best, col_best, sib_best = compare(
        stage_b,
        [(dx, None, 2, 2 * dx) for dx in range(n_x)]
        + [(n_x, dx, 2, 2 * n_x + 2 * dx) for dx in range(n_x)]
        + [(n_x + 1, None, n_x, 4 * n_x)],
        third_in + [second_in, away],
        [stage_a],
        past_a,
        [],
        "pairs_b",
    )
    sib_rows = lax.ppermute(sib_best, "core", swap)
    back = lax.all_to_all(col_best, ("x", "z"), split_axis=0, concat_axis=0, tiled=True)
    shared = pl.pallas_call(
        merge_kernel,
        out_shape=jax.ShapeDtypeStruct((n_rep, blocks, rows), f32),
        in_specs=[smem, vmem, vmem, vmem, vmem],
        out_specs=vmem,
        scratch_shapes=[pltpu.VMEM((blocks, quarter), f32)],
        cost_estimate=cost,
        name="merge",
    )(pair_table, local_best, row_best, sib_rows, back)
    shared = lax.all_to_all(shared, "rep", split_axis=0, concat_axis=0, tiled=True)
    result = pl.pallas_call(
        finish_kernel,
        out_shape=jax.ShapeDtypeStruct((blocks * n_rep, quarter), f32),
        in_specs=[smem, vmem],
        out_specs=vmem,
        cost_estimate=cost,
        name="finish",
    )(valid_rows, shared)
    return result.reshape(-1)


def solution(mesh):
    grid = Mesh(mesh.devices.reshape(n_x, n_z, n_core, n_rep), ("x", "z", "core", "rep"))
    return jax.shard_map(
        on_device,
        mesh=grid,
        in_specs=(P(("x", "z", "core"), None), P(), P()),
        out_specs=P(("x", "z", "core")),
        check_vma=False,
    )
```

time: 498 us -> 184 us (0.37)
  waiting for transfers between devices: 249 us -> 64.2 us
  local copies, waits for them, and re-layouts: 100 us -> 3.94 us
  Pallas kernels: 0 us -> 61.1 us
  matrix products: 44.1 us -> 0 us
  other arithmetic: 39.5 us -> 1.03 us
  loops' own time: 6.21 us -> 0 us
  blocking collectives: 13.9 us -> 8.35 us
    all_to_all x2, waiting for transfers between devices: 249 us -> 8.36 us  [the longest x1 8.36 us: on_device(): lax.all_to_all(col_best, ('x', 'z'), split_axis=0, concat_axis=0, tiled=T...]
    gather x38 -> x0, local copies, waits for them, and re-layouts: 91.7 us -> none  [the longest x6 38.1 us: visit(): own_units = jnp.take(unit_blocks, own_index, axis=0)]
    pallas_call x0 -> x8, Pallas kernels: none -> 61.1 us  [the longest x1 21.8 us: on_device(): pl.pallas_call(local_kernel, grid=(2 * blocks,), out_shape=(jax.ShapeDtyp...]
    ppermute x0 -> x16, waiting for transfers between devices: none -> 55.8 us  [the longest x14 54.4 us: move(): return lax.ppermute(value, ('x', 'z'), steps)]
    dot_general x14 -> x0, matrix products: 44.1 us -> none  [the longest x6 25.6 us: visit(): jnp.einsum('grd,gcd->grc', own_units, partner_units, preferred_element_ty...]
    ppermute x0 -> x16, starting transfers between devices: none -> 27.4 us  [the longest x14 27.3 us: move(): return lax.ppermute(value, ('x', 'z'), steps)]
    all_to_all x2, starting transfers between devices: 39.6 us -> 14.8 us  [the longest x1 10.4 us: on_device(): lax.all_to_all(col_best, ('x', 'z'), split_axis=0, concat_axis=0, tiled=T...]
    pmax x1 -> x0, blocking collectives: 13.9 us -> none  [on_device(): merged = lax.pmax(combined, 'rep')]
  transfers between devices with their start and end apart: 2 -> 18, of which waited for: 2 -> 10; matrix products, arithmetic and copies ran while one was open for 6% -> 1% of each run, Pallas kernels for 0% -> 22%
where the time goes in v1:
time: 184 us; the launch traced here: 181 us
  waiting for transfers between devices  64.2 us (35%)
  Pallas kernels  61.1 us (33%)
  starting transfers between devices  42.2 us (23%)
  blocking collectives  8.35 us (5%)
  local copies, waits for them, and re-layouts  3.94 us (2%)
    ppermute x14, waiting for transfers between devices, move(): return lax.ppermute(value, ('x', 'z'), steps)  54.4 us
    ppermute x14, starting transfers between devices, move(): return lax.ppermute(value, ('x', 'z'), steps)  27.3 us
    pallas_call x1, Pallas kernels, on_device(): pl.pallas_call(local_kernel, grid=(2 * blocks,), out_shape=(jax.ShapeDtyp...  21.8 us
    pallas_call x2, Pallas kernels, compare(): pl.pallas_call(functools.partial(pair_kernel, stage, feeds, before), out_...  21.2 us
    all_to_all x1, starting transfers between devices, on_device(): lax.all_to_all(col_best, ('x', 'z'), split_axis=0, concat_axis=0, tiled=T...  10.4 us
    pallas_call x2, Pallas kernels, pick(): pl.pallas_call(functools.partial(pick_kernel, wanted, sources, spread), o...  9.37 us
    all_to_all x1, waiting for transfers between devices, on_device(): lax.all_to_all(col_best, ('x', 'z'), split_axis=0, concat_axis=0, tiled=T...  8.36 us
    all_to_all x1, blocking collectives, on_device(): lax.all_to_all(shared, 'rep', split_axis=0, concat_axis=0, tiled=True)  8.35 us
  transfers between devices with their start and end apart: 18, of which 10 were waited for; matrix products, arithmetic and copies ran while one was open for 1% of the time, Pallas kernels for 22%

profile of v1, /device:TPU:24, one launch (start us, length us, event | category | flops | bytes accessed | tf_op | source)
XLA Modules:
  0.0 180.9 jit_solution(17742055011950676623)
XLA Ops:
  0.0 0.0 collective-permute-start.4
  0.0 5.0 %prep.1 = (bf16[8,128,768]{2,1,0:T(8,128)(2,1)}, bf16[1,128,768]{2,1,0:T(8,128)(2,1)}, bf16[1,128,768]{2,1,0:T(8,128)(2,1)}, bf16[1,128,768]{2,1,0:T(8,128)(2,1)}, bf16[1,128,768]{2,1,0:T(8,128)(2,1)}) custom-call(s32[64,64]{1,0:T(8,128)} %table.11, bf16[8,512,768]{2,1,0:T(8,128)(2,1)} %bitcast.5), custom_call_target="tpu_custom_call" | custom-call | bytes 65536 | tf_op jit(solution)/shard_map/prep/pallas_call | solution.py:327
  5.1 2.0 %collective-permute-start = (bf16[8,128,768]{2,1,0:T(8,128)(2,1)}, bf16[8,128,768]{2,1,0:T(8,128)(2,1)S(1)}, u32[]{:S(2)}, u32[]{:S(2)}) collective-permute-start(bf16[8,128,768]{2,1,0:T(8,128)(2,1)} %get-tuple-element.31.cols.refs_0_), channel_id=1, source_target_pairs={{0,8},{8,16},{16,24},{24,32},{32,40},{40,48},{48,56},{56,0},{64,72... | collective-permute-start | bytes 4718600 | tf_op jit(solution)/shard_map/ppermute | solution.py:269
  7.1 1.5 collective-permute-start.1
  8.5 2.7 %collective-permute-start.2 = (bf16[1,128,768]{2,1,0:T(8,128)(2,1)}, bf16[1,128,768]{2,1,0:T(8,128)(2,1)S(1)}, u32[]{:S(2)}, u32[]{:S(2)}) collective-permute-start(bf16[1,128,768]{2,1,0:T(8,128)(2,1)} %get-tuple-element.34), channel_id=1, source_target_pairs={{0,128},{8,136},{16,144},{24,152},{32,160},{40,168},{48,176},{56,1... | collective-permute-start | bytes 589832 | tf_op jit(solution)/shard_map/ppermute | solution.py:269
  11.3 1.4 collective-permute-start.3
  12.7 2.8 %collective-permute-done.1 = bf16[1,128,768]{2,1,0:T(8,128)(2,1)S(1)} collective-permute-done((bf16[1,128,768]{2,1,0:T(8,128)(2,1)}, bf16[1,128,768]{2,1,0:T(8,128)(2,1)S(1)}, u32[]{:S(2)}, u32[]{:S(2)}) %collective-permute-start.1) | collective-permute-done | bytes 196640 | tf_op jit(solution)/shard_map/ppermute | solution.py:269
  15.5 5.2 %collective-permute-done.2 = bf16[1,128,768]{2,1,0:T(8,128)(2,1)S(1)} collective-permute-done((bf16[1,128,768]{2,1,0:T(8,128)(2,1)}, bf16[1,128,768]{2,1,0:T(8,128)(2,1)S(1)}, u32[]{:S(2)}, u32[]{:S(2)}) %collective-permute-start.2) | collective-permute-done | bytes 196640 | tf_op jit(solution)/shard_map/ppermute | solution.py:269
  20.7 0.0 collective-permute-done.3
  20.7 1.0 pad_maximum_fusion
  21.7 0.0 collective-permute-done.4.sib
  21.8 21.8 %local.1 = (bf16[16,512,768]{2,1,0:T(8,128)(2,1)}, f32[8,512]{1,0:T(8,128)}) custom-call(s32[512]{0:T(512)} %valid.7, bf16[8,512,768]{2,1,0:T(8,128)(2,1)} %bitcast.6, bf16[8,512,768]{2,1,0:T(8,128)(2,1)} %collective-permute-done.4.sib, bf16[8,128,768]{2,1,0:T(8,128)(2,1)} %get-tuple-element.31.cols.refs_0_), custom_call_target="tpu_custom_call" | custom-call | bytes 65536 | tf_op jit(solution)/shard_map/local/pallas_call | solution.py:349
  43.5 2.8 %collective-permute-done.refs_1_ = bf16[8,128,768]{2,1,0:T(8,128)(2,1)S(1)} collective-permute-done((bf16[8,128,768]{2,1,0:T(8,128)(2,1)}, bf16[8,128,768]{2,1,0:T(8,128)(2,1)S(1)}, u32[]{:S(2)}, u32[]{:S(2)}) %collective-permute-start) | collective-permute-done | bytes 1572896 | tf_op jit(solution)/shard_map/ppermute | solution.py:269
  46.3 0.0 collective-permute-start.8
  46.3 3.2 %collective-permute-start.9 = (bf16[4,128,768]{2,1,0:T(8,128)(2,1)S(1)}, bf16[4,128,768]{2,1,0:T(8,128)(2,1)}, u32[]{:S(2)}, u32[]{:S(2)}) collective-permute-start(bf16[4,128,768]{2,1,0:T(8,128)(2,1)S(1)} %pad_maximum_fusion), channel_id=1, source_target_pairs={{0,48},{8,56},{16,0},{24,8},{32,16},{40,24},{48,32},{56,40},{64,11... | collective-permute-start | bytes 2359304 | tf_op jit(solution)/shard_map/ppermute | solution.py:269
  49.5 0.0 copy-done.4
  49.5 4.2 %pick_a.1 = (bf16[3,128,768]{2,1,0:T(8,128)(2,1)}, bf16[3,128,768]{2,1,0:T(8,128)(2,1)}, bf16[3,128,768]{2,1,0:T(8,128)(2,1)}, bf16[3,128,768]{2,1,0:T(8,128)(2,1)}) custom-call(s32[64,64]{1,0:T(8,128)} %table.11, bf16[8,128,768]{2,1,0:T(8,128)(2,1)} %get-tuple-element.31.cols.refs_0_, bf16[8,128,768]{2,1,0:T(8,128)(2,1)} %copy-done.4), custom_call_target="tpu_custom_call" | custom-call | bytes 65536 | tf_op jit(solution)/shard_map/pick_a/pallas_call | solution.py:287
  53.6 1.6 collective-permute-start.5
  55.3 2.7 %collective-permute-start.6 = (bf16[3,128,768]{2,1,0:T(8,128)(2,1)}, bf16[3,128,768]{2,1,0:T(8,128)(2,1)S(1)}, u32[]{:S(2)}, u32[]{:S(2)}) collective-permute-start(bf16[3,128,768]{2,1,0:T(8,128)(2,1)} %get-tuple-element.42), channel_id=1, source_target_pairs={{0,128},{8,136},{16,144},{24,152},{32,160},{40,168},{48,176},{56,1... | collective-permute-start | bytes 1769480 | tf_op jit(solution)/shard_map/ppermute | solution.py:269
  58.0 1.4 collective-permute-start.7
  59.4 19.9 %collective-permute-done.9 = bf16[4,128,768]{2,1,0:T(8,128)(2,1)} collective-permute-done((bf16[4,128,768]{2,1,0:T(8,128)(2,1)S(1)}, bf16[4,128,768]{2,1,0:T(8,128)(2,1)}, u32[]{:S(2)}, u32[]{:S(2)}) %collective-permute-start.9) | collective-permute-done | bytes 786464 | tf_op jit(solution)/shard_map/ppermute | solution.py:269
  79.3 4.5 %collective-permute-done.8.refs_0_ = bf16[8,128,768]{2,1,0:T(8,128)(2,1)} collective-permute-done((bf16[8,128,768]{2,1,0:T(8,128)(2,1)S(1)}, bf16[8,128,768]{2,1,0:T(8,128)(2,1)}, u32[]{:S(2)}, u32[]{:S(2)}) %collective-permute-start.8) | collective-permute-done | bytes 1572896 | tf_op jit(solution)/shard_map/ppermute | solution.py:269
  83.8 0.0 collective-permute-done.5.refs_2_.refs_1_
  83.8 0.0 collective-permute-done.6.refs_3_.refs_2_
  83.8 0.0 copy-start.2
  83.8 0.0 collective-permute-done.7.refs_4_.refs_3_
  83.8 0.0 copy-start.3
  83.9 0.8 copy-done.1
  84.7 0.2 copy-done.2
  84.9 0.2 copy-done.3
  85.1 5.2 %pick_b.1 = (bf16[2,128,768]{2,1,0:T(8,128)(2,1)}, bf16[2,128,768]{2,1,0:T(8,128)(2,1)}, bf16[2,128,768]{2,1,0:T(8,128)(2,1)}, bf16[2,128,768]{2,1,0:T(8,128)(2,1)}, bf16[4,2,128,768]{3,2,1,0:T(8,128)(2,1)}) custom-call(s32[64,64]{1,0:T(8,128)} %table.11, bf16[8,128,768]{2,1,0:T(8,128)(2,1)} %collective-permute-done.8.refs_0_, ...), custom_call_target="tpu_custom_call" | custom-call | bytes 65536 | tf_op jit(solution)/shard_map/pick_b/pallas_call | solution.py:287
  90.3 4.4 %all-to-all-start = ((bf16[4,2,128,768]{3,2,1,0:T(8,128)(2,1)}), bf16[4,2,128,768]{3,2,1,0:T(8,128)(2,1)S(1)}, u32[]{:S(2)}, u32[]{:S(2)}) async-start(bf16[4,2,128,768]{3,2,1,0:T(8,128)(2,1)} %get-tuple-element.52), calls=%async_computation | async-start | bytes 3145728 | tf_op jit(solution)/shard_map/all_to_all | solution.py:379
  94.7 3.5 %collective-permute-start.14 = (bf16[4,128,768]{2,1,0:T(8,128)(2,1)}, bf16[4,128,768]{2,1,0:T(8,128)(2,1)S(1)}, u32[]{:S(2)}, u32[]{:S(2)}) collective-permute-start(bf16[4,128,768]{2,1,0:T(8,128)(2,1)} %collective-permute-done.9), channel_id=1, source_target_pairs={{0,48},{8,56},{16,0},{24,8},{32,16},{40,24},{48,32},{56,40},{64,11... | collective-permute-start | bytes 2359304 | tf_op jit(solution)/shard_map/ppermute | solution.py:269
  98.2 0.5 collective-permute-start.10
  98.6 1.5 collective-permute-start.11
  100.1 4.4 %collective-permute-start.12 = (bf16[2,128,768]{2,1,0:T(8,128)(2,1)}, bf16[2,128,768]{2,1,0:T(8,128)(2,1)S(1)}, u32[]{:S(2)}, u32[]{:S(2)}) collective-permute-start(bf16[2,128,768]{2,1,0:T(8,128)(2,1)} %get-tuple-element.50), channel_id=1, source_target_pairs={{0,136},{8,144},{16,152},{24,160},{32,168},{40,176},{48,184},{56,1... | collective-permute-start | bytes 1179656 | tf_op jit(solution)/shard_map/ppermute | solution.py:269
  104.5 0.9 collective-permute-start.13
  105.4 8.5 %pairs_a.1 = (f32[16,512]{1,0:T(8,128)}, f32[12,128]{1,0:T(8,128)}) custom-call(s32[64,64]{1,0:T(8,128)} %table.11, s32[512]{0:T(512)} %valid.7, bf16[16,512,768]{2,1,0:T(8,128)(2,1)} %get-tuple-element.38.own, bf16[3,128,768]{2,1,0:T(8,128)(2,1)} %get-tuple-element.40.refs_1_.refs_0_, bf16[3,128,768]{2,1,0:T(8,128)(2,1)} %copy-done.1, ...), custom_call_target="tpu_custom_call" | custom-call | bytes 65536 | tf_op jit(solution)/shard_map/pairs_a/pallas_call | solution.py:307
  114.0 0.0 collective-permute-done.10.refs_2_
  114.0 0.0 copy-start.6
  114.0 8.9 %collective-permute-done.11.refs_3_ = bf16[2,128,768]{2,1,0:T(8,128)(2,1)S(1)} collective-permute-done((bf16[2,128,768]{2,1,0:T(8,128)(2,1)}, bf16[2,128,768]{2,1,0:T(8,128)(2,1)S(1)}, u32[]{:S(2)}, u32[]{:S(2)}) %collective-permute-start.11) | collective-permute-done | bytes 393248 | tf_op jit(solution)/shard_map/ppermute | solution.py:269
  122.9 7.6 %collective-permute-done.12.refs_4_ = bf16[2,128,768]{2,1,0:T(8,128)(2,1)S(1)} collective-permute-done((bf16[2,128,768]{2,1,0:T(8,128)(2,1)}, bf16[2,128,768]{2,1,0:T(8,128)(2,1)S(1)}, u32[]{:S(2)}, u32[]{:S(2)}) %collective-permute-start.12) | collective-permute-done | bytes 393248 | tf_op jit(solution)/shard_map/ppermute | solution.py:269
  130.5 0.0 copy-start.8
  130.5 2.8 %collective-permute-done.13.refs_5_ = bf16[2,128,768]{2,1,0:T(8,128)(2,1)S(1)} collective-permute-done((bf16[2,128,768]{2,1,0:T(8,128)(2,1)}, bf16[2,128,768]{2,1,0:T(8,128)(2,1)S(1)}, u32[]{:S(2)}, u32[]{:S(2)}) %collective-permute-start.13) | collective-permute-done | bytes 393248 | tf_op jit(solution)/shard_map/ppermute | solution.py:269
  133.2 0.0 copy-start.9
  133.2 0.7 copy-done.9
  134.0 0.0 collective-permute-done.14.refs_7_
  134.0 0.0 all-to-all-done.refs_6_
  134.0 0.0 copy-start
  134.0 0.0 copy-done.6
  134.0 0.0 copy-done.7
  134.0 0.0 copy-done.8
  134.0 0.8 copy-done.5
  134.9 0.5 copy-done
  135.4 12.7 %pairs_b.1 = (f32[16,512]{1,0:T(8,128)}, f32[64,128]{1,0:T(8,128)}, f32[8,512]{1,0:T(8,128)}) custom-call(s32[64,64]{1,0:T(8,128)} %table.11, s32[512]{0:T(512)} %valid.7, bf16[16,512,768]{2,1,0:T(8,128)(2,1)} %get-tuple-element.38.own, f32[16,512]{1,0:T(8,128)} %get-tuple-element.47.refs_0_, f32[12,128]{1,0:T(8,128)} %get-tuple-element.48.refs_1_, ...), custom_call_target="tpu_custom_call" | custom-call | bytes 65536 | tf_op jit(solution)/shard_map/pairs_b/pallas_call | solution.py:307
  148.1 10.4 %all-to-all-start.1 = ((f32[32,2,128]{2,1,0:T(2,128)}), f32[32,2,128]{2,1,0:T(2,128)S(1)}, u32[]{:S(2)}, u32[]{:S(2)}) async-start(f32[32,2,128]{2,1,0:T(2,128)} %bitcast.8), calls=%async_computation.1 | async-start | bytes 65536 | tf_op jit(solution)/shard_map/all_to_all | solution.py:402
  158.5 0.1 collective-permute-start.15
  158.6 1.4 collective-permute-done.15.sib_rows
  160.0 8.4 %all-to-all-done.1 = f32[32,2,128]{2,1,0:T(2,128)S(1)} async-done(((f32[32,2,128]{2,1,0:T(2,128)}), f32[32,2,128]{2,1,0:T(2,128)S(1)}, u32[]{:S(2)}, u32[]{:S(2)}) %all-to-all-start.1) | async-done | bytes 32800 | tf_op jit(solution)/shard_map/all_to_all | solution.py:402
  168.3 0.0 copy-done.11
  168.3 0.6 copy-done.10
  168.9 2.1 %merge.1 = f32[4,8,512]{2,1,0:T(8,128)} custom-call(s32[64,64]{1,0:T(8,128)} %table.11, f32[8,512]{1,0:T(8,128)} %get-tuple-element.37.local, f32[16,512]{1,0:T(8,128)} %get-tuple-element.54.row_best, f32[8,512]{1,0:T(8,128)} %copy-done.11, f32[64,128]{1,0:T(8,128)} %bitcast.7), custom_call_target="tpu_custom_call" | custom-call | bytes 65536 | tf_op jit(solution)/shard_map/merge/pallas_call | solution.py:403
  171.1 8.3 %all_to_all.21.got = f32[4,8,512]{2,1,0:T(8,128)} all-to-all(f32[4,8,512]{2,1,0:T(8,128)} %merge.1), channel_id=1, replica_groups=mesh['x'=4,'z'=8,'core'=2,'rep'=4] {'rep'}, dimensions={0} | all-to-all | bytes 131072 | tf_op jit(solution)/shard_map/all_to_all | solution.py:412
  179.4 1.5 finish.1
  (6 shorter events, 0.0 us)
Async XLA Ops:
  0.0 21.7 %collective-permute-start.4 = (bf16[8,512,768]{2,1,0:T(8,128)(2,1)}, bf16[8,512,768]{2,1,0:T(8,128)(2,1)}, u32[]{:S(2)}, u32[]{:S(2)}) collective-permute-start(bf16[8,512,768]{2,1,0:T(8,128)(2,1)} %bitcast.4), channel_id=1, source_target_pairs={{0,4},{4,0},{1,5},{5,1},{2,6},{6,2},{3,7},{7,3},{8,12},{12,8},{9,1... | collective-permute-start | bytes 18874376 | tf_op jit(solution)/shard_map/ppermute | solution.py:346
  5.1 41.2 %collective-permute-start = (bf16[8,128,768]{2,1,0:T(8,128)(2,1)}, bf16[8,128,768]{2,1,0:T(8,128)(2,1)S(1)}, u32[]{:S(2)}, u32[]{:S(2)}) collective-permute-start(bf16[8,128,768]{2,1,0:T(8,128)(2,1)} %get-tuple-element.31.cols.refs_0_), channel_id=1, source_target_pairs={{0,8},{8,16},{16,24},{24,32},{32,40},{40,48},{48,56},{56,0},{64,72... | collective-permute-start | bytes 4718600 | tf_op jit(solution)/shard_map/ppermute | solution.py:269
  7.1 8.5 %collective-permute-start.1 = (bf16[1,128,768]{2,1,0:T(8,128)(2,1)}, bf16[1,128,768]{2,1,0:T(8,128)(2,1)S(1)}, u32[]{:S(2)}, u32[]{:S(2)}) collective-permute-start(bf16[1,128,768]{2,1,0:T(8,128)(2,1)} %get-tuple-element.33), channel_id=1, source_target_pairs={{0,64},{8,72},{16,80},{24,88},{32,96},{40,104},{48,112},{56,120},{... | collective-permute-start | bytes 589832 | tf_op jit(solution)/shard_map/ppermute | solution.py:269
  8.5 12.2 %collective-permute-start.2 = (bf16[1,128,768]{2,1,0:T(8,128)(2,1)}, bf16[1,128,768]{2,1,0:T(8,128)(2,1)S(1)}, u32[]{:S(2)}, u32[]{:S(2)}) collective-permute-start(bf16[1,128,768]{2,1,0:T(8,128)(2,1)} %get-tuple-element.34), channel_id=1, source_target_pairs={{0,128},{8,136},{16,144},{24,152},{32,160},{40,168},{48,176},{56,1... | collective-permute-start | bytes 589832 | tf_op jit(solution)/shard_map/ppermute | solution.py:269
  11.3 9.4 %collective-permute-start.3 = (bf16[1,128,768]{2,1,0:T(8,128)(2,1)}, bf16[1,128,768]{2,1,0:T(8,128)(2,1)S(1)}, u32[]{:S(2)}, u32[]{:S(2)}) collective-permute-start(bf16[1,128,768]{2,1,0:T(8,128)(2,1)} %get-tuple-element.35), channel_id=1, source_target_pairs={{0,192},{8,200},{16,208},{24,216},{32,224},{40,232},{48,240},{56,2... | collective-permute-start | bytes 589832 | tf_op jit(solution)/shard_map/ppermute | solution.py:269
  46.3 3.2 %copy-start.4 = (bf16[8,128,768]{2,1,0:T(8,128)(2,1)}, bf16[8,128,768]{2,1,0:T(8,128)(2,1)S(1)}, u32[]{:S(2)}) copy-start(bf16[8,128,768]{2,1,0:T(8,128)(2,1)S(1)} %collective-permute-done.refs_1_) | copy-start | bytes 4718596
  46.3 37.5 %collective-permute-start.8 = (bf16[8,128,768]{2,1,0:T(8,128)(2,1)S(1)}, bf16[8,128,768]{2,1,0:T(8,128)(2,1)}, u32[]{:S(2)}, u32[]{:S(2)}) collective-permute-start(bf16[8,128,768]{2,1,0:T(8,128)(2,1)S(1)} %collective-permute-done.refs_1_), channel_id=1, source_target_pairs={{0,8},{8,16},{16,24},{24,32},{32,40},{40,48},{48,56},{56,0},{64,72... | collective-permute-start | bytes 4718600 | tf_op jit(solution)/shard_map/ppermute | solution.py:269
  46.3 33.0 %collective-permute-start.9 = (bf16[4,128,768]{2,1,0:T(8,128)(2,1)S(1)}, bf16[4,128,768]{2,1,0:T(8,128)(2,1)}, u32[]{:S(2)}, u32[]{:S(2)}) collective-permute-start(bf16[4,128,768]{2,1,0:T(8,128)(2,1)S(1)} %pad_maximum_fusion), channel_id=1, source_target_pairs={{0,48},{8,56},{16,0},{24,8},{32,16},{40,24},{48,32},{56,40},{64,11... | collective-permute-start | bytes 2359304 | tf_op jit(solution)/shard_map/ppermute | solution.py:269
  53.6 30.2 %collective-permute-start.5 = (bf16[3,128,768]{2,1,0:T(8,128)(2,1)}, bf16[3,128,768]{2,1,0:T(8,128)(2,1)S(1)}, u32[]{:S(2)}, u32[]{:S(2)}) collective-permute-start(bf16[3,128,768]{2,1,0:T(8,128)(2,1)} %get-tuple-element.41), channel_id=1, source_target_pairs={{0,64},{8,72},{16,80},{24,88},{32,96},{40,104},{48,112},{56,120},{... | collective-permute-start | bytes 1769480 | tf_op jit(solution)/shard_map/ppermute | solution.py:269
  55.3 28.5 %collective-permute-start.6 = (bf16[3,128,768]{2,1,0:T(8,128)(2,1)}, bf16[3,128,768]{2,1,0:T(8,128)(2,1)S(1)}, u32[]{:S(2)}, u32[]{:S(2)}) collective-permute-start(bf16[3,128,768]{2,1,0:T(8,128)(2,1)} %get-tuple-element.42), channel_id=1, source_target_pairs={{0,128},{8,136},{16,144},{24,152},{32,160},{40,168},{48,176},{56,1... | collective-permute-start | bytes 1769480 | tf_op jit(solution)/shard_map/ppermute | solution.py:269
  58.0 25.9 %collective-permute-start.7 = (bf16[3,128,768]{2,1,0:T(8,128)(2,1)}, bf16[3,128,768]{2,1,0:T(8,128)(2,1)S(1)}, u32[]{:S(2)}, u32[]{:S(2)}) collective-permute-start(bf16[3,128,768]{2,1,0:T(8,128)(2,1)} %get-tuple-element.43), channel_id=1, source_target_pairs={{0,192},{8,200},{16,208},{24,216},{32,224},{40,232},{48,240},{56,2... | collective-permute-start | bytes 1769480 | tf_op jit(solution)/shard_map/ppermute | solution.py:269
  83.8 0.8 copy-start.1
  83.8 1.1 copy-start.2
  83.8 1.2 copy-start.3
  90.3 43.7 %all-to-all-start = ((bf16[4,2,128,768]{3,2,1,0:T(8,128)(2,1)}), bf16[4,2,128,768]{3,2,1,0:T(8,128)(2,1)S(1)}, u32[]{:S(2)}, u32[]{:S(2)}) async-start(bf16[4,2,128,768]{3,2,1,0:T(8,128)(2,1)} %get-tuple-element.52), calls=%async_computation | async-start | bytes 3145728 | tf_op jit(solution)/shard_map/all_to_all | solution.py:379
  94.7 39.3 %collective-permute-start.14 = (bf16[4,128,768]{2,1,0:T(8,128)(2,1)}, bf16[4,128,768]{2,1,0:T(8,128)(2,1)S(1)}, u32[]{:S(2)}, u32[]{:S(2)}) collective-permute-start(bf16[4,128,768]{2,1,0:T(8,128)(2,1)} %collective-permute-done.9), channel_id=1, source_target_pairs={{0,48},{8,56},{16,0},{24,8},{32,16},{40,24},{48,32},{56,40},{64,11... | collective-permute-start | bytes 2359304 | tf_op jit(solution)/shard_map/ppermute | solution.py:269
  98.2 15.8 %collective-permute-start.10 = (bf16[2,128,768]{2,1,0:T(8,128)(2,1)}, bf16[2,128,768]{2,1,0:T(8,128)(2,1)S(1)}, u32[]{:S(2)}, u32[]{:S(2)}) collective-permute-start(bf16[2,128,768]{2,1,0:T(8,128)(2,1)} %get-tuple-element.46.refs_4_), channel_id=1, source_target_pairs={{0,8},{8,16},{16,24},{24,32},{32,40},{40,48},{48,56},{56,0},{64,72... | collective-permute-start | bytes 1179656 | tf_op jit(solution)/shard_map/ppermute | solution.py:269
  98.6 24.2 %collective-permute-start.11 = (bf16[2,128,768]{2,1,0:T(8,128)(2,1)}, bf16[2,128,768]{2,1,0:T(8,128)(2,1)S(1)}, u32[]{:S(2)}, u32[]{:S(2)}) collective-permute-start(bf16[2,128,768]{2,1,0:T(8,128)(2,1)} %get-tuple-element.49), channel_id=1, source_target_pairs={{0,72},{8,80},{16,88},{24,96},{32,104},{40,112},{48,120},{56,64},{... | collective-permute-start | bytes 1179656 | tf_op jit(solution)/shard_map/ppermute | solution.py:269
  100.1 30.3 %collective-permute-start.12 = (bf16[2,128,768]{2,1,0:T(8,128)(2,1)}, bf16[2,128,768]{2,1,0:T(8,128)(2,1)S(1)}, u32[]{:S(2)}, u32[]{:S(2)}) collective-permute-start(bf16[2,128,768]{2,1,0:T(8,128)(2,1)} %get-tuple-element.50), channel_id=1, source_target_pairs={{0,136},{8,144},{16,152},{24,160},{32,168},{40,176},{48,184},{56,1... | collective-permute-start | bytes 1179656 | tf_op jit(solution)/shard_map/ppermute | solution.py:269
  104.5 28.7 %collective-permute-start.13 = (bf16[2,128,768]{2,1,0:T(8,128)(2,1)}, bf16[2,128,768]{2,1,0:T(8,128)(2,1)S(1)}, u32[]{:S(2)}, u32[]{:S(2)}) collective-permute-start(bf16[2,128,768]{2,1,0:T(8,128)(2,1)} %get-tuple-element.51), channel_id=1, source_target_pairs={{0,200},{8,208},{16,216},{24,224},{32,232},{40,240},{48,248},{56,1... | collective-permute-start | bytes 1179656 | tf_op jit(solution)/shard_map/ppermute | solution.py:269
  114.0 20.0 %copy-start.6 = (bf16[2,128,768]{2,1,0:T(8,128)(2,1)}, bf16[2,128,768]{2,1,0:T(8,128)(2,1)S(1)}, u32[]{:S(2)}) copy-start(bf16[2,128,768]{2,1,0:T(8,128)(2,1)S(1)} %collective-permute-done.10.refs_2_) | copy-start | bytes 1179652
  122.9 11.1 %copy-start.7 = (bf16[2,128,768]{2,1,0:T(8,128)(2,1)}, bf16[2,128,768]{2,1,0:T(8,128)(2,1)S(1)}, u32[]{:S(2)}) copy-start(bf16[2,128,768]{2,1,0:T(8,128)(2,1)S(1)} %collective-permute-done.11.refs_3_) | copy-start | bytes 1179652
  130.5 3.6 %copy-start.8 = (bf16[2,128,768]{2,1,0:T(8,128)(2,1)}, bf16[2,128,768]{2,1,0:T(8,128)(2,1)S(1)}, u32[]{:S(2)}) copy-start(bf16[2,128,768]{2,1,0:T(8,128)(2,1)S(1)} %collective-permute-done.12.refs_4_) | copy-start | bytes 1179652
  133.2 0.7 copy-start.9
  134.0 0.9 copy-start.5
  134.0 1.4 copy-start
  148.1 20.2 %all-to-all-start.1 = ((f32[32,2,128]{2,1,0:T(2,128)}), f32[32,2,128]{2,1,0:T(2,128)S(1)}, u32[]{:S(2)}, u32[]{:S(2)}) async-start(f32[32,2,128]{2,1,0:T(2,128)} %bitcast.8), calls=%async_computation.1 | async-start | bytes 65536 | tf_op jit(solution)/shard_map/all_to_all | solution.py:402
  158.5 1.5 collective-permute-start.15
  160.0 8.4 %copy-start.11 = (f32[8,512]{1,0:T(8,128)}, f32[8,512]{1,0:T(8,128)S(1)}, u32[]{:S(2)}) copy-start(f32[8,512]{1,0:T(8,128)S(1)} %collective-permute-done.15.sib_rows) | copy-start | bytes 49156
  168.3 0.6 copy-start.10

commit v2 on v1

v2 whole, which is shorter than its diff:
```python
import functools

import jax
import jax.numpy as jnp
from jax import lax
from jax.experimental import pallas as pl
from jax.experimental.pallas import tpu as pltpu
from jax.sharding import Mesh, PartitionSpec as P

absent = -2.0
epsilon = 1e-06
n_x, n_z, n_core, n_rep = 4, 8, 2, 4
chips = n_x * n_z
blocks = 8
rows = 512
quarter = rows // n_rep
width = 768
vmem_bytes = 60 << 20


def dot_t(left, right):
    return lax.dot_general(
        left, right, (((1,), (1,)), ((), ())), preferred_element_type=jnp.float32
    )


def normalise(raw):
    wide = raw.astype(jnp.float32)
    scale = lax.rsqrt(jnp.sum(wide * wide, axis=-1, keepdims=True) + epsilon)
    return (wide * scale).astype(jnp.bfloat16)


def place():
    return lax.axis_index("x"), lax.axis_index("z"), lax.axis_index("core"), lax.axis_index("rep")


def pair_info(table, source, target, core, many, which):
    side = which if many == 2 else jnp.where(source < target, core, 1 - core)
    forth = table[source * n_core + core, target * n_core + side]
    back = table[target * n_core + side, source * n_core + core]
    live = (forth >= 0) | (back >= 0)
    if many == 1:
        live = live & ((source != target) | (core == 0))
    source_block = jnp.where(forth >= 0, forth >> 3, back & 7)
    target_block = jnp.where(forth >= 0, forth & 7, (back >> 3) & 7)
    return live, side, source_block, target_block


def chip_at(x, z, dx, dz):
    return ((x + dx + n_x) & (n_x - 1)) * n_z + ((z + dz + n_z) & (n_z - 1))


first = [[(dx, 0, 1, 0), (dx, 1, 2, 0), (dx, 1, 2, 1)] for dx in range(n_x)]
second = [[(dx, 2, 2, 0), (dx, 2, 2, 1)] for dx in range(n_x)]
third = [[(dx, 3, 2, 0), (dx, 3, 2, 1)] for dx in (0, 1, 3)]
far = [(dx, 4, 1, 0) for dx in range(n_x)]
down = [(2, 5, 2, 0), (2, 5, 2, 1)]
stages = [sum(first, []) + far, third[0] + third[1], third[2] + down + sum(second, [])]
every = sum(stages, [])
gone_of = {0: 0, 1: 1, 2: 2, 3: 2}
at_pick, at_back, at_back_row, at_row, at_own = 0, 32, 64, 96, 128
at_stage, plan_size = [], 144
for stage in stages:
    at_stage.append(plan_size)
    plan_size += 16 + len(stage) + 1 + 16 * (len(stage) + 2)


def plan_kernel(table, valid, after, plan):
    x, z, core, rep = place()
    chip = chip_at(x, z, 0, 0)
    start = rep * quarter
    for o in range(2 * blocks):
        owner = chip * n_core + (core if o < blocks else 1 - core)
        plan[at_own + o] = valid[owner * blocks + o % blocks]
    number = 0
    for stage, base in zip(stages, at_stage):
        slots = len(stage)
        counts, lists = base + 2 * blocks, base + 2 * blocks + slots + 1
        for o in range(2 * blocks):
            plan[base + o] = 0
        for slot, (dx, dz, many, which) in enumerate(stage):
            target = chip_at(x, z, dx, dz)
            _, _, block, _ = pair_info(table, chip, target, core, many, which)
            plan[at_back + number] = block
            plan[at_back_row + number] = 2 * target + which
            if dz in gone_of:
                gone = gone_of[dz]
                source, target = chip_at(x, z, 0, -gone), chip_at(x, z, dx, dz - gone)
                _, _, block, _ = pair_info(table, source, target, core, many, which)
                plan[at_pick + number] = block
            source = chip_at(x, z, -dx, -dz)
            live, side, block, own_block = pair_info(table, source, chip, core, many, which)
            mine = jnp.where(side == core, 0, blocks) + own_block
            filled = plan[base + mine]
            plan[lists + mine * (slots + 2) + filled] = jnp.where(live, slot, slots)
            plan[lists + mine * (slots + 2) + filled + 1] = slots
            plan[base + mine] = filled + live.astype(jnp.int32)
            plan[counts + slot] = valid[(source * n_core + core) * blocks + block] - start
            plan[at_row + number] = 2 * source + which
            number += 1
        plan[counts + slots] = 0


def prep_kernel(table, emb, units, to0, to1, to2, to3, around, raw, unit, sem_in, sems):
    x, z, core, rep = place()
    chip = chip_at(x, z, 0, 0)
    loads = [
        pltpu.make_async_copy(emb.at[b, pl.ds(rep * quarter, quarter)], raw.at[b], sem_in.at[b])
        for b in range(blocks)
    ]
    for load in loads:
        load.start()
    copies = []
    for b in range(blocks):
        loads[b].wait()
        unit[b] = normalise(raw[b])
        copies.append(pltpu.make_async_copy(unit.at[b], units.at[b], sem_in.at[b]))
        copies[-1].start()
    outs = [to0.at[0], to1.at[0], to2.at[0], to3.at[0], around.at[0], around.at[1]]
    for a, (dx, dz, many, which) in enumerate(far + down):
        _, _, block, _ = pair_info(table, chip, chip_at(x, z, dx, dz), core, many, which)
        copies.append(pltpu.make_async_copy(unit.at[block], outs[a], sems.at[a]))
        copies[-1].start()
    for copy in copies:
        copy.wait()


def pick_kernel(wanted, spread, plan, *refs):
    near_by, hop = refs[:2]
    parts, get_sems, put_sems = refs[-3:]
    x, z, core, rep = place()
    n = len(wanted)
    if spread:
        outs = list(refs[-n + n_x - 4 : -4])
        outs += [refs[-4].at[(x + dx) & (n_x - 1)] for dx in range(n_x)]
    else:
        outs = refs[-n - 3 : -3]
    gets, puts = [], []
    for a, numbers in enumerate(wanted):
        for place_in, number in enumerate(numbers):
            held = near_by if every[number][1] == 0 else hop
            gets.append(
                pltpu.make_async_copy(
                    held.at[plan[at_pick + number]],
                    parts.at[a, place_in],
                    get_sems.at[3 * a + place_in],
                )
            )
            gets[-1].start()
    left = list(gets)
    for a, (out, numbers) in enumerate(zip(outs, wanted)):
        for _ in numbers:
            left.pop(0).wait()
        puts.append(
            pltpu.make_async_copy(parts.at[a, pl.ds(0, len(numbers))], out, put_sems.at[a])
        )
        puts[-1].start()
    for copy in puts:
        copy.wait()


def local_kernel(valid, own, sib, cols, unit_out, best):
    step = pl.program_id(0)
    x, z, core, rep = place()
    dev = chip_at(x, z, 0, 0) * n_core + core
    start = rep * quarter

    @pl.when(step >= blocks)
    def _():
        unit_out[0] = normalise(sib[0])

    @pl.when(step < blocks)
    def _():
        mine = normalise(own[0])
        unit_out[0] = mine
        part = lax.broadcasted_iota(jnp.int32, (quarter, rows), 0)
        gap = lax.broadcasted_iota(jnp.int32, (quarter, rows), 1) - part
        found = jnp.full((1, rows), absent, jnp.float32)
        for k in range(0, blocks, 2):
            pair = jnp.concatenate([cols[k], cols[k + 1]], axis=0)
            scores = dot_t(pair, mine)
            for half in range(2):
                count = valid[dev * blocks + k + half] - start
                own_gap = jnp.where(k + half == step, start, rows)
                allowed = (part < count) & (gap != own_gap)
                here = jnp.where(allowed, scores[half * quarter : (half + 1) * quarter], absent)
                found = jnp.maximum(found, jnp.max(here, axis=0, keepdims=True))
        best[pl.ds(step, 1), :] = found


def pair_kernel(stage, feeds, plan, own, *refs):
    final = stage == len(stages) - 1
    slots, base = len(stages[stage]), at_stage[stage]
    counts, lists = base + 2 * blocks, base + 2 * blocks + slots + 1
    units, held, cols, sem_u, sem_g = refs[-5:]
    outs, arrays, past = refs[-8 if final else -7 : -5], refs, ()
    if final:
        past, arrays = refs[: 2 * stage], refs[2 * stage :]
    x, z, core, rep = place()
    gets = []
    for a, (array, dx, count, first_slot) in enumerate(feeds):
        came = arrays[array] if dx is None else arrays[array].at[(x - dx + n_x) & (n_x - 1)]
        gets.append(pltpu.make_async_copy(came, held.at[pl.ds(first_slot, count)], sem_g.at[a]))
        gets[-1].start()
    loads = []
    for o in range(2 * blocks):
        loads.append(pltpu.make_async_copy(own.at[o], units.at[o], sem_u.at[o]))

        @pl.when(plan[base + o] > 0)
        def _():
            loads[o].start()

    row_out, col_out = outs[:2]
    row_out[...] = jnp.full((2 * blocks, rows), absent, jnp.float32)
    for ref in past[::2]:
        row_out[...] = jnp.maximum(row_out[...], ref[...])
    cols[...] = jnp.full(cols.shape, absent, jnp.float32)
    if final:
        col_out[...] = jnp.full(col_out.shape, absent, jnp.float32)
        number = 0
        for ref, done in zip(past[1::2], stages):
            for slot in range(len(done)):
                col_out[pl.ds(plan[at_row + number], 1), :] = ref[slot : slot + 1, :]
                number += 1
    part = lax.broadcasted_iota(jnp.int32, (quarter, rows), 0)
    lane = lax.broadcasted_iota(jnp.int32, (2 * quarter, rows), 1)
    for copy in gets:
        copy.wait()
    for o in range(2 * blocks):
        own_count = plan[at_own + o]

        @pl.when(plan[base + o] > 0)
        def _():
            loads[o].wait()

        def visit(turn, carry):
            at = lists + o * (slots + 2) + 2 * turn
            pair = [plan[at], plan[at + 1]]
            here_slot = [pair[0], jnp.minimum(pair[1], slots - 1)]
            scores = dot_t(
                jnp.concatenate([held[here_slot[0]], held[here_slot[1]]], axis=0), units[o]
            )
            ok = jnp.where(lane < own_count, scores, absent)
            folded = jnp.maximum(
                jnp.maximum(ok[:, 0:128], ok[:, 128:256]), jnp.maximum(ok[:, 256:384], ok[:, 384:512])
            )
            top = row_out[o : o + 1, :]
            for half in range(2):
                span = slice(half * quarter, (half + 1) * quarter)
                here = jnp.where(part < plan[counts + pair[half]], scores[span], absent)
                top = jnp.maximum(top, jnp.max(here, axis=0, keepdims=True))
                cols[pl.ds(pair[half], 1), :] = jnp.max(folded[span].T, axis=0, keepdims=True)
            row_out[o : o + 1, :] = top
            return carry

        lax.fori_loop(0, (plan[base + o] + 1) >> 1, visit, 0)
    if final:
        outs[2][...] = row_out[blocks:]
        for slot in range(slots):
            number = len(every) - slots + slot
            col_out[pl.ds(plan[at_row + number], 1), :] = cols[slot : slot + 1, :]
    else:
        col_out[...] = cols[0:slots]


def spread_in(running, best, rep):
    wide = jnp.concatenate([best] * n_rep, axis=1)
    lane = lax.broadcasted_iota(jnp.int32, (blocks, rows), 1)
    mine = (lane >= rep * quarter) & (lane < (rep + 1) * quarter)
    return jnp.where(mine, jnp.maximum(running, wide), running)


def merge_kernel(plan, local, row_best, sib_rows, back, out, best):
    rep = lax.axis_index("rep")
    best[...] = jnp.full((blocks, quarter), absent, jnp.float32)
    for number in range(len(every)):
        block = plan[at_back + number]
        best[pl.ds(block, 1), :] = jnp.maximum(
            best[pl.ds(block, 1), :], back[pl.ds(plan[at_back_row + number], 1), :]
        )
    merged = jnp.maximum(jnp.maximum(local[...], row_best[0:blocks]), sib_rows[...])
    out[...] = spread_in(merged, best[...], rep)


def finish_kernel(plan, one, two, three, four, out):
    best = jnp.maximum(jnp.maximum(one[...], two[...]), jnp.maximum(three[...], four[...]))
    lane = lax.broadcasted_iota(jnp.int32, (1, quarter), 1)
    for b in range(blocks):
        count = plan[at_own + b]
        for q in range(n_rep):
            span = best[b : b + 1, q * quarter : (q + 1) * quarter]
            out[n_rep * b + q : n_rep * b + q + 1, :] = jnp.where(
                lane + q * quarter < count, span, -1.0
            )


def move(value, dx, dz):
    if dx % n_x == 0 and dz % n_z == 0:
        return value
    steps = [
        (x * n_z + z, (x + dx) % n_x * n_z + (z + dz) % n_z) for x in range(n_x) for z in range(n_z)
    ]
    return lax.ppermute(value, ("x", "z"), steps)


def on_device(embeddings, valid_rows, pair_table):
    smem = pl.BlockSpec(memory_space=pltpu.SMEM)
    vmem = pl.BlockSpec(memory_space=pltpu.VMEM)
    hbm = pl.BlockSpec(memory_space=pl.ANY)
    params = pltpu.CompilerParams(vmem_limit_bytes=vmem_bytes)
    cost = pl.CostEstimate(flops=0, bytes_accessed=1 << 16, transcendentals=0)
    f32, bf16 = jnp.float32, jnp.bfloat16
    part = (quarter, width)
    raw = embeddings.reshape(blocks, rows, width)

    def pick(wanted, spread, held, after, name):
        n = len(wanted)
        shapes = [(len(numbers),) + part for numbers in wanted]
        if spread:
            shapes = shapes[:-n_x] + [(n_x,) + shapes[-1]]
        return pl.pallas_call(
            functools.partial(pick_kernel, wanted, spread),
            out_shape=[jax.ShapeDtypeStruct(shape, bf16) for shape in shapes],
            in_specs=[smem] + [hbm] * len(held + after),
            out_specs=[hbm] * len(shapes),
            scratch_shapes=[
                pltpu.VMEM((n, 3) + part, bf16),
                pltpu.SemaphoreType.DMA((3 * n,)),
                pltpu.SemaphoreType.DMA((n,)),
            ],
            compiler_params=params,
            cost_estimate=cost,
            name=name,
        )(plan, *held, *after)

    def compare(stage, feeds, arrays, past, after, name):
        slots = len(stages[stage])
        shapes = [(2 * blocks, rows), (slots, quarter)]
        if past:
            shapes = [(2 * blocks, rows), (2 * chips, quarter), (blocks, rows)]
        return pl.pallas_call(
            functools.partial(pair_kernel, stage, feeds),
            out_shape=[jax.ShapeDtypeStruct(shape, f32) for shape in shapes],
            in_specs=[smem, hbm] + [vmem] * len(past) + [hbm] * len(arrays + after),
            out_specs=[vmem] * len(shapes),
            scratch_shapes=[
                pltpu.VMEM((2 * blocks, rows, width), bf16),
                pltpu.VMEM((slots,) + part, bf16),
                pltpu.VMEM((slots // 8 * 8 + 8, quarter), f32),
                pltpu.SemaphoreType.DMA((2 * blocks,)),
                pltpu.SemaphoreType.DMA((len(feeds),)),
            ],
            compiler_params=params,
            cost_estimate=cost,
            name=name,
        )(plan, units, *past, *arrays, *after)

    def numbers(wanted):
        return [[every.index(slot) for slot in slots] for slots in wanted]

    cols, *away, around = pl.pallas_call(
        prep_kernel,
        out_shape=[jax.ShapeDtypeStruct((blocks,) + part, bf16)]
        + [jax.ShapeDtypeStruct((1,) + part, bf16)] * n_x
        + [jax.ShapeDtypeStruct((2,) + part, bf16)],
        in_specs=[smem, hbm],
        out_specs=[hbm] * (2 + n_x),
        scratch_shapes=[
            pltpu.VMEM((blocks,) + part, bf16),
            pltpu.VMEM((blocks,) + part, bf16),
            pltpu.SemaphoreType.DMA((blocks,)),
            pltpu.SemaphoreType.DMA((len(far + down),)),
        ],
        compiler_params=params,
        cost_estimate=cost,
        name="prep",
    )(pair_table, raw)
    swap = [(0, 1), (1, 0)]
    sib_raw = lax.ppermute(raw, "core", swap)
    hop1 = move(cols, 0, 1)
    away = [move(a, dx, -2) for dx, a in enumerate(away)]
    plan = pl.pallas_call(
        plan_kernel,
        out_shape=jax.ShapeDtypeStruct((plan_size,), jnp.int32),
        in_specs=[smem, smem, hbm],
        out_specs=smem,
        compiler_params=params,
        cost_estimate=cost,
        name="plan",
    )(pair_table, valid_rows, cols)
    units, local_best = pl.pallas_call(
        local_kernel,
        grid=(2 * blocks,),
        out_shape=(
            jax.ShapeDtypeStruct((2 * blocks, rows, width), bf16),
            jax.ShapeDtypeStruct((blocks, rows), f32),
        ),
        in_specs=[
            smem,
            pl.BlockSpec((1, rows, width), lambda i: (jnp.minimum(i, blocks - 1), 0, 0)),
            pl.BlockSpec((1, rows, width), lambda i: (jnp.maximum(i - blocks, 0), 0, 0)),
            pl.BlockSpec((blocks,) + part, lambda i: (0, 0, 0)),
        ],
        out_specs=(
            pl.BlockSpec((1, rows, width), lambda i: (i, 0, 0)),
            pl.BlockSpec((blocks, rows), lambda i: (0, 0)),
        ),
        compiler_params=params,
        cost_estimate=cost,
        name="local",
    )(valid_rows, raw, sib_raw, cols)
    hop1, away, local_best, plan = lax.optimization_barrier((hop1, away, local_best, plan))
    hop2 = move(hop1, 0, 1)
    away = move(jnp.concatenate(away, axis=0), 0, -2)
    picked = pick(numbers(first), False, [cols, hop1], [], "pick_a")
    first_in = [move(a, dx, 0) for dx, a in enumerate(picked)]
    hop2, away, around = lax.optimization_barrier((hop2, away, around))
    picked = pick(numbers(third + second), True, [cols, hop2], first_in, "pick_b")
    third_in = [move(a, slots[0][0], 1) for slots, a in zip(third, picked)]
    second_in = lax.all_to_all(picked[-1], "x", split_axis=0, concat_axis=0, tiled=True)
    down_in = move(around, 2, -3)

    past_a = compare(
        0,
        [(dx, None, 3, 3 * dx) for dx in range(n_x)] + [(n_x, None, n_x, 3 * n_x)],
        first_in + [away],
        [],
        [picked[0]],
        "pairs_a",
    )
    past_b = compare(
        1,
        [(0, None, 2, 0), (1, None, 2, 2)],
        third_in[:2],
        [],
        [past_a[0]],
        "pairs_b",
    )
    row_best, col_best, sib_best = compare(
        2,
        [(0, None, 2, 0), (1, None, 2, 2)] + [(2, dx, 2, 4 + 2 * dx) for dx in range(n_x)],
        [third_in[2], down_in, second_in],
        [*past_a, *past_b],
        [],
        "pairs_c",
    )
    sib_rows = lax.ppermute(sib_best, "core", swap)
    back = lax.all_to_all(col_best, ("x", "z"), split_axis=0, concat_axis=0, tiled=True)
    combined = pl.pallas_call(
        merge_kernel,
        out_shape=jax.ShapeDtypeStruct((blocks, rows), f32),
        in_specs=[smem, vmem, vmem, vmem, vmem],
        out_specs=vmem,
        scratch_shapes=[pltpu.VMEM((blocks, quarter), f32)],
        cost_estimate=cost,
        name="merge",
    )(plan, local_best, row_best, sib_rows, back)
    others = [
        lax.ppermute(combined, "rep", [(y, (y + d) % n_rep) for y in range(n_rep)])
        for d in range(1, n_rep)
    ]
    result = pl.pallas_call(
        finish_kernel,
        out_shape=jax.ShapeDtypeStruct((blocks * n_rep, quarter), f32),
        in_specs=[smem, vmem, vmem, vmem, vmem],
        out_specs=vmem,
        cost_estimate=cost,
        name="finish",
    )(plan, combined, *others)
    return result.reshape(-1)


def solution(mesh):
    grid = Mesh(mesh.devices.reshape(n_x, n_z, n_core, n_rep), ("x", "z", "core", "rep"))
    return jax.shard_map(
        on_device,
        mesh=grid,
        in_specs=(P(("x", "z", "core"), None), P(), P()),
        out_specs=P(("x", "z", "core")),
        check_vma=False,
    )
```

time: 184 us -> 175 us (0.951); the launches traced: 181 us -> 174 us
  waiting for transfers between devices: 64.2 us -> 52.3 us
  starting transfers between devices: 42.2 us -> 52.4 us
  blocking collectives: 8.35 us -> 0 us
  Pallas kernels: 61.1 us -> 63.6 us
    ppermute x14, waiting for transfers between devices: 54.4 us -> 37.4 us  [move(): return lax.ppermute(value, ('x', 'z'), steps)]
    all_to_all x1 -> x0, blocking collectives: 8.35 us -> none  [on_device(): lax.all_to_all(shared, 'rep', split_axis=0, concat_axis=0, tiled=True)]
    ppermute x14, starting transfers between devices: 27.3 us -> 35.5 us  [move(): return lax.ppermute(value, ('x', 'z'), steps)]
    ppermute x0 -> x3, waiting for transfers between devices: none -> 5.15 us  [on_device(): lax.ppermute(combined, 'rep', [(y, (y + d) % n_rep) for y in range(n_rep)])]
    pallas_call x5 -> x7, Pallas kernels: 32.8 us -> 36 us  [the longest x3 23.7 us: compare(): pl.pallas_call(functools.partial(pair_kernel, stage, feeds), out_shape=[j...]
    ppermute x0 -> x3, starting transfers between devices: none -> 2.81 us  [on_device(): lax.ppermute(combined, 'rep', [(y, (y + d) % n_rep) for y in range(n_rep)])]
    unnamed x24 -> x30, local copies, waits for them, and re-layouts: 3.94 us -> 4.53 us
  transfers between devices with their start and end apart: 18 -> 21, of which waited for: 10 -> 10; matrix products, arithmetic and copies ran while one was open for 1% -> 1% of each run, Pallas kernels for 22% -> 27%
where the time goes in v2:
time: 175 us; the launch traced here: 174 us
  Pallas kernels  63.6 us (36%)
  starting transfers between devices  52.4 us (30%)
  waiting for transfers between devices  52.3 us (30%)
  local copies, waits for them, and re-layouts  4.53 us (3%)
    ppermute x14, waiting for transfers between devices, move(): return lax.ppermute(value, ('x', 'z'), steps)  37.4 us
    ppermute x14, starting transfers between devices, move(): return lax.ppermute(value, ('x', 'z'), steps)  35.5 us
    pallas_call x3, Pallas kernels, compare(): pl.pallas_call(functools.partial(pair_kernel, stage, feeds), out_shape=[j...  23.7 us
    pallas_call x1, Pallas kernels, on_device(): pl.pallas_call(local_kernel, grid=(2 * blocks,), out_shape=(jax.ShapeDtyp...  21.8 us
    all_to_all x1, starting transfers between devices, on_device(): lax.all_to_all(col_best, ('x', 'z'), split_axis=0, concat_axis=0, tiled=T...  9.31 us
    all_to_all x1, waiting for transfers between devices, on_device(): lax.all_to_all(col_best, ('x', 'z'), split_axis=0, concat_axis=0, tiled=T...  8.36 us
    pallas_call x2, Pallas kernels, pick(): pl.pallas_call(functools.partial(pick_kernel, wanted, spread), out_shape=...  8.09 us
    ppermute x3, waiting for transfers between devices, on_device(): lax.ppermute(combined, 'rep', [(y, (y + d) % n_rep) for y in range(n_rep)])  5.15 us
  transfers between devices with their start and end apart: 21, of which 10 were waited for; matrix products, arithmetic and copies ran while one was open for 1% of the time, Pallas kernels for 27%

profile of v2, /device:TPU:24, one launch (start us, length us, event | category | flops | bytes accessed | tf_op | source)
XLA Modules:
  0.0 174.0 jit_solution(5322459922437889808)
XLA Ops:
  0.0 0.0 collective-permute-start.5
  0.0 4.4 %prep.1 = (bf16[8,128,768]{2,1,0:T(8,128)(2,1)}, bf16[1,128,768]{2,1,0:T(8,128)(2,1)}, bf16[1,128,768]{2,1,0:T(8,128)(2,1)}, bf16[1,128,768]{2,1,0:T(8,128)(2,1)...) custom-call(s32[64,64]{1,0:T(8,128)} %table.3, bf16[8,512,768]{2,1,0:T(8,128)(2,1)} %bitcast.5), custom_call_target="tpu_custom_call" | custom-call | bytes 65536 | tf_op jit(solution)/shard_map/prep/pallas_call | solution.py:361
  4.4 2.0 %collective-permute-start = (bf16[8,128,768]{2,1,0:T(8,128)(2,1)}, bf16[8,128,768]{2,1,0:T(8,128)(2,1)S(1)}, u32[]{:S(2)}, u32[]{:S(2)}) collective-permute-start(bf16[8,128,768]{2,1,0:T(8,128)(2,1)} %get-tuple-element.38.cols.after.refs_0_), channel_id=1, source_target_pairs={{0,8},{8,16},{16,24},{24,32},{32,40},{40,48},{48,56},{56,0},{64,72... | collective-permute-start | bytes 4718600 | tf_op jit(solution)/shard_map/ppermute | solution.py:303
  6.4 5.4 %collective-permute-start.1 = (bf16[1,128,768]{2,1,0:T(8,128)(2,1)}, bf16[1,128,768]{2,1,0:T(8,128)(2,1)S(1)}, u32[]{:S(2)}, u32[]{:S(2)}) collective-permute-start(bf16[1,128,768]{2,1,0:T(8,128)(2,1)} %get-tuple-element.39), channel_id=1, source_target_pairs={{0,48},{8,56},{16,0},{24,8},{32,16},{40,24},{48,32},{56,40},{64,11... | collective-permute-start | bytes 589832 | tf_op jit(solution)/shard_map/ppermute | solution.py:303
  11.8 2.4 %collective-permute-start.2 = (bf16[1,128,768]{2,1,0:T(8,128)(2,1)}, bf16[1,128,768]{2,1,0:T(8,128)(2,1)S(1)}, u32[]{:S(2)}, u32[]{:S(2)}) collective-permute-start(bf16[1,128,768]{2,1,0:T(8,128)(2,1)} %get-tuple-element.40), channel_id=1, source_target_pairs={{0,112},{8,120},{16,64},{24,72},{32,80},{40,88},{48,96},{56,104},{... | collective-permute-start | bytes 589832 | tf_op jit(solution)/shard_map/ppermute | solution.py:303
  14.1 2.7 %collective-permute-start.3 = (bf16[1,128,768]{2,1,0:T(8,128)(2,1)}, bf16[1,128,768]{2,1,0:T(8,128)(2,1)S(1)}, u32[]{:S(2)}, u32[]{:S(2)}) collective-permute-start(bf16[1,128,768]{2,1,0:T(8,128)(2,1)} %get-tuple-element.41), channel_id=1, source_target_pairs={{0,176},{8,184},{16,128},{24,136},{32,144},{40,152},{48,160},{56,1... | collective-permute-start | bytes 589832 | tf_op jit(solution)/shard_map/ppermute | solution.py:303
  16.9 0.0 collective-permute-done.5.sib
  16.9 2.1 %collective-permute-start.4 = (bf16[1,128,768]{2,1,0:T(8,128)(2,1)}, bf16[1,128,768]{2,1,0:T(8,128)(2,1)S(1)}, u32[]{:S(2)}, u32[]{:S(2)}) collective-permute-start(bf16[1,128,768]{2,1,0:T(8,128)(2,1)} %get-tuple-element.42), channel_id=1, source_target_pairs={{0,240},{8,248},{16,192},{24,200},{32,208},{40,216},{48,224},{56,2... | collective-permute-start | bytes 589832 | tf_op jit(solution)/shard_map/ppermute | solution.py:303
  19.0 2.6 %plan.1 = s32[835]{0:T(1024)} custom-call(s32[64,64]{1,0:T(8,128)} %table.3, s32[512]{0:T(512)} %valid.3, bf16[8,128,768]{2,1,0:T(8,128)(2,1)} %get-tuple-element.38.cols.after.refs_0_), custom_call_target="tpu_custom_call" | custom-call | bytes 65536 | tf_op jit(solution)/shard_map/plan/pallas_call | solution.py:382
  21.6 21.8 %local.1 = (bf16[16,512,768]{2,1,0:T(8,128)(2,1)}, f32[8,512]{1,0:T(8,128)}) custom-call(s32[512]{0:T(512)} %valid.3, bf16[8,512,768]{2,1,0:T(8,128)(2,1)} %bitcast.6, bf16[8,512,768]{2,1,0:T(8,128)(2,1)} %collective-permute-done.5.sib, bf16[8,128,768]{2,1,0:T(8,128)(2,1)} %get-tuple-element.38.cols.after.refs_0_), custom_call_target="tpu_custom_call" | custom-call | bytes 65536 | tf_op jit(solution)/shard_map/local/pallas_call | solution.py:391
  43.4 0.0 collective-permute-done.1
  43.4 0.0 collective-permute-done.2
  43.4 0.0 collective-permute-done.3
  43.4 2.7 %collective-permute-done.4 = bf16[1,128,768]{2,1,0:T(8,128)(2,1)S(1)} collective-permute-done((bf16[1,128,768]{2,1,0:T(8,128)(2,1)}, bf16[1,128,768]{2,1,0:T(8,128)(2,1)S(1)}, u32[]{:S(2)}, u32[]{:S(2)}) %collective-permute-start.4) | collective-permute-done | bytes 196640 | tf_op jit(solution)/shard_map/ppermute | solution.py:303
  46.1 0.0 collective-permute-done.refs_1_
  46.1 2.5 %collective-permute-start.9 = (bf16[8,128,768]{2,1,0:T(8,128)(2,1)S(1)}, bf16[8,128,768]{2,1,0:T(8,128)(2,1)}, u32[]{:S(2)}, u32[]{:S(2)}) collective-permute-start(bf16[8,128,768]{2,1,0:T(8,128)(2,1)S(1)} %collective-permute-done.refs_1_), channel_id=1, source_target_pairs={{0,8},{8,16},{16,24},{24,32},{32,40},{40,48},{48,56},{56,0},{64,72... | collective-permute-start | bytes 4718600 | tf_op jit(solution)/shard_map/ppermute | solution.py:303
  48.6 1.0 pad_maximum_fusion
  49.7 3.0 %collective-permute-start.10 = (bf16[4,128,768]{2,1,0:T(8,128)(2,1)}, bf16[4,128,768]{2,1,0:T(8,128)(2,1)S(1)}, u32[]{:S(2)}, u32[]{:S(2)}) collective-permute-start(bf16[4,128,768]{2,1,0:T(8,128)(2,1)} %pad_maximum_fusion), channel_id=1, source_target_pairs={{0,48},{8,56},{16,0},{24,8},{32,16},{40,24},{48,32},{56,40},{64,11... | collective-permute-start | bytes 2359304 | tf_op jit(solution)/shard_map/ppermute | solution.py:303
  52.6 4.0 %pick_a.1 = (bf16[3,128,768]{2,1,0:T(8,128)(2,1)}, bf16[3,128,768]{2,1,0:T(8,128)(2,1)}, bf16[3,128,768]{2,1,0:T(8,128)(2,1)}, bf16[3,128,768]{2,1,0:T(8,128)(2,1)}) custom-call(s32[835]{0:T(1024)} %plan.1, bf16[8,128,768]{2,1,0:T(8,128)(2,1)} %get-tuple-element.38.cols.after.refs_0_, bf16[8,128,768]{2,1,0:T(8,128)(2,1)} %copy-done.4), custom_call_target="tpu_custom_call" | custom-call | bytes 65536 | tf_op jit(solution)/shard_map/pick_a/pallas_call | solution.py:321
  56.6 1.4 collective-permute-start.6
  57.9 1.7 collective-permute-start.7
  59.7 2.3 %collective-permute-start.8 = (bf16[3,128,768]{2,1,0:T(8,128)(2,1)}, bf16[3,128,768]{2,1,0:T(8,128)(2,1)S(1)}, u32[]{:S(2)}, u32[]{:S(2)}) collective-permute-start(bf16[3,128,768]{2,1,0:T(8,128)(2,1)} %get-tuple-element.51), channel_id=1, source_target_pairs={{0,192},{8,200},{16,208},{24,216},{32,224},{40,232},{48,240},{56,2... | collective-permute-start | bytes 1769480 | tf_op jit(solution)/shard_map/ppermute | solution.py:303
  61.9 23.6 %collective-permute-done.10.refs_4_ = bf16[4,128,768]{2,1,0:T(8,128)(2,1)S(1)} collective-permute-done((bf16[4,128,768]{2,1,0:T(8,128)(2,1)}, bf16[4,128,768]{2,1,0:T(8,128)(2,1)S(1)}, u32[]{:S(2)}, u32[]{:S(2)}) %collective-permute-start.10) | collective-permute-done | bytes 786464 | tf_op jit(solution)/shard_map/ppermute | solution.py:303
  85.5 0.0 collective-permute-done.9.refs_1_
  85.5 0.0 collective-permute-done.6.refs_3_.refs_1_
  85.5 0.0 collective-permute-done.7.refs_4_.refs_2_
  85.6 0.0 collective-permute-done.8.refs_5_.refs_3_
  85.6 0.8 copy-done.1
  86.4 0.2 copy-done.2
  86.6 0.2 copy-done.3
  86.8 4.1 %pick_b.1 = (bf16[2,128,768]{2,1,0:T(8,128)(2,1)}, bf16[2,128,768]{2,1,0:T(8,128)(2,1)}, bf16[2,128,768]{2,1,0:T(8,128)(2,1)}, bf16[4,2,128,768]{3,2,1,0:T(8,128)(2,1)}) custom-call(s32[835]{0:T(1024)} %plan.1, bf16[8,128,768]{2,1,0:T(8,128)(2,1)} %get-tuple-element.38.cols.after.refs_0_, bf16[8,128,768]{2,1,0:T(8,128)(2,1)} %collective-permute-done.9.refs_1_, ...), custom_call_target="tpu_custom_call" | custom-call | bytes 65536 | tf_op jit(solution)/shard_map/pick_b/pallas_call | solution.py:321
  91.0 4.7 %all-to-all-start = ((bf16[4,2,128,768]{3,2,1,0:T(8,128)(2,1)}), bf16[4,2,128,768]{3,2,1,0:T(8,128)(2,1)S(1)}, u32[]{:S(2)}, u32[]{:S(2)}) async-start(bf16[4,2,128,768]{3,2,1,0:T(8,128)(2,1)} %get-tuple-element.67), calls=%async_computation | async-start | bytes 3145728 | tf_op jit(solution)/shard_map/all_to_all | solution.py:420
  95.6 1.5 collective-permute-start.11
  97.2 1.5 collective-permute-start.12
  98.6 3.8 %collective-permute-start.13 = (bf16[2,128,768]{2,1,0:T(8,128)(2,1)}, bf16[2,128,768]{2,1,0:T(8,128)(2,1)S(1)}, u32[]{:S(2)}, u32[]{:S(2)}) collective-permute-start(bf16[2,128,768]{2,1,0:T(8,128)(2,1)} %get-tuple-element.65), channel_id=1, source_target_pairs={{0,200},{8,208},{16,216},{24,224},{32,232},{40,240},{48,248},{56,1... | collective-permute-start | bytes 1179656 | tf_op jit(solution)/shard_map/ppermute | solution.py:303
  102.5 3.2 %collective-permute-start.14 = (bf16[2,128,768]{2,1,0:T(8,128)(2,1)}, bf16[2,128,768]{2,1,0:T(8,128)(2,1)S(1)}, u32[]{:S(2)}, u32[]{:S(2)}) collective-permute-start(bf16[2,128,768]{2,1,0:T(8,128)(2,1)} %get-tuple-element.66), channel_id=1, source_target_pairs={{0,168},{8,176},{16,184},{24,128},{32,136},{40,144},{48,152},{56,1... | collective-permute-start | bytes 1179656 | tf_op jit(solution)/shard_map/ppermute | solution.py:303
  105.7 0.0 copy-done.5
  105.7 9.9 %pairs_a.1 = (f32[16,512]{1,0:T(8,128)}, f32[16,128]{1,0:T(8,128)}) custom-call(s32[835]{0:T(1024)} %plan.1, bf16[16,512,768]{2,1,0:T(8,128)(2,1)} %get-tuple-element.46.own, bf16[3,128,768]{2,1,0:T(8,128)(2,1)} %get-tuple-element.48.refs_2_.refs_0_, bf16[3,128,768]{2,1,0:T(8,128)(2,1)} %copy-done.1, bf16[3,128,768]{2,1,0:T(8,128)(2,1)} %copy-done.2, ...), custom_call_target="tpu_custom_call" | custom-call | bytes 65536 | tf_op jit(solution)/shard_map/pairs_a/pallas_call | solution.py:341
  115.6 0.0 collective-permute-done.11.refs_0_
  115.6 0.0 copy-start.6
  115.6 4.7 %collective-permute-done.12.refs_1_ = bf16[2,128,768]{2,1,0:T(8,128)(2,1)S(1)} collective-permute-done((bf16[2,128,768]{2,1,0:T(8,128)(2,1)}, bf16[2,128,768]{2,1,0:T(8,128)(2,1)S(1)}, u32[]{:S(2)}, u32[]{:S(2)}) %collective-permute-start.12) | collective-permute-done | bytes 393248 | tf_op jit(solution)/shard_map/ppermute | solution.py:303
  120.3 0.8 copy-done.7
  121.1 4.9 %pairs_b.1 = (f32[16,512]{1,0:T(8,128)}, f32[4,128]{1,0:T(4,128)}) custom-call(s32[835]{0:T(1024)} %plan.1, bf16[16,512,768]{2,1,0:T(8,128)(2,1)} %get-tuple-element.46.own, bf16[2,128,768]{2,1,0:T(8,128)(2,1)} %copy-done.6, bf16[2,128,768]{2,1,0:T(8,128)(2,1)} %copy-done.7, f32[16,512]{1,0:T(8,128)} %get-tuple-element.60.refs_2_.refs_0_), custom_call_target="tpu_custom_call" | custom-call | bytes 65536 | tf_op jit(solution)/shard_map/pairs_b/pallas_call | solution.py:341
  126.0 1.8 %collective-permute-done.13.refs_4_ = bf16[2,128,768]{2,1,0:T(8,128)(2,1)S(1)} collective-permute-done((bf16[2,128,768]{2,1,0:T(8,128)(2,1)}, bf16[2,128,768]{2,1,0:T(8,128)(2,1)S(1)}, u32[]{:S(2)}, u32[]{:S(2)}) %collective-permute-start.13) | collective-permute-done | bytes 393248 | tf_op jit(solution)/shard_map/ppermute | solution.py:303
  127.8 4.6 %collective-permute-done.14.refs_5_ = bf16[2,128,768]{2,1,0:T(8,128)(2,1)S(1)} collective-permute-done((bf16[2,128,768]{2,1,0:T(8,128)(2,1)}, bf16[2,128,768]{2,1,0:T(8,128)(2,1)S(1)}, u32[]{:S(2)}, u32[]{:S(2)}) %collective-permute-start.14) | collective-permute-done | bytes 393248 | tf_op jit(solution)/shard_map/ppermute | solution.py:303
  132.4 0.0 all-to-all-done.refs_6_
  132.4 0.8 copy-done.9
  133.1 0.5 copy-done
  133.6 8.9 %pairs_c.1 = (f32[16,512]{1,0:T(8,128)}, f32[64,128]{1,0:T(8,128)}, f32[8,512]{1,0:T(8,128)}) custom-call(s32[835]{0:T(1024)} %plan.1, bf16[16,512,768]{2,1,0:T(8,128)(2,1)} %get-tuple-element.46.own, f32[16,512]{1,0:T(8,128)} %get-tuple-element.60.refs_2_.refs_0_, f32[16,128]{1,0:T(8,128)} %get-tuple-element.61.refs_1_, ...), custom_call_target="tpu_custom_call" | custom-call | bytes 65536 | tf_op jit(solution)/shard_map/pairs_c/pallas_call | solution.py:341
  142.6 9.3 %all-to-all-start.1 = ((f32[32,2,128]{2,1,0:T(2,128)}), f32[32,2,128]{2,1,0:T(2,128)S(1)}, u32[]{:S(2)}, u32[]{:S(2)}) async-start(f32[32,2,128]{2,1,0:T(2,128)} %bitcast.8), calls=%async_computation.1 | async-start | bytes 65536 | tf_op jit(solution)/shard_map/all_to_all | solution.py:448
  151.9 0.1 collective-permute-start.15
  152.0 1.4 collective-permute-done.15.sib_rows
  153.4 8.4 %all-to-all-done.1 = f32[32,2,128]{2,1,0:T(2,128)S(1)} async-done(((f32[32,2,128]{2,1,0:T(2,128)}), f32[32,2,128]{2,1,0:T(2,128)S(1)}, u32[]{:S(2)}, u32[]{:S(2)}) %all-to-all-start.1) | async-done | bytes 32800 | tf_op jit(solution)/shard_map/all_to_all | solution.py:448
  161.7 0.0 copy-done.14
  161.7 0.6 copy-done.10
  162.4 1.6 merge.1.one
  163.9 0.2 collective-permute-start.16
  164.2 2.6 %collective-permute-start.17 = (f32[8,512]{1,0:T(8,128)}, f32[8,512]{1,0:T(8,128)S(1)}, u32[]{:S(2)}, u32[]{:S(2)}) collective-permute-start(f32[8,512]{1,0:T(8,128)} %merge.1.one), channel_id=1, source_target_pairs={{0,2},{1,3},{2,0},{3,1},{4,6},{5,7},{6,4},{7,5},{8,10},{9,11},{10,... | collective-permute-start | bytes 49160 | tf_op jit(solution)/shard_map/ppermute | solution.py:459
  166.8 0.0 collective-permute-start.18
  166.8 1.1 collective-permute-done.16.two
  167.9 1.7 collective-permute-done.17.three
  169.6 2.3 %collective-permute-done.18.four = f32[8,512]{1,0:T(8,128)S(1)} collective-permute-done((f32[8,512]{1,0:T(8,128)}, f32[8,512]{1,0:T(8,128)S(1)}, u32[]{:S(2)}, u32[]{:S(2)}) %collective-permute-start.18) | collective-permute-done | bytes 16416 | tf_op jit(solution)/shard_map/ppermute | solution.py:459
  171.9 0.6 copy-done.13
  172.5 1.5 finish.1
  (19 shorter events, 0.0 us)
Async XLA Ops:
  0.0 16.9 %collective-permute-start.5 = (bf16[8,512,768]{2,1,0:T(8,128)(2,1)}, bf16[8,512,768]{2,1,0:T(8,128)(2,1)}, u32[]{:S(2)}, u32[]{:S(2)}) collective-permute-start(bf16[8,512,768]{2,1,0:T(8,128)(2,1)} %bitcast.4), channel_id=1, source_target_pairs={{0,4},{4,0},{1,5},{5,1},{2,6},{6,2},{3,7},{7,3},{8,12},{12,8},{9,1... | collective-permute-start | bytes 18874376 | tf_op jit(solution)/shard_map/ppermute | solution.py:379
  4.4 41.7 %collective-permute-start = (bf16[8,128,768]{2,1,0:T(8,128)(2,1)}, bf16[8,128,768]{2,1,0:T(8,128)(2,1)S(1)}, u32[]{:S(2)}, u32[]{:S(2)}) collective-permute-start(bf16[8,128,768]{2,1,0:T(8,128)(2,1)} %get-tuple-element.38.cols.after.refs_0_), channel_id=1, source_target_pairs={{0,8},{8,16},{16,24},{24,32},{32,40},{40,48},{48,56},{56,0},{64,72... | collective-permute-start | bytes 4718600 | tf_op jit(solution)/shard_map/ppermute | solution.py:303
  6.4 37.0 %collective-permute-start.1 = (bf16[1,128,768]{2,1,0:T(8,128)(2,1)}, bf16[1,128,768]{2,1,0:T(8,128)(2,1)S(1)}, u32[]{:S(2)}, u32[]{:S(2)}) collective-permute-start(bf16[1,128,768]{2,1,0:T(8,128)(2,1)} %get-tuple-element.39), channel_id=1, source_target_pairs={{0,48},{8,56},{16,0},{24,8},{32,16},{40,24},{48,32},{56,40},{64,11... | collective-permute-start | bytes 589832 | tf_op jit(solution)/shard_map/ppermute | solution.py:303
  11.8 31.6 %collective-permute-start.2 = (bf16[1,128,768]{2,1,0:T(8,128)(2,1)}, bf16[1,128,768]{2,1,0:T(8,128)(2,1)S(1)}, u32[]{:S(2)}, u32[]{:S(2)}) collective-permute-start(bf16[1,128,768]{2,1,0:T(8,128)(2,1)} %get-tuple-element.40), channel_id=1, source_target_pairs={{0,112},{8,120},{16,64},{24,72},{32,80},{40,88},{48,96},{56,104},{... | collective-permute-start | bytes 589832 | tf_op jit(solution)/shard_map/ppermute | solution.py:303
  14.1 29.3 %collective-permute-start.3 = (bf16[1,128,768]{2,1,0:T(8,128)(2,1)}, bf16[1,128,768]{2,1,0:T(8,128)(2,1)S(1)}, u32[]{:S(2)}, u32[]{:S(2)}) collective-permute-start(bf16[1,128,768]{2,1,0:T(8,128)(2,1)} %get-tuple-element.41), channel_id=1, source_target_pairs={{0,176},{8,184},{16,128},{24,136},{32,144},{40,152},{48,160},{56,1... | collective-permute-start | bytes 589832 | tf_op jit(solution)/shard_map/ppermute | solution.py:303
  16.9 29.2 %collective-permute-start.4 = (bf16[1,128,768]{2,1,0:T(8,128)(2,1)}, bf16[1,128,768]{2,1,0:T(8,128)(2,1)S(1)}, u32[]{:S(2)}, u32[]{:S(2)}) collective-permute-start(bf16[1,128,768]{2,1,0:T(8,128)(2,1)} %get-tuple-element.42), channel_id=1, source_target_pairs={{0,240},{8,248},{16,192},{24,200},{32,208},{40,216},{48,224},{56,2... | collective-permute-start | bytes 589832 | tf_op jit(solution)/shard_map/ppermute | solution.py:303
  46.1 6.5 %copy-start.4 = (bf16[8,128,768]{2,1,0:T(8,128)(2,1)}, bf16[8,128,768]{2,1,0:T(8,128)(2,1)S(1)}, u32[]{:S(2)}) copy-start(bf16[8,128,768]{2,1,0:T(8,128)(2,1)S(1)} %collective-permute-done.refs_1_) | copy-start | bytes 4718596
  46.1 39.4 %collective-permute-start.9 = (bf16[8,128,768]{2,1,0:T(8,128)(2,1)S(1)}, bf16[8,128,768]{2,1,0:T(8,128)(2,1)}, u32[]{:S(2)}, u32[]{:S(2)}) collective-permute-start(bf16[8,128,768]{2,1,0:T(8,128)(2,1)S(1)} %collective-permute-done.refs_1_), channel_id=1, source_target_pairs={{0,8},{8,16},{16,24},{24,32},{32,40},{40,48},{48,56},{56,0},{64,72... | collective-permute-start | bytes 4718600 | tf_op jit(solution)/shard_map/ppermute | solution.py:303
  49.7 35.9 %collective-permute-start.10 = (bf16[4,128,768]{2,1,0:T(8,128)(2,1)}, bf16[4,128,768]{2,1,0:T(8,128)(2,1)S(1)}, u32[]{:S(2)}, u32[]{:S(2)}) collective-permute-start(bf16[4,128,768]{2,1,0:T(8,128)(2,1)} %pad_maximum_fusion), channel_id=1, source_target_pairs={{0,48},{8,56},{16,0},{24,8},{32,16},{40,24},{48,32},{56,40},{64,11... | collective-permute-start | bytes 2359304 | tf_op jit(solution)/shard_map/ppermute | solution.py:303
  56.6 29.0 %collective-permute-start.6 = (bf16[3,128,768]{2,1,0:T(8,128)(2,1)}, bf16[3,128,768]{2,1,0:T(8,128)(2,1)S(1)}, u32[]{:S(2)}, u32[]{:S(2)}) collective-permute-start(bf16[3,128,768]{2,1,0:T(8,128)(2,1)} %get-tuple-element.49), channel_id=1, source_target_pairs={{0,64},{8,72},{16,80},{24,88},{32,96},{40,104},{48,112},{56,120},{... | collective-permute-start | bytes 1769480 | tf_op jit(solution)/shard_map/ppermute | solution.py:303
  57.9 27.6 %collective-permute-start.7 = (bf16[3,128,768]{2,1,0:T(8,128)(2,1)}, bf16[3,128,768]{2,1,0:T(8,128)(2,1)S(1)}, u32[]{:S(2)}, u32[]{:S(2)}) collective-permute-start(bf16[3,128,768]{2,1,0:T(8,128)(2,1)} %get-tuple-element.50), channel_id=1, source_target_pairs={{0,128},{8,136},{16,144},{24,152},{32,160},{40,168},{48,176},{56,1... | collective-permute-start | bytes 1769480 | tf_op jit(solution)/shard_map/ppermute | solution.py:303
  59.7 25.9 %collective-permute-start.8 = (bf16[3,128,768]{2,1,0:T(8,128)(2,1)}, bf16[3,128,768]{2,1,0:T(8,128)(2,1)S(1)}, u32[]{:S(2)}, u32[]{:S(2)}) collective-permute-start(bf16[3,128,768]{2,1,0:T(8,128)(2,1)} %get-tuple-element.51), channel_id=1, source_target_pairs={{0,192},{8,200},{16,208},{24,216},{32,224},{40,232},{48,240},{56,2... | collective-permute-start | bytes 1769480 | tf_op jit(solution)/shard_map/ppermute | solution.py:303
  85.5 20.1 %copy-start.5 = (bf16[4,128,768]{2,1,0:T(8,128)(2,1)}, bf16[4,128,768]{2,1,0:T(8,128)(2,1)S(1)}, u32[]{:S(2)}) copy-start(bf16[4,128,768]{2,1,0:T(8,128)(2,1)S(1)} %collective-permute-done.10.refs_4_) | copy-start | bytes 2359300
  85.5 0.9 copy-start.1
  85.5 1.1 copy-start.2
  85.6 1.2 copy-start.3
  91.0 41.4 %all-to-all-start = ((bf16[4,2,128,768]{3,2,1,0:T(8,128)(2,1)}), bf16[4,2,128,768]{3,2,1,0:T(8,128)(2,1)S(1)}, u32[]{:S(2)}, u32[]{:S(2)}) async-start(bf16[4,2,128,768]{3,2,1,0:T(8,128)(2,1)} %get-tuple-element.67), calls=%async_computation | async-start | bytes 3145728 | tf_op jit(solution)/shard_map/all_to_all | solution.py:420
  95.6 20.0 %collective-permute-start.11 = (bf16[2,128,768]{2,1,0:T(8,128)(2,1)}, bf16[2,128,768]{2,1,0:T(8,128)(2,1)S(1)}, u32[]{:S(2)}, u32[]{:S(2)}) collective-permute-start(bf16[2,128,768]{2,1,0:T(8,128)(2,1)} %get-tuple-element.59.refs_5_), channel_id=1, source_target_pairs={{0,8},{8,16},{16,24},{24,32},{32,40},{40,48},{48,56},{56,0},{64,72... | collective-permute-start | bytes 1179656 | tf_op jit(solution)/shard_map/ppermute | solution.py:303
  97.2 23.1 %collective-permute-start.12 = (bf16[2,128,768]{2,1,0:T(8,128)(2,1)}, bf16[2,128,768]{2,1,0:T(8,128)(2,1)S(1)}, u32[]{:S(2)}, u32[]{:S(2)}) collective-permute-start(bf16[2,128,768]{2,1,0:T(8,128)(2,1)} %get-tuple-element.62), channel_id=1, source_target_pairs={{0,72},{8,80},{16,88},{24,96},{32,104},{40,112},{48,120},{56,64},{... | collective-permute-start | bytes 1179656 | tf_op jit(solution)/shard_map/ppermute | solution.py:303
  98.6 29.1 %collective-permute-start.13 = (bf16[2,128,768]{2,1,0:T(8,128)(2,1)}, bf16[2,128,768]{2,1,0:T(8,128)(2,1)S(1)}, u32[]{:S(2)}, u32[]{:S(2)}) collective-permute-start(bf16[2,128,768]{2,1,0:T(8,128)(2,1)} %get-tuple-element.65), channel_id=1, source_target_pairs={{0,200},{8,208},{16,216},{24,224},{32,232},{40,240},{48,248},{56,1... | collective-permute-start | bytes 1179656 | tf_op jit(solution)/shard_map/ppermute | solution.py:303
  102.5 29.9 %collective-permute-start.14 = (bf16[2,128,768]{2,1,0:T(8,128)(2,1)}, bf16[2,128,768]{2,1,0:T(8,128)(2,1)S(1)}, u32[]{:S(2)}, u32[]{:S(2)}) collective-permute-start(bf16[2,128,768]{2,1,0:T(8,128)(2,1)} %get-tuple-element.66), channel_id=1, source_target_pairs={{0,168},{8,176},{16,184},{24,128},{32,136},{40,144},{48,152},{56,1... | collective-permute-start | bytes 1179656 | tf_op jit(solution)/shard_map/ppermute | solution.py:303
  115.6 4.7 %copy-start.6 = (bf16[2,128,768]{2,1,0:T(8,128)(2,1)}, bf16[2,128,768]{2,1,0:T(8,128)(2,1)S(1)}, u32[]{:S(2)}) copy-start(bf16[2,128,768]{2,1,0:T(8,128)(2,1)S(1)} %collective-permute-done.11.refs_0_) | copy-start | bytes 1179652
  120.3 0.8 copy-start.7
  127.8 4.6 %copy-start.8 = (bf16[2,128,768]{2,1,0:T(8,128)(2,1)}, bf16[2,128,768]{2,1,0:T(8,128)(2,1)S(1)}, u32[]{:S(2)}) copy-start(bf16[2,128,768]{2,1,0:T(8,128)(2,1)S(1)} %collective-permute-done.13.refs_4_) | copy-start | bytes 1179652
  132.4 0.8 copy-start.9
  132.4 1.3 copy-start
  142.6 19.2 %all-to-all-start.1 = ((f32[32,2,128]{2,1,0:T(2,128)}), f32[32,2,128]{2,1,0:T(2,128)S(1)}, u32[]{:S(2)}, u32[]{:S(2)}) async-start(f32[32,2,128]{2,1,0:T(2,128)} %bitcast.8), calls=%async_computation.1 | async-start | bytes 65536 | tf_op jit(solution)/shard_map/all_to_all | solution.py:448
  151.9 1.5 collective-permute-start.15
  153.4 8.4 %copy-start.14 = (f32[8,512]{1,0:T(8,128)}, f32[8,512]{1,0:T(8,128)S(1)}, u32[]{:S(2)}) copy-start(f32[8,512]{1,0:T(8,128)S(1)} %collective-permute-done.15.sib_rows) | copy-start | bytes 49156
  161.7 0.6 copy-start.10
  163.9 3.9 %collective-permute-start.16 = (f32[8,512]{1,0:T(8,128)}, f32[8,512]{1,0:T(8,128)S(1)}, u32[]{:S(2)}, u32[]{:S(2)}) collective-permute-start(f32[8,512]{1,0:T(8,128)} %merge.1.one), channel_id=1, source_target_pairs={{0,1},{1,2},{2,3},{3,0},{4,5},{5,6},{6,7},{7,4},{8,9},{9,10},{10,1... | collective-permute-start | bytes 49160 | tf_op jit(solution)/shard_map/ppermute | solution.py:459
  164.2 5.5 %collective-permute-start.17 = (f32[8,512]{1,0:T(8,128)}, f32[8,512]{1,0:T(8,128)S(1)}, u32[]{:S(2)}, u32[]{:S(2)}) collective-permute-start(f32[8,512]{1,0:T(8,128)} %merge.1.one), channel_id=1, source_target_pairs={{0,2},{1,3},{2,0},{3,1},{4,6},{5,7},{6,4},{7,5},{8,10},{9,11},{10,... | collective-permute-start | bytes 49160 | tf_op jit(solution)/shard_map/ppermute | solution.py:459
  166.8 5.2 %collective-permute-start.18 = (f32[8,512]{1,0:T(8,128)}, f32[8,512]{1,0:T(8,128)S(1)}, u32[]{:S(2)}, u32[]{:S(2)}) collective-permute-start(f32[8,512]{1,0:T(8,128)} %merge.1.one), channel_id=1, source_target_pairs={{0,3},{1,0},{2,1},{3,2},{4,7},{5,4},{6,5},{7,6},{8,11},{9,8},{10,9... | collective-permute-start | bytes 49160 | tf_op jit(solution)/shard_map/ppermute | solution.py:459
  167.9 4.0 %copy-start.11 = (f32[8,512]{1,0:T(8,128)}, f32[8,512]{1,0:T(8,128)S(1)}, u32[]{:S(2)}) copy-start(f32[8,512]{1,0:T(8,128)S(1)} %collective-permute-done.16.two) | copy-start | bytes 49156
  169.6 2.3 %copy-start.12 = (f32[8,512]{1,0:T(8,128)}, f32[8,512]{1,0:T(8,128)S(1)}, u32[]{:S(2)}) copy-start(f32[8,512]{1,0:T(8,128)S(1)} %collective-permute-done.17.three) | copy-start | bytes 49156
  171.9 0.6 copy-start.13

commit v3 on v2

--- a/solution.py
+++ b/solution.py
@@ -62,10 +62,18 @@
 at_stage, plan_size = [], 144
 for stage in stages:
     at_stage.append(plan_size)
-    plan_size += 16 + len(stage) + 1 + 16 * (len(stage) + 2)
-
-
-def plan_kernel(table, valid, after, plan):
+    plan_size += 16 + len(stage) + 1 + 1 + 3 * (len(stage) + 2)
+
+
+def places(stage, base):
+    slots = len(stage)
+    counts = base + 2 * blocks
+    groups = counts + slots + 1
+    own_of = groups + 1
+    return counts, groups, own_of, own_of + slots + 2, own_of + 2 * (slots + 2)
+
+
+def plan_kernel(table, valid, after, plan, latest):
     x, z, core, rep = place()
     chip = chip_at(x, z, 0, 0)
     start = rep * quarter
@@ -75,9 +83,11 @@
     number = 0
     for stage, base in zip(stages, at_stage):
         slots = len(stage)
-        counts, lists = base + 2 * blocks, base + 2 * blocks + slots + 1
+        counts, groups, own_of, first_of, second_of = places(stage, base)
         for o in range(2 * blocks):
             plan[base + o] = 0
+            latest[o] = 0
+        plan[groups] = 0
         for slot, (dx, dz, many, which) in enumerate(stage):
             target = chip_at(x, z, dx, dz)
             _, _, block, _ = pair_info(table, chip, target, core, many, which)
@@ -91,14 +101,23 @@
             source = chip_at(x, z, -dx, -dz)
             live, side, block, own_block = pair_info(table, source, chip, core, many, which)
             mine = jnp.where(side == core, 0, blocks) + own_block
-            filled = plan[base + mine]
-            plan[lists + mine * (slots + 2) + filled] = jnp.where(live, slot, slots)
-            plan[lists + mine * (slots + 2) + filled + 1] = slots
-            plan[base + mine] = filled + live.astype(jnp.int32)
+            count = plan[groups]
+            joins = (plan[base + mine] & 1) == 1
+            group = jnp.where(live, jnp.where(joins, latest[mine], count), slots + 1)
+            plan[own_of + group] = mine
+            plan[first_of + group] = jnp.where(joins, plan[first_of + group], slot)
+            plan[second_of + group] = jnp.where(joins, slot, slots)
+            latest[mine] = jnp.where(live, group, latest[mine])
+            plan[groups] = count + (live & jnp.logical_not(joins)).astype(jnp.int32)
+            plan[base + mine] = plan[base + mine] + live.astype(jnp.int32)
             plan[counts + slot] = valid[(source * n_core + core) * blocks + block] - start
             plan[at_row + number] = 2 * source + which
             number += 1
         plan[counts + slots] = 0
+        count = plan[groups]
+        plan[own_of + count] = plan[own_of]
+        plan[first_of + count] = slots
+        plan[second_of + count] = slots
 
 
 def prep_kernel(table, emb, units, to0, to1, to2, to3, around, raw, unit, sem_in, sems):
@@ -191,7 +210,7 @@
 def pair_kernel(stage, feeds, plan, own, *refs):
     final = stage == len(stages) - 1
     slots, base = len(stages[stage]), at_stage[stage]
-    counts, lists = base + 2 * blocks, base + 2 * blocks + slots + 1
+    counts, groups, own_of, first_of, second_of = places(stages[stage], base)
     units, held, cols, sem_u, sem_g = refs[-5:]
     outs, arrays, past = refs[-8 if final else -7 : -5], refs, ()
     if final:
@@ -227,33 +246,33 @@
     for copy in gets:
         copy.wait()
     for o in range(2 * blocks):
-        own_count = plan[at_own + o]
 
         @pl.when(plan[base + o] > 0)
         def _():
             loads[o].wait()
 
-        def visit(turn, carry):
-            at = lists + o * (slots + 2) + 2 * turn
-            pair = [plan[at], plan[at + 1]]
-            here_slot = [pair[0], jnp.minimum(pair[1], slots - 1)]
+    def visit(turn, carry):
+        for group in (2 * turn, 2 * turn + 1):
+            o = plan[own_of + group]
+            pair = [plan[first_of + group], plan[second_of + group]]
+            here_slot = [jnp.minimum(slot, slots - 1) for slot in pair]
             scores = dot_t(
                 jnp.concatenate([held[here_slot[0]], held[here_slot[1]]], axis=0), units[o]
             )
-            ok = jnp.where(lane < own_count, scores, absent)
+            ok = jnp.where(lane < plan[at_own + o], scores, absent)
             folded = jnp.maximum(
                 jnp.maximum(ok[:, 0:128], ok[:, 128:256]), jnp.maximum(ok[:, 256:384], ok[:, 384:512])
             )
-            top = row_out[o : o + 1, :]
+            top = jnp.full((1, rows), absent, jnp.float32)
             for half in range(2):
                 span = slice(half * quarter, (half + 1) * quarter)
                 here = jnp.where(part < plan[counts + pair[half]], scores[span], absent)
                 top = jnp.maximum(top, jnp.max(here, axis=0, keepdims=True))
                 cols[pl.ds(pair[half], 1), :] = jnp.max(folded[span].T, axis=0, keepdims=True)
-            row_out[o : o + 1, :] = top
-            return carry
-
-        lax.fori_loop(0, (plan[base + o] + 1) >> 1, visit, 0)
+            row_out[pl.ds(o, 1), :] = jnp.maximum(row_out[pl.ds(o, 1), :], top)
+        return carry
+
+    lax.fori_loop(0, (plan[groups] + 1) >> 1, visit, 0)
     if final:
         outs[2][...] = row_out[blocks:]
         for slot in range(slots):
@@ -279,19 +298,19 @@
             best[pl.ds(block, 1), :], back[pl.ds(plan[at_back_row + number], 1), :]
         )
     merged = jnp.maximum(jnp.maximum(local[...], row_best[0:blocks]), sib_rows[...])
-    out[...] = spread_in(merged, best[...], rep)
-
-
-def finish_kernel(plan, one, two, three, four, out):
+    merged = spread_in(merged, best[...], rep)
+    lane = lax.broadcasted_iota(jnp.int32, (1, rows), 1)
+    for b in range(blocks):
+        out[b : b + 1, :] = jnp.where(lane < plan[at_own + b], merged[b : b + 1], -1.0)
+
+
+def finish_kernel(one, two, three, four, out):
     best = jnp.maximum(jnp.maximum(one[...], two[...]), jnp.maximum(three[...], four[...]))
-    lane = lax.broadcasted_iota(jnp.int32, (1, quarter), 1)
     for b in range(blocks):
-        count = plan[at_own + b]
         for q in range(n_rep):
-            span = best[b : b + 1, q * quarter : (q + 1) * quarter]
-            out[n_rep * b + q : n_rep * b + q + 1, :] = jnp.where(
-                lane + q * quarter < count, span, -1.0
-            )
+            out[n_rep * b + q : n_rep * b + q + 1, :] = best[
+                b : b + 1, q * quarter : (q + 1) * quarter
+            ]
 
 
 def move(value, dx, dz):
@@ -307,7 +326,10 @@
     smem = pl.BlockSpec(memory_space=pltpu.SMEM)
     vmem = pl.BlockSpec(memory_space=pltpu.VMEM)
     hbm = pl.BlockSpec(memory_space=pl.ANY)
+    pinned = pl.BlockSpec(memory_space=pltpu.HBM)
     params = pltpu.CompilerParams(vmem_limit_bytes=vmem_bytes)
+    middle = pltpu.CompilerParams(vmem_limit_bytes=56 << 20)
+    small = pltpu.CompilerParams(vmem_limit_bytes=8 << 20)
     cost = pl.CostEstimate(flops=0, bytes_accessed=1 << 16, transcendentals=0)
     f32, bf16 = jnp.float32, jnp.bfloat16
     part = (quarter, width)
@@ -328,7 +350,7 @@
                 pltpu.SemaphoreType.DMA((3 * n,)),
                 pltpu.SemaphoreType.DMA((n,)),
             ],
-            compiler_params=params,
+            compiler_params=middle,
             cost_estimate=cost,
             name=name,
         )(plan, *held, *after)
@@ -341,7 +363,7 @@
         return pl.pallas_call(
             functools.partial(pair_kernel, stage, feeds),
             out_shape=[jax.ShapeDtypeStruct(shape, f32) for shape in shapes],
-            in_specs=[smem, hbm] + [vmem] * len(past) + [hbm] * len(arrays + after),
+            in_specs=[smem, pinned] + [vmem] * len(past) + [hbm] * len(arrays + after),
             out_specs=[vmem] * len(shapes),
             scratch_shapes=[
                 pltpu.VMEM((2 * blocks, rows, width), bf16),
@@ -350,7 +372,7 @@
                 pltpu.SemaphoreType.DMA((2 * blocks,)),
                 pltpu.SemaphoreType.DMA((len(feeds),)),
             ],
-            compiler_params=params,
+            compiler_params=middle,
             cost_estimate=cost,
             name=name,
         )(plan, units, *past, *arrays, *after)
@@ -384,6 +406,7 @@
         out_shape=jax.ShapeDtypeStruct((plan_size,), jnp.int32),
         in_specs=[smem, smem, hbm],
         out_specs=smem,
+        scratch_shapes=[pltpu.SMEM((2 * blocks,), jnp.int32)],
         compiler_params=params,
         cost_estimate=cost,
         name="plan",
@@ -452,6 +475,7 @@
         in_specs=[smem, vmem, vmem, vmem, vmem],
         out_specs=vmem,
         scratch_shapes=[pltpu.VMEM((blocks, quarter), f32)],
+        compiler_params=small,
         cost_estimate=cost,
         name="merge",
     )(plan, local_best, row_best, sib_rows, back)
@@ -462,11 +486,12 @@
     result = pl.pallas_call(
         finish_kernel,
         out_shape=jax.ShapeDtypeStruct((blocks * n_rep, quarter), f32),
-        in_specs=[smem, vmem, vmem, vmem, vmem],
+        in_specs=[vmem, vmem, vmem, vmem],
         out_specs=vmem,
+        compiler_params=small,
         cost_estimate=cost,
         name="finish",
-    )(plan, combined, *others)
+    )(combined, *others)
     return result.reshape(-1)
 
 

time: 175 us -> 171 us (0.977)
  Pallas kernels: 63.6 us -> 60.7 us
  transfers between devices with their start and end apart: 21 -> 21, of which waited for: 10 -> 12; matrix products, arithmetic and copies ran while one was open for 1% -> 0% of each run, Pallas kernels for 27% -> 27%
where the time goes in v3:
time: 171 us; the launch traced here: 170 us
  Pallas kernels  60.7 us (35%)
  waiting for transfers between devices  52.9 us (31%)
  starting transfers between devices  51.8 us (30%)
  local copies, waits for them, and re-layouts  3.96 us (2%)
    ppermute x14, waiting for transfers between devices, move(): return lax.ppermute(value, ('x', 'z'), steps)  37.8 us
    ppermute x14, starting transfers between devices, move(): return lax.ppermute(value, ('x', 'z'), steps)  36.1 us
    pallas_call x3, Pallas kernels, compare(): pl.pallas_call(functools.partial(pair_kernel, stage, feeds), out_shape=[j...  22.9 us
    pallas_call x1, Pallas kernels, on_device(): pl.pallas_call(local_kernel, grid=(2 * blocks,), out_shape=(jax.ShapeDtyp...  21.8 us
    all_to_all x1, waiting for transfers between devices, on_device(): lax.all_to_all(col_best, ('x', 'z'), split_axis=0, concat_axis=0, tiled=T...  8.37 us
    all_to_all x1, starting transfers between devices, on_device(): lax.all_to_all(col_best, ('x', 'z'), split_axis=0, concat_axis=0, tiled=T...  8.16 us
    pallas_call x2, Pallas kernels, pick(): pl.pallas_call(functools.partial(pick_kernel, wanted, spread), out_shape=...  7.56 us
    ppermute x3, waiting for transfers between devices, on_device(): lax.ppermute(combined, 'rep', [(y, (y + d) % n_rep) for y in range(n_rep)])  4.95 us
  transfers between devices with their start and end apart: 21, of which 12 were waited for; matrix products, arithmetic and copies ran while one was open for 0% of the time, Pallas kernels for 27%

profile of v3, /device:TPU:24, one launch (start us, length us, event | category | flops | bytes accessed | tf_op | source)
XLA Modules:
  0.0 169.6 jit_solution(6274583597008111162)
XLA Ops:
  0.0 0.0 collective-permute-start.5
  0.0 4.4 %prep.1 = (bf16[8,128,768]{2,1,0:T(8,128)(2,1)}, bf16[1,128,768]{2,1,0:T(8,128)(2,1)}, bf16[1,128,768]{2,1,0:T(8,128)(2,1)}, bf16[1,128,768]{2,1,0:T(8,128)(2,1)...) custom-call(s32[64,64]{1,0:T(8,128)} %table.3, bf16[8,512,768]{2,1,0:T(8,128)(2,1)} %bitcast.6), custom_call_target="tpu_custom_call" | custom-call | bytes 65536 | tf_op jit(solution)/shard_map/prep/pallas_call | solution.py:383
  4.4 2.0 %collective-permute-start = (bf16[8,128,768]{2,1,0:T(8,128)(2,1)}, bf16[8,128,768]{2,1,0:T(8,128)(2,1)S(1)}, u32[]{:S(2)}, u32[]{:S(2)}) collective-permute-start(bf16[8,128,768]{2,1,0:T(8,128)(2,1)} %get-tuple-element.38.cols.after.refs_0_), channel_id=1, source_target_pairs={{0,8},{8,16},{16,24},{24,32},{32,40},{40,48},{48,56},{56,0},{64,72... | collective-permute-start | bytes 4718600 | tf_op jit(solution)/shard_map/ppermute | solution.py:322
  6.4 5.4 %collective-permute-start.1 = (bf16[1,128,768]{2,1,0:T(8,128)(2,1)}, bf16[1,128,768]{2,1,0:T(8,128)(2,1)S(1)}, u32[]{:S(2)}, u32[]{:S(2)}) collective-permute-start(bf16[1,128,768]{2,1,0:T(8,128)(2,1)} %get-tuple-element.39), channel_id=1, source_target_pairs={{0,48},{8,56},{16,0},{24,8},{32,16},{40,24},{48,32},{56,40},{64,11... | collective-permute-start | bytes 589832 | tf_op jit(solution)/shard_map/ppermute | solution.py:322
  11.8 2.4 %collective-permute-start.2 = (bf16[1,128,768]{2,1,0:T(8,128)(2,1)}, bf16[1,128,768]{2,1,0:T(8,128)(2,1)S(1)}, u32[]{:S(2)}, u32[]{:S(2)}) collective-permute-start(bf16[1,128,768]{2,1,0:T(8,128)(2,1)} %get-tuple-element.40), channel_id=1, source_target_pairs={{0,112},{8,120},{16,64},{24,72},{32,80},{40,88},{48,96},{56,104},{... | collective-permute-start | bytes 589832 | tf_op jit(solution)/shard_map/ppermute | solution.py:322
  14.1 2.7 %collective-permute-start.3 = (bf16[1,128,768]{2,1,0:T(8,128)(2,1)}, bf16[1,128,768]{2,1,0:T(8,128)(2,1)S(1)}, u32[]{:S(2)}, u32[]{:S(2)}) collective-permute-start(bf16[1,128,768]{2,1,0:T(8,128)(2,1)} %get-tuple-element.41), channel_id=1, source_target_pairs={{0,176},{8,184},{16,128},{24,136},{32,144},{40,152},{48,160},{56,1... | collective-permute-start | bytes 589832 | tf_op jit(solution)/shard_map/ppermute | solution.py:322
  16.9 0.0 collective-permute-done.5.sib
  16.9 2.1 %collective-permute-start.4 = (bf16[1,128,768]{2,1,0:T(8,128)(2,1)}, bf16[1,128,768]{2,1,0:T(8,128)(2,1)S(1)}, u32[]{:S(2)}, u32[]{:S(2)}) collective-permute-start(bf16[1,128,768]{2,1,0:T(8,128)(2,1)} %get-tuple-element.42), channel_id=1, source_target_pairs={{0,240},{8,248},{16,192},{24,200},{32,208},{40,216},{48,224},{56,2... | collective-permute-start | bytes 589832 | tf_op jit(solution)/shard_map/ppermute | solution.py:322
  19.0 2.8 %plan.1 = s32[344]{0:T(512)} custom-call(s32[64,64]{1,0:T(8,128)} %table.3, s32[512]{0:T(512)} %valid.3, bf16[8,128,768]{2,1,0:T(8,128)(2,1)} %get-tuple-element.38.cols.after.refs_0_), custom_call_target="tpu_custom_call" | custom-call | bytes 65536 | tf_op jit(solution)/shard_map/plan/pallas_call | solution.py:404
  21.8 21.8 %local.1 = (bf16[16,512,768]{2,1,0:T(8,128)(2,1)}, f32[8,512]{1,0:T(8,128)}) custom-call(s32[512]{0:T(512)} %valid.3, bf16[8,512,768]{2,1,0:T(8,128)(2,1)} %bitcast.7, bf16[8,512,768]{2,1,0:T(8,128)(2,1)} %collective-permute-done.5.sib, bf16[8,128,768]{2,1,0:T(8,128)(2,1)} %get-tuple-element.38.cols.after.refs_0_), custom_call_target="tpu_custom_call" | custom-call | bytes 65536 | tf_op jit(solution)/shard_map/local/pallas_call | solution.py:414
  43.6 0.0 collective-permute-done.1
  43.6 0.0 collective-permute-done.2
  43.6 0.0 collective-permute-done.3
  43.6 2.5 %collective-permute-done.4 = bf16[1,128,768]{2,1,0:T(8,128)(2,1)S(1)} collective-permute-done((bf16[1,128,768]{2,1,0:T(8,128)(2,1)}, bf16[1,128,768]{2,1,0:T(8,128)(2,1)S(1)}, u32[]{:S(2)}, u32[]{:S(2)}) %collective-permute-start.4) | collective-permute-done | bytes 196640 | tf_op jit(solution)/shard_map/ppermute | solution.py:322
  46.1 0.0 collective-permute-done.refs_1_
  46.1 2.5 %collective-permute-start.9 = (bf16[8,128,768]{2,1,0:T(8,128)(2,1)S(1)}, bf16[8,128,768]{2,1,0:T(8,128)(2,1)S(1)}, u32[]{:S(2)}, u32[]{:S(2)}) collective-permute-start(bf16[8,128,768]{2,1,0:T(8,128)(2,1)S(1)} %collective-permute-done.refs_1_), channel_id=1, source_target_pairs={{0,8},{8,16},{16,24},{24,32},{32,40},{40,48},{48,56},{56,0},{64,72... | collective-permute-start | bytes 4718600 | tf_op jit(solution)/shard_map/ppermute | solution.py:322
  48.6 0.1 pad_maximum_fusion
  48.7 3.0 %collective-permute-start.10 = (bf16[4,128,768]{2,1,0:T(8,128)(2,1)S(1)}, bf16[4,128,768]{2,1,0:T(8,128)(2,1)S(1)}, u32[]{:S(2)}, u32[]{:S(2)}) collective-permute-start(bf16[4,128,768]{2,1,0:T(8,128)(2,1)S(1)} %pad_maximum_fusion), channel_id=1, source_target_pairs={{0,48},{8,56},{16,0},{24,8},{32,16},{40,24},{48,32},{56,40},{64,11... | collective-permute-start | bytes 2359304 | tf_op jit(solution)/shard_map/ppermute | solution.py:322
  51.7 0.0 copy-done.7
  51.7 3.4 %pick_a.1 = (bf16[3,128,768]{2,1,0:T(8,128)(2,1)}, bf16[3,128,768]{2,1,0:T(8,128)(2,1)}, bf16[3,128,768]{2,1,0:T(8,128)(2,1)}, bf16[3,128,768]{2,1,0:T(8,128)(2,1)}) custom-call(s32[344]{0:T(512)} %plan.1, bf16[8,128,768]{2,1,0:T(8,128)(2,1)} %get-tuple-element.38.cols.after.refs_0_, bf16[8,128,768]{2,1,0:T(8,128)(2,1)} %copy-done.7), custom_call_target="tpu_custom_call" | custom-call | bytes 65536 | tf_op jit(solution)/shard_map/pick_a/pallas_call | solution.py:343
  55.1 1.8 %collective-permute-start.6 = (bf16[3,128,768]{2,1,0:T(8,128)(2,1)}, bf16[3,128,768]{2,1,0:T(8,128)(2,1)S(1)}, u32[]{:S(2)}, u32[]{:S(2)}) collective-permute-start(bf16[3,128,768]{2,1,0:T(8,128)(2,1)} %get-tuple-element.49), channel_id=1, source_target_pairs={{0,64},{8,72},{16,80},{24,88},{32,96},{40,104},{48,112},{56,120},{... | collective-permute-start | bytes 1769480 | tf_op jit(solution)/shard_map/ppermute | solution.py:322
  57.0 1.8 %collective-permute-start.7 = (bf16[3,128,768]{2,1,0:T(8,128)(2,1)}, bf16[3,128,768]{2,1,0:T(8,128)(2,1)S(1)}, u32[]{:S(2)}, u32[]{:S(2)}) collective-permute-start(bf16[3,128,768]{2,1,0:T(8,128)(2,1)} %get-tuple-element.50), channel_id=1, source_target_pairs={{0,128},{8,136},{16,144},{24,152},{32,160},{40,168},{48,176},{56,1... | collective-permute-start | bytes 1769480 | tf_op jit(solution)/shard_map/ppermute | solution.py:322
  58.8 2.2 %collective-permute-start.8 = (bf16[3,128,768]{2,1,0:T(8,128)(2,1)}, bf16[3,128,768]{2,1,0:T(8,128)(2,1)S(1)}, u32[]{:S(2)}, u32[]{:S(2)}) collective-permute-start(bf16[3,128,768]{2,1,0:T(8,128)(2,1)} %get-tuple-element.51), channel_id=1, source_target_pairs={{0,192},{8,200},{16,208},{24,216},{32,224},{40,232},{48,240},{56,2... | collective-permute-start | bytes 1769480 | tf_op jit(solution)/shard_map/ppermute | solution.py:322
  61.0 23.4 %collective-permute-done.10.refs_4_ = bf16[4,128,768]{2,1,0:T(8,128)(2,1)S(1)} collective-permute-done((bf16[4,128,768]{2,1,0:T(8,128)(2,1)S(1)}, bf16[4,128,768]{2,1,0:T(8,128)(2,1)S(1)}, u32[]{:S(2)}, u32[]{:S(2)}) %collective-permute-start.10) | collective-permute-done | bytes 786464 | tf_op jit(solution)/shard_map/ppermute | solution.py:322
  84.4 0.0 collective-permute-done.9.refs_1_
  84.4 0.0 collective-permute-done.6.refs_3_.refs_1_
  84.4 0.0 copy-start.4
  84.4 0.0 collective-permute-done.7.refs_4_.refs_2_
  84.4 0.5 collective-permute-done.8.refs_5_.refs_3_
  84.9 0.7 copy-done.8
  85.6 0.2 copy-done.4
  85.8 0.2 copy-done.5
  86.0 0.2 copy-done.6
  86.1 4.1 %pick_b.1 = (bf16[2,128,768]{2,1,0:T(8,128)(2,1)}, bf16[2,128,768]{2,1,0:T(8,128)(2,1)}, bf16[2,128,768]{2,1,0:T(8,128)(2,1)}, bf16[4,2,128,768]{3,2,1,0:T(8,128)(2,1)}) custom-call(s32[344]{0:T(512)} %plan.1, bf16[8,128,768]{2,1,0:T(8,128)(2,1)} %get-tuple-element.38.cols.after.refs_0_, bf16[8,128,768]{2,1,0:T(8,128)(2,1)} %copy-done.8, ...), custom_call_target="tpu_custom_call" | custom-call | bytes 65536 | tf_op jit(solution)/shard_map/pick_b/pallas_call | solution.py:343
  90.3 4.5 %all-to-all-start = ((bf16[4,2,128,768]{3,2,1,0:T(8,128)(2,1)}), bf16[4,2,128,768]{3,2,1,0:T(8,128)(2,1)S(1)}, u32[]{:S(2)}, u32[]{:S(2)}) async-start(bf16[4,2,128,768]{3,2,1,0:T(8,128)(2,1)} %get-tuple-element.67), calls=%async_computation | async-start | bytes 3145728 | tf_op jit(solution)/shard_map/all_to_all | solution.py:443
  94.8 2.0 %collective-permute-start.11 = (bf16[2,128,768]{2,1,0:T(8,128)(2,1)S(1)}, bf16[2,128,768]{2,1,0:T(8,128)(2,1)S(1)}, u32[]{:S(2)}, u32[]{:S(2)}) collective-permute-start(bf16[2,128,768]{2,1,0:T(8,128)(2,1)S(1)} %copy-done.14), channel_id=1, source_target_pairs={{0,8},{8,16},{16,24},{24,32},{32,40},{40,48},{48,56},{56,0},{64,72... | collective-permute-start | bytes 1179656 | tf_op jit(solution)/shard_map/ppermute | solution.py:322
  96.8 1.5 collective-permute-start.12
  98.3 3.7 %collective-permute-start.13 = (bf16[2,128,768]{2,1,0:T(8,128)(2,1)}, bf16[2,128,768]{2,1,0:T(8,128)(2,1)S(1)}, u32[]{:S(2)}, u32[]{:S(2)}) collective-permute-start(bf16[2,128,768]{2,1,0:T(8,128)(2,1)} %get-tuple-element.65), channel_id=1, source_target_pairs={{0,200},{8,208},{16,216},{24,224},{32,232},{40,240},{48,248},{56,1... | collective-permute-start | bytes 1179656 | tf_op jit(solution)/shard_map/ppermute | solution.py:322
  102.0 3.0 %collective-permute-start.14 = (bf16[2,128,768]{2,1,0:T(8,128)(2,1)}, bf16[2,128,768]{2,1,0:T(8,128)(2,1)S(1)}, u32[]{:S(2)}, u32[]{:S(2)}) collective-permute-start(bf16[2,128,768]{2,1,0:T(8,128)(2,1)} %get-tuple-element.66), channel_id=1, source_target_pairs={{0,168},{8,176},{16,184},{24,128},{32,136},{40,144},{48,152},{56,1... | collective-permute-start | bytes 1179656 | tf_op jit(solution)/shard_map/ppermute | solution.py:322
  104.9 9.1 %pairs_a.1 = (f32[16,512]{1,0:T(8,128)}, f32[16,128]{1,0:T(8,128)}) custom-call(s32[344]{0:T(512)} %plan.1, bf16[16,512,768]{2,1,0:T(8,128)(2,1)} %get-tuple-element.46.own, bf16[3,128,768]{2,1,0:T(8,128)(2,1)} %get-tuple-element.48.refs_2_.refs_0_, bf16[3,128,768]{2,1,0:T(8,128)(2,1)} %copy-done.4, bf16[3,128,768]{2,1,0:T(8,128)(2,1)} %copy-done.5, ...), custom_call_target="tpu_custom_call" | custom-call | bytes 65536 | tf_op jit(solution)/shard_map/pairs_a/pallas_call | solution.py:363
  114.1 0.0 collective-permute-done.11.refs_0_
  114.1 0.0 copy-start.10
  114.1 5.8 %collective-permute-done.12.refs_1_ = bf16[2,128,768]{2,1,0:T(8,128)(2,1)S(1)} collective-permute-done((bf16[2,128,768]{2,1,0:T(8,128)(2,1)}, bf16[2,128,768]{2,1,0:T(8,128)(2,1)S(1)}, u32[]{:S(2)}, u32[]{:S(2)}) %collective-permute-start.12) | collective-permute-done | bytes 393248 | tf_op jit(solution)/shard_map/ppermute | solution.py:322
  119.9 0.8 copy-done.11
  120.6 4.9 %pairs_b.1 = (f32[16,512]{1,0:T(8,128)}, f32[4,128]{1,0:T(4,128)}) custom-call(s32[344]{0:T(512)} %plan.1, bf16[16,512,768]{2,1,0:T(8,128)(2,1)} %get-tuple-element.46.own, bf16[2,128,768]{2,1,0:T(8,128)(2,1)} %copy-done.10, bf16[2,128,768]{2,1,0:T(8,128)(2,1)} %copy-done.11, f32[16,512]{1,0:T(8,128)} %get-tuple-element.60.refs_2_.refs_0_), custom_call_target="tpu_custom_call" | custom-call | bytes 65536 | tf_op jit(solution)/shard_map/pairs_b/pallas_call | solution.py:363
  125.6 1.3 collective-permute-done.13.refs_4_
  126.9 4.3 %collective-permute-done.14.refs_5_ = bf16[2,128,768]{2,1,0:T(8,128)(2,1)S(1)} collective-permute-done((bf16[2,128,768]{2,1,0:T(8,128)(2,1)}, bf16[2,128,768]{2,1,0:T(8,128)(2,1)S(1)}, u32[]{:S(2)}, u32[]{:S(2)}) %collective-permute-start.14) | collective-permute-done | bytes 393248 | tf_op jit(solution)/shard_map/ppermute | solution.py:322
  131.2 0.4 all-to-all-done.refs_6_
  131.7 0.4 copy-done.13
  132.0 0.8 copy-done.3
  132.8 8.8 %pairs_c.1 = (f32[16,512]{1,0:T(8,128)}, f32[64,128]{1,0:T(8,128)}, f32[8,512]{1,0:T(8,128)}) custom-call(s32[344]{0:T(512)} %plan.1, bf16[16,512,768]{2,1,0:T(8,128)(2,1)} %get-tuple-element.46.own, f32[16,512]{1,0:T(8,128)} %get-tuple-element.60.refs_2_.refs_0_, f32[16,128]{1,0:T(8,128)} %get-tuple-element.61.refs_1_, ...), custom_call_target="tpu_custom_call" | custom-call | bytes 65536 | tf_op jit(solution)/shard_map/pairs_c/pallas_call | solution.py:363
  141.6 8.2 %all-to-all-start.1 = ((f32[32,2,128]{2,1,0:T(2,128)}), f32[32,2,128]{2,1,0:T(2,128)S(1)}, u32[]{:S(2)}, u32[]{:S(2)}) async-start(f32[32,2,128]{2,1,0:T(2,128)} %bitcast.8), calls=%async_computation.1 | async-start | bytes 65536 | tf_op jit(solution)/shard_map/all_to_all | solution.py:471
  149.8 0.1 collective-permute-start.15
  149.9 1.4 collective-permute-done.15.sib_rows
  151.3 8.4 %all-to-all-done.1 = f32[32,2,128]{2,1,0:T(2,128)S(1)} async-done(((f32[32,2,128]{2,1,0:T(2,128)}), f32[32,2,128]{2,1,0:T(2,128)S(1)}, u32[]{:S(2)}, u32[]{:S(2)}) %all-to-all-start.1) | async-done | bytes 32800 | tf_op jit(solution)/shard_map/all_to_all | solution.py:471
  159.7 0.8 copy-done.1
  160.4 0.7 merge.1.one
  161.2 0.3 collective-permute-start.16
  161.5 2.6 %collective-permute-start.17 = (f32[8,512]{1,0:T(8,128)S(1)}, f32[8,512]{1,0:T(8,128)S(1)}, u32[]{:S(2)}, u32[]{:S(2)}) collective-permute-start(f32[8,512]{1,0:T(8,128)S(1)} %merge.1.one), channel_id=1, source_target_pairs={{0,2},{1,3},{2,0},{3,1},{4,6},{5,7},{6,4},{7,5},{8,10},{9,11},{10,... | collective-permute-start | bytes 49160 | tf_op jit(solution)/shard_map/ppermute | solution.py:483
  164.0 0.0 collective-permute-start.18
  164.0 0.9 collective-permute-done.16.two
  165.0 1.8 %collective-permute-done.17.three = f32[8,512]{1,0:T(8,128)S(1)} collective-permute-done((f32[8,512]{1,0:T(8,128)S(1)}, f32[8,512]{1,0:T(8,128)S(1)}, u32[]{:S(2)}, u32[]{:S(2)}) %collective-permute-start.17) | collective-permute-done | bytes 16416 | tf_op jit(solution)/shard_map/ppermute | solution.py:483
  166.7 2.3 %collective-permute-done.18.four = f32[8,512]{1,0:T(8,128)S(1)} collective-permute-done((f32[8,512]{1,0:T(8,128)S(1)}, f32[8,512]{1,0:T(8,128)S(1)}, u32[]{:S(2)}, u32[]{:S(2)}) %collective-permute-start.18) | collective-permute-done | bytes 16416 | tf_op jit(solution)/shard_map/ppermute | solution.py:483
  169.0 0.6 finish.1
  (19 shorter events, 0.0 us)
Async XLA Ops:
  0.0 16.9 %collective-permute-start.5 = (bf16[8,512,768]{2,1,0:T(8,128)(2,1)}, bf16[8,512,768]{2,1,0:T(8,128)(2,1)}, u32[]{:S(2)}, u32[]{:S(2)}) collective-permute-start(bf16[8,512,768]{2,1,0:T(8,128)(2,1)} %bitcast.5), channel_id=1, source_target_pairs={{0,4},{4,0},{1,5},{5,1},{2,6},{6,2},{3,7},{7,3},{8,12},{12,8},{9,1... | collective-permute-start | bytes 18874376 | tf_op jit(solution)/shard_map/ppermute | solution.py:401
  4.4 41.7 %collective-permute-start = (bf16[8,128,768]{2,1,0:T(8,128)(2,1)}, bf16[8,128,768]{2,1,0:T(8,128)(2,1)S(1)}, u32[]{:S(2)}, u32[]{:S(2)}) collective-permute-start(bf16[8,128,768]{2,1,0:T(8,128)(2,1)} %get-tuple-element.38.cols.after.refs_0_), channel_id=1, source_target_pairs={{0,8},{8,16},{16,24},{24,32},{32,40},{40,48},{48,56},{56,0},{64,72... | collective-permute-start | bytes 4718600 | tf_op jit(solution)/shard_map/ppermute | solution.py:322
  6.4 37.3 %collective-permute-start.1 = (bf16[1,128,768]{2,1,0:T(8,128)(2,1)}, bf16[1,128,768]{2,1,0:T(8,128)(2,1)S(1)}, u32[]{:S(2)}, u32[]{:S(2)}) collective-permute-start(bf16[1,128,768]{2,1,0:T(8,128)(2,1)} %get-tuple-element.39), channel_id=1, source_target_pairs={{0,48},{8,56},{16,0},{24,8},{32,16},{40,24},{48,32},{56,40},{64,11... | collective-permute-start | bytes 589832 | tf_op jit(solution)/shard_map/ppermute | solution.py:322
  11.8 31.9 %collective-permute-start.2 = (bf16[1,128,768]{2,1,0:T(8,128)(2,1)}, bf16[1,128,768]{2,1,0:T(8,128)(2,1)S(1)}, u32[]{:S(2)}, u32[]{:S(2)}) collective-permute-start(bf16[1,128,768]{2,1,0:T(8,128)(2,1)} %get-tuple-element.40), channel_id=1, source_target_pairs={{0,112},{8,120},{16,64},{24,72},{32,80},{40,88},{48,96},{56,104},{... | collective-permute-start | bytes 589832 | tf_op jit(solution)/shard_map/ppermute | solution.py:322
  14.1 29.5 %collective-permute-start.3 = (bf16[1,128,768]{2,1,0:T(8,128)(2,1)}, bf16[1,128,768]{2,1,0:T(8,128)(2,1)S(1)}, u32[]{:S(2)}, u32[]{:S(2)}) collective-permute-start(bf16[1,128,768]{2,1,0:T(8,128)(2,1)} %get-tuple-element.41), channel_id=1, source_target_pairs={{0,176},{8,184},{16,128},{24,136},{32,144},{40,152},{48,160},{56,1... | collective-permute-start | bytes 589832 | tf_op jit(solution)/shard_map/ppermute | solution.py:322
  16.9 29.2 %collective-permute-start.4 = (bf16[1,128,768]{2,1,0:T(8,128)(2,1)}, bf16[1,128,768]{2,1,0:T(8,128)(2,1)S(1)}, u32[]{:S(2)}, u32[]{:S(2)}) collective-permute-start(bf16[1,128,768]{2,1,0:T(8,128)(2,1)} %get-tuple-element.42), channel_id=1, source_target_pairs={{0,240},{8,248},{16,192},{24,200},{32,208},{40,216},{48,224},{56,2... | collective-permute-start | bytes 589832 | tf_op jit(solution)/shard_map/ppermute | solution.py:322
  46.1 5.6 %copy-start.7 = (bf16[8,128,768]{2,1,0:T(8,128)(2,1)}, bf16[8,128,768]{2,1,0:T(8,128)(2,1)S(1)}, u32[]{:S(2)}) copy-start(bf16[8,128,768]{2,1,0:T(8,128)(2,1)S(1)} %collective-permute-done.refs_1_) | copy-start | bytes 4718596
  46.1 38.3 %collective-permute-start.9 = (bf16[8,128,768]{2,1,0:T(8,128)(2,1)S(1)}, bf16[8,128,768]{2,1,0:T(8,128)(2,1)S(1)}, u32[]{:S(2)}, u32[]{:S(2)}) collective-permute-start(bf16[8,128,768]{2,1,0:T(8,128)(2,1)S(1)} %collective-permute-done.refs_1_), channel_id=1, source_target_pairs={{0,8},{8,16},{16,24},{24,32},{32,40},{40,48},{48,56},{56,0},{64,72... | collective-permute-start | bytes 4718600 | tf_op jit(solution)/shard_map/ppermute | solution.py:322
  48.7 35.6 %collective-permute-start.10 = (bf16[4,128,768]{2,1,0:T(8,128)(2,1)S(1)}, bf16[4,128,768]{2,1,0:T(8,128)(2,1)S(1)}, u32[]{:S(2)}, u32[]{:S(2)}) collective-permute-start(bf16[4,128,768]{2,1,0:T(8,128)(2,1)S(1)} %pad_maximum_fusion), channel_id=1, source_target_pairs={{0,48},{8,56},{16,0},{24,8},{32,16},{40,24},{48,32},{56,40},{64,11... | collective-permute-start | bytes 2359304 | tf_op jit(solution)/shard_map/ppermute | solution.py:322
  55.1 29.2 %collective-permute-start.6 = (bf16[3,128,768]{2,1,0:T(8,128)(2,1)}, bf16[3,128,768]{2,1,0:T(8,128)(2,1)S(1)}, u32[]{:S(2)}, u32[]{:S(2)}) collective-permute-start(bf16[3,128,768]{2,1,0:T(8,128)(2,1)} %get-tuple-element.49), channel_id=1, source_target_pairs={{0,64},{8,72},{16,80},{24,88},{32,96},{40,104},{48,112},{56,120},{... | collective-permute-start | bytes 1769480 | tf_op jit(solution)/shard_map/ppermute | solution.py:322
  57.0 27.4 %collective-permute-start.7 = (bf16[3,128,768]{2,1,0:T(8,128)(2,1)}, bf16[3,128,768]{2,1,0:T(8,128)(2,1)S(1)}, u32[]{:S(2)}, u32[]{:S(2)}) collective-permute-start(bf16[3,128,768]{2,1,0:T(8,128)(2,1)} %get-tuple-element.50), channel_id=1, source_target_pairs={{0,128},{8,136},{16,144},{24,152},{32,160},{40,168},{48,176},{56,1... | collective-permute-start | bytes 1769480 | tf_op jit(solution)/shard_map/ppermute | solution.py:322
  58.8 26.1 %collective-permute-start.8 = (bf16[3,128,768]{2,1,0:T(8,128)(2,1)}, bf16[3,128,768]{2,1,0:T(8,128)(2,1)S(1)}, u32[]{:S(2)}, u32[]{:S(2)}) collective-permute-start(bf16[3,128,768]{2,1,0:T(8,128)(2,1)} %get-tuple-element.51), channel_id=1, source_target_pairs={{0,192},{8,200},{16,208},{24,216},{32,224},{40,232},{48,240},{56,2... | collective-permute-start | bytes 1769480 | tf_op jit(solution)/shard_map/ppermute | solution.py:322
  84.4 20.6 %copy-start.9 = (bf16[4,128,768]{2,1,0:T(8,128)(2,1)}, bf16[4,128,768]{2,1,0:T(8,128)(2,1)S(1)}, u32[]{:S(2)}) copy-start(bf16[4,128,768]{2,1,0:T(8,128)(2,1)S(1)} %collective-permute-done.10.refs_4_) | copy-start | bytes 2359300
  84.4 1.2 copy-start.8
  84.4 1.4 copy-start.4
  84.4 1.5 copy-start.5
  84.9 1.3 copy-start.6
  90.3 4.5 %copy-start.14 = (bf16[2,128,768]{2,1,0:T(8,128)(2,1)S(1)}, bf16[2,128,768]{2,1,0:T(8,128)(2,1)}, u32[]{:S(2)}) copy-start(bf16[2,128,768]{2,1,0:T(8,128)(2,1)} %get-tuple-element.59.refs_5_) | copy-start | bytes 1179652
  90.3 41.4 %all-to-all-start = ((bf16[4,2,128,768]{3,2,1,0:T(8,128)(2,1)}), bf16[4,2,128,768]{3,2,1,0:T(8,128)(2,1)S(1)}, u32[]{:S(2)}, u32[]{:S(2)}) async-start(bf16[4,2,128,768]{3,2,1,0:T(8,128)(2,1)} %get-tuple-element.67), calls=%async_computation | async-start | bytes 3145728 | tf_op jit(solution)/shard_map/all_to_all | solution.py:443
  94.8 19.3 %collective-permute-start.11 = (bf16[2,128,768]{2,1,0:T(8,128)(2,1)S(1)}, bf16[2,128,768]{2,1,0:T(8,128)(2,1)S(1)}, u32[]{:S(2)}, u32[]{:S(2)}) collective-permute-start(bf16[2,128,768]{2,1,0:T(8,128)(2,1)S(1)} %copy-done.14), channel_id=1, source_target_pairs={{0,8},{8,16},{16,24},{24,32},{32,40},{40,48},{48,56},{56,0},{64,72... | collective-permute-start | bytes 1179656 | tf_op jit(solution)/shard_map/ppermute | solution.py:322
  96.8 23.1 %collective-permute-start.12 = (bf16[2,128,768]{2,1,0:T(8,128)(2,1)}, bf16[2,128,768]{2,1,0:T(8,128)(2,1)S(1)}, u32[]{:S(2)}, u32[]{:S(2)}) collective-permute-start(bf16[2,128,768]{2,1,0:T(8,128)(2,1)} %get-tuple-element.62), channel_id=1, source_target_pairs={{0,72},{8,80},{16,88},{24,96},{32,104},{40,112},{48,120},{56,64},{... | collective-permute-start | bytes 1179656 | tf_op jit(solution)/shard_map/ppermute | solution.py:322
  98.3 28.6 %collective-permute-start.13 = (bf16[2,128,768]{2,1,0:T(8,128)(2,1)}, bf16[2,128,768]{2,1,0:T(8,128)(2,1)S(1)}, u32[]{:S(2)}, u32[]{:S(2)}) collective-permute-start(bf16[2,128,768]{2,1,0:T(8,128)(2,1)} %get-tuple-element.65), channel_id=1, source_target_pairs={{0,200},{8,208},{16,216},{24,224},{32,232},{40,240},{48,248},{56,1... | collective-permute-start | bytes 1179656 | tf_op jit(solution)/shard_map/ppermute | solution.py:322
  102.0 29.3 %collective-permute-start.14 = (bf16[2,128,768]{2,1,0:T(8,128)(2,1)}, bf16[2,128,768]{2,1,0:T(8,128)(2,1)S(1)}, u32[]{:S(2)}, u32[]{:S(2)}) collective-permute-start(bf16[2,128,768]{2,1,0:T(8,128)(2,1)} %get-tuple-element.66), channel_id=1, source_target_pairs={{0,168},{8,176},{16,184},{24,128},{32,136},{40,144},{48,152},{56,1... | collective-permute-start | bytes 1179656 | tf_op jit(solution)/shard_map/ppermute | solution.py:322
  114.1 5.8 %copy-start.10 = (bf16[2,128,768]{2,1,0:T(8,128)(2,1)}, bf16[2,128,768]{2,1,0:T(8,128)(2,1)S(1)}, u32[]{:S(2)}) copy-start(bf16[2,128,768]{2,1,0:T(8,128)(2,1)S(1)} %collective-permute-done.11.refs_0_) | copy-start | bytes 1179652
  119.9 0.8 copy-start.11
  126.9 4.8 %copy-start.12 = (bf16[2,128,768]{2,1,0:T(8,128)(2,1)}, bf16[2,128,768]{2,1,0:T(8,128)(2,1)S(1)}, u32[]{:S(2)}) copy-start(bf16[2,128,768]{2,1,0:T(8,128)(2,1)S(1)} %collective-permute-done.13.refs_4_) | copy-start | bytes 1179652
  131.2 0.8 copy-start.13
  131.6 1.2 copy-start.3
  132.8 26.9 %copy-start = (s32[344]{0:T(512)S(1)}, s32[344]{0:T(512)}, u32[]{:S(2)}) copy-start(s32[344]{0:T(512)} %plan.1) | copy-start | bytes 4132
  132.8 26.9 %copy-start.2 = (f32[8,512]{1,0:T(8,128)S(1)}, f32[8,512]{1,0:T(8,128)}, u32[]{:S(2)}) copy-start(f32[8,512]{1,0:T(8,128)} %get-tuple-element.45.local) | copy-start | bytes 49156
  141.6 18.0 %all-to-all-start.1 = ((f32[32,2,128]{2,1,0:T(2,128)}), f32[32,2,128]{2,1,0:T(2,128)S(1)}, u32[]{:S(2)}, u32[]{:S(2)}) async-start(f32[32,2,128]{2,1,0:T(2,128)} %bitcast.8), calls=%async_computation.1 | async-start | bytes 65536 | tf_op jit(solution)/shard_map/all_to_all | solution.py:471
  149.8 1.5 collective-permute-start.15
  159.7 0.8 copy-start.1
  161.2 3.8 %collective-permute-start.16 = (f32[8,512]{1,0:T(8,128)S(1)}, f32[8,512]{1,0:T(8,128)S(1)}, u32[]{:S(2)}, u32[]{:S(2)}) collective-permute-start(f32[8,512]{1,0:T(8,128)S(1)} %merge.1.one), channel_id=1, source_target_pairs={{0,1},{1,2},{2,3},{3,0},{4,5},{5,6},{6,7},{7,4},{8,9},{9,10},{10,1... | collective-permute-start | bytes 49160 | tf_op jit(solution)/shard_map/ppermute | solution.py:483
  161.5 5.2 %collective-permute-start.17 = (f32[8,512]{1,0:T(8,128)S(1)}, f32[8,512]{1,0:T(8,128)S(1)}, u32[]{:S(2)}, u32[]{:S(2)}) collective-permute-start(f32[8,512]{1,0:T(8,128)S(1)} %merge.1.one), channel_id=1, source_target_pairs={{0,2},{1,3},{2,0},{3,1},{4,6},{5,7},{6,4},{7,5},{8,10},{9,11},{10,... | collective-permute-start | bytes 49160 | tf_op jit(solution)/shard_map/ppermute | solution.py:483
  164.0 4.9 %collective-permute-start.18 = (f32[8,512]{1,0:T(8,128)S(1)}, f32[8,512]{1,0:T(8,128)S(1)}, u32[]{:S(2)}, u32[]{:S(2)}) collective-permute-start(f32[8,512]{1,0:T(8,128)S(1)} %merge.1.one), channel_id=1, source_target_pairs={{0,3},{1,0},{2,1},{3,2},{4,7},{5,4},{6,5},{7,6},{8,11},{9,8},{10,9... | collective-permute-start | bytes 49160 | tf_op jit(solution)/shard_map/ppermute | solution.py:483

commit v4 on v3

--- a/solution.py
+++ b/solution.py
@@ -62,7 +62,7 @@
 at_stage, plan_size = [], 144
 for stage in stages:
     at_stage.append(plan_size)
-    plan_size += 16 + len(stage) + 1 + 1 + 3 * (len(stage) + 2)
+    plan_size += 16 + len(stage) + 1 + 1 + 4 * (len(stage) + 2)
 
 
 def places(stage, base):
@@ -70,7 +70,7 @@
     counts = base + 2 * blocks
     groups = counts + slots + 1
     own_of = groups + 1
-    return counts, groups, own_of, own_of + slots + 2, own_of + 2 * (slots + 2)
+    return counts, groups, own_of, *(own_of + k * (slots + 2) for k in (1, 2, 3))
 
 
 def plan_kernel(table, valid, after, plan, latest):
@@ -83,7 +83,7 @@
     number = 0
     for stage, base in zip(stages, at_stage):
         slots = len(stage)
-        counts, groups, own_of, first_of, second_of = places(stage, base)
+        counts, groups, own_of, first_of, second_of, fresh_of = places(stage, base)
         for o in range(2 * blocks):
             plan[base + o] = 0
             latest[o] = 0
@@ -105,6 +105,8 @@
             joins = (plan[base + mine] & 1) == 1
             group = jnp.where(live, jnp.where(joins, latest[mine], count), slots + 1)
             plan[own_of + group] = mine
+            fresh = (plan[base + mine] == 0).astype(jnp.int32)
+            plan[fresh_of + group] = jnp.where(joins, plan[fresh_of + group], fresh)
             plan[first_of + group] = jnp.where(joins, plan[first_of + group], slot)
             plan[second_of + group] = jnp.where(joins, slot, slots)
             latest[mine] = jnp.where(live, group, latest[mine])
@@ -117,6 +119,7 @@
         count = plan[groups]
         plan[own_of + count] = plan[own_of]
         plan[first_of + count] = slots
+        plan[fresh_of + count] = 0
         plan[second_of + count] = slots
 
 
@@ -210,7 +213,7 @@
 def pair_kernel(stage, feeds, plan, own, *refs):
     final = stage == len(stages) - 1
     slots, base = len(stages[stage]), at_stage[stage]
-    counts, groups, own_of, first_of, second_of = places(stages[stage], base)
+    counts, groups, own_of, first_of, second_of, fresh_of = places(stages[stage], base)
     units, held, cols, sem_u, sem_g = refs[-5:]
     outs, arrays, past = refs[-8 if final else -7 : -5], refs, ()
     if final:
@@ -245,13 +248,15 @@
     lane = lax.broadcasted_iota(jnp.int32, (2 * quarter, rows), 1)
     for copy in gets:
         copy.wait()
-    for o in range(2 * blocks):
-
-        @pl.when(plan[base + o] > 0)
-        def _():
-            loads[o].wait()
 
     def visit(turn, carry):
+        for group in (2 * turn, 2 * turn + 1):
+
+            @pl.when(plan[fresh_of + group] == 1)
+            def _():
+                o = plan[own_of + group]
+                pltpu.make_async_copy(own.at[o], units.at[o], sem_u.at[o]).wait()
+
         for group in (2 * turn, 2 * turn + 1):
             o = plan[own_of + group]
             pair = [plan[first_of + group], plan[second_of + group]]
@@ -289,7 +294,11 @@
     return jnp.where(mine, jnp.maximum(running, wide), running)
 
 
-def merge_kernel(plan, local, row_best, sib_rows, back, out, best):
+def blend_kernel(local, row_best, sib_rows, out):
+    out[...] = jnp.maximum(jnp.maximum(local[...], row_best[0:blocks]), sib_rows[...])
+
+
+def merge_kernel(plan, blended, back, out, best):
     rep = lax.axis_index("rep")
     best[...] = jnp.full((blocks, quarter), absent, jnp.float32)
     for number in range(len(every)):
@@ -297,20 +306,23 @@
         best[pl.ds(block, 1), :] = jnp.maximum(
             best[pl.ds(block, 1), :], back[pl.ds(plan[at_back_row + number], 1), :]
         )
-    merged = jnp.maximum(jnp.maximum(local[...], row_best[0:blocks]), sib_rows[...])
-    merged = spread_in(merged, best[...], rep)
+    merged = spread_in(blended[...], best[...], rep)
     lane = lax.broadcasted_iota(jnp.int32, (1, rows), 1)
     for b in range(blocks):
         out[b : b + 1, :] = jnp.where(lane < plan[at_own + b], merged[b : b + 1], -1.0)
 
 
-def finish_kernel(one, two, three, four, out):
-    best = jnp.maximum(jnp.maximum(one[...], two[...]), jnp.maximum(three[...], four[...]))
+def finish_kernel(one, two, out):
+    best = jnp.maximum(one[...], two[...])
     for b in range(blocks):
         for q in range(n_rep):
             out[n_rep * b + q : n_rep * b + q + 1, :] = best[
                 b : b + 1, q * quarter : (q + 1) * quarter
             ]
+
+
+def higher_kernel(one, two, out):
+    out[...] = jnp.maximum(one[...], two[...])
 
 
 def move(value, dx, dz):
@@ -469,29 +481,45 @@
     )
     sib_rows = lax.ppermute(sib_best, "core", swap)
     back = lax.all_to_all(col_best, ("x", "z"), split_axis=0, concat_axis=0, tiled=True)
+    blended = pl.pallas_call(
+        blend_kernel,
+        out_shape=jax.ShapeDtypeStruct((blocks, rows), f32),
+        in_specs=[vmem, vmem, vmem],
+        out_specs=vmem,
+        compiler_params=small,
+        cost_estimate=cost,
+        name="blend",
+    )(local_best, row_best, sib_rows)
     combined = pl.pallas_call(
         merge_kernel,
         out_shape=jax.ShapeDtypeStruct((blocks, rows), f32),
-        in_specs=[smem, vmem, vmem, vmem, vmem],
+        in_specs=[smem, vmem, vmem],
         out_specs=vmem,
         scratch_shapes=[pltpu.VMEM((blocks, quarter), f32)],
         compiler_params=small,
         cost_estimate=cost,
         name="merge",
-    )(plan, local_best, row_best, sib_rows, back)
-    others = [
-        lax.ppermute(combined, "rep", [(y, (y + d) % n_rep) for y in range(n_rep)])
-        for d in range(1, n_rep)
-    ]
+    )(plan, blended, back)
+    other = lax.ppermute(combined, "rep", [(y, y ^ 1) for y in range(n_rep)])
+    combined = pl.pallas_call(
+        higher_kernel,
+        out_shape=jax.ShapeDtypeStruct((blocks, rows), f32),
+        in_specs=[vmem, vmem],
+        out_specs=vmem,
+        compiler_params=small,
+        cost_estimate=cost,
+        name="higher",
+    )(combined, other)
+    other = lax.ppermute(combined, "rep", [(y, y ^ 2) for y in range(n_rep)])
     result = pl.pallas_call(
         finish_kernel,
         out_shape=jax.ShapeDtypeStruct((blocks * n_rep, quarter), f32),
-        in_specs=[vmem, vmem, vmem, vmem],
+        in_specs=[vmem, vmem],
         out_specs=vmem,
         compiler_params=small,
         cost_estimate=cost,
         name="finish",
-    )(combined, *others)
+    )(combined, other)
     return result.reshape(-1)
 
 

time: 171 us -> 171 us (level)
  Pallas kernels: 60.7 us -> 56.3 us
  waiting for transfers between devices: 52.9 us -> 55.4 us
    pallas_call x3, Pallas kernels: 22.9 us -> 18.1 us  [compare(): pl.pallas_call(functools.partial(pair_kernel, stage, feeds), out_shape=[j...]
    all_to_all x1, starting transfers between devices: 8.16 us -> 10.9 us  [on_device(): lax.all_to_all(col_best, ('x', 'z'), split_axis=0, concat_axis=0, tiled=T...]
    ppermute x3 -> x2, waiting for transfers between devices: 4.95 us -> 7 us  [the longest x1 4.01 us: on_device(): other = lax.ppermute(combined, 'rep', [(y, y ^ 2) for y in range(n_rep)])]
  transfers between devices with their start and end apart: 21 -> 20, of which waited for: 12 -> 11; matrix products, arithmetic and copies ran while one was open for 0% -> 0% of each run, Pallas kernels for 27% -> 27%
where the time goes in v4:
time: 171 us; the launch traced here: 169 us
  Pallas kernels  56.3 us (33%)
  waiting for transfers between devices  55.4 us (32%)
  starting transfers between devices  53.4 us (31%)
  local copies, waits for them, and re-layouts  3.97 us (2%)
    ppermute x14, waiting for transfers between devices, move(): return lax.ppermute(value, ('x', 'z'), steps)  39.3 us
    ppermute x14, starting transfers between devices, move(): return lax.ppermute(value, ('x', 'z'), steps)  35.8 us
    pallas_call x1, Pallas kernels, on_device(): pl.pallas_call(local_kernel, grid=(2 * blocks,), out_shape=(jax.ShapeDtyp...  21.8 us
    pallas_call x3, Pallas kernels, compare(): pl.pallas_call(functools.partial(pair_kernel, stage, feeds), out_shape=[j...  18.1 us
    all_to_all x1, starting transfers between devices, on_device(): lax.all_to_all(col_best, ('x', 'z'), split_axis=0, concat_axis=0, tiled=T...  10.9 us
    pallas_call x2, Pallas kernels, pick(): pl.pallas_call(functools.partial(pick_kernel, wanted, spread), out_shape=...  7.83 us
    all_to_all x1, waiting for transfers between devices, on_device(): lax.all_to_all(col_best, ('x', 'z'), split_axis=0, concat_axis=0, tiled=T...  7.62 us
    all_to_all x1, starting transfers between devices, on_device(): lax.all_to_all(picked[-1], 'x', split_axis=0, concat_axis=0, tiled=True)  4.55 us
  transfers between devices with their start and end apart: 20, of which 11 were waited for; matrix products, arithmetic and copies ran while one was open for 0% of the time, Pallas kernels for 27%

profile of v4, /device:TPU:24, one launch (start us, length us, event | category | flops | bytes accessed | tf_op | source)
XLA Modules:
  0.0 169.4 jit_solution(18113502170161738660)
XLA Ops:
  0.0 0.0 collective-permute-start.5
  0.0 4.4 %prep.1 = (bf16[8,128,768]{2,1,0:T(8,128)(2,1)}, bf16[1,128,768]{2,1,0:T(8,128)(2,1)}, bf16[1,128,768]{2,1,0:T(8,128)(2,1)}, bf16[1,128,768]{2,1,0:T(8,128)(2,1)...) custom-call(s32[64,64]{1,0:T(8,128)} %table.3, bf16[8,512,768]{2,1,0:T(8,128)(2,1)} %bitcast.6), custom_call_target="tpu_custom_call" | custom-call | bytes 65536 | tf_op jit(solution)/shard_map/prep/pallas_call | solution.py:395
  4.4 2.0 %collective-permute-start = (bf16[8,128,768]{2,1,0:T(8,128)(2,1)}, bf16[8,128,768]{2,1,0:T(8,128)(2,1)S(1)}, u32[]{:S(2)}, u32[]{:S(2)}) collective-permute-start(bf16[8,128,768]{2,1,0:T(8,128)(2,1)} %get-tuple-element.38.cols.after.refs_0_), channel_id=1, source_target_pairs={{0,8},{8,16},{16,24},{24,32},{32,40},{40,48},{48,56},{56,0},{64,72... | collective-permute-start | bytes 4718600 | tf_op jit(solution)/shard_map/ppermute | solution.py:334
  6.4 5.4 %collective-permute-start.1 = (bf16[1,128,768]{2,1,0:T(8,128)(2,1)}, bf16[1,128,768]{2,1,0:T(8,128)(2,1)S(1)}, u32[]{:S(2)}, u32[]{:S(2)}) collective-permute-start(bf16[1,128,768]{2,1,0:T(8,128)(2,1)} %get-tuple-element.39), channel_id=1, source_target_pairs={{0,48},{8,56},{16,0},{24,8},{32,16},{40,24},{48,32},{56,40},{64,11... | collective-permute-start | bytes 589832 | tf_op jit(solution)/shard_map/ppermute | solution.py:334
  11.8 2.4 %collective-permute-start.2 = (bf16[1,128,768]{2,1,0:T(8,128)(2,1)}, bf16[1,128,768]{2,1,0:T(8,128)(2,1)S(1)}, u32[]{:S(2)}, u32[]{:S(2)}) collective-permute-start(bf16[1,128,768]{2,1,0:T(8,128)(2,1)} %get-tuple-element.40), channel_id=1, source_target_pairs={{0,112},{8,120},{16,64},{24,72},{32,80},{40,88},{48,96},{56,104},{... | collective-permute-start | bytes 589832 | tf_op jit(solution)/shard_map/ppermute | solution.py:334
  14.1 2.7 %collective-permute-start.3 = (bf16[1,128,768]{2,1,0:T(8,128)(2,1)}, bf16[1,128,768]{2,1,0:T(8,128)(2,1)S(1)}, u32[]{:S(2)}, u32[]{:S(2)}) collective-permute-start(bf16[1,128,768]{2,1,0:T(8,128)(2,1)} %get-tuple-element.41), channel_id=1, source_target_pairs={{0,176},{8,184},{16,128},{24,136},{32,144},{40,152},{48,160},{56,1... | collective-permute-start | bytes 589832 | tf_op jit(solution)/shard_map/ppermute | solution.py:334
  16.9 0.0 collective-permute-done.5.sib
  16.9 2.1 %collective-permute-start.4 = (bf16[1,128,768]{2,1,0:T(8,128)(2,1)}, bf16[1,128,768]{2,1,0:T(8,128)(2,1)S(1)}, u32[]{:S(2)}, u32[]{:S(2)}) collective-permute-start(bf16[1,128,768]{2,1,0:T(8,128)(2,1)} %get-tuple-element.42), channel_id=1, source_target_pairs={{0,240},{8,248},{16,192},{24,200},{32,208},{40,216},{48,224},{56,2... | collective-permute-start | bytes 589832 | tf_op jit(solution)/shard_map/ppermute | solution.py:334
  19.0 2.9 %plan.1 = s32[382]{0:T(512)} custom-call(s32[64,64]{1,0:T(8,128)} %table.3, s32[512]{0:T(512)} %valid.3, bf16[8,128,768]{2,1,0:T(8,128)(2,1)} %get-tuple-element.38.cols.after.refs_0_), custom_call_target="tpu_custom_call" | custom-call | bytes 65536 | tf_op jit(solution)/shard_map/plan/pallas_call | solution.py:416
  21.9 21.8 %local.1 = (bf16[16,512,768]{2,1,0:T(8,128)(2,1)}, f32[8,512]{1,0:T(8,128)}) custom-call(s32[512]{0:T(512)} %valid.3, bf16[8,512,768]{2,1,0:T(8,128)(2,1)} %bitcast.7, bf16[8,512,768]{2,1,0:T(8,128)(2,1)} %collective-permute-done.5.sib, bf16[8,128,768]{2,1,0:T(8,128)(2,1)} %get-tuple-element.38.cols.after.refs_0_), custom_call_target="tpu_custom_call" | custom-call | bytes 65536 | tf_op jit(solution)/shard_map/local/pallas_call | solution.py:426
  43.7 0.0 collective-permute-done.1
  43.7 0.0 collective-permute-done.2
  43.7 0.0 collective-permute-done.3
  43.7 2.4 %collective-permute-done.4 = bf16[1,128,768]{2,1,0:T(8,128)(2,1)S(1)} collective-permute-done((bf16[1,128,768]{2,1,0:T(8,128)(2,1)}, bf16[1,128,768]{2,1,0:T(8,128)(2,1)S(1)}, u32[]{:S(2)}, u32[]{:S(2)}) %collective-permute-start.4) | collective-permute-done | bytes 196640 | tf_op jit(solution)/shard_map/ppermute | solution.py:334
  46.1 0.0 collective-permute-done.refs_1_
  46.1 2.5 %collective-permute-start.9 = (bf16[8,128,768]{2,1,0:T(8,128)(2,1)S(1)}, bf16[8,128,768]{2,1,0:T(8,128)(2,1)S(1)}, u32[]{:S(2)}, u32[]{:S(2)}) collective-permute-start(bf16[8,128,768]{2,1,0:T(8,128)(2,1)S(1)} %collective-permute-done.refs_1_), channel_id=1, source_target_pairs={{0,8},{8,16},{16,24},{24,32},{32,40},{40,48},{48,56},{56,0},{64,72... | collective-permute-start | bytes 4718600 | tf_op jit(solution)/shard_map/ppermute | solution.py:334
  48.6 0.1 pad_maximum_fusion
  48.7 3.0 %collective-permute-start.10 = (bf16[4,128,768]{2,1,0:T(8,128)(2,1)S(1)}, bf16[4,128,768]{2,1,0:T(8,128)(2,1)S(1)}, u32[]{:S(2)}, u32[]{:S(2)}) collective-permute-start(bf16[4,128,768]{2,1,0:T(8,128)(2,1)S(1)} %pad_maximum_fusion), channel_id=1, source_target_pairs={{0,48},{8,56},{16,0},{24,8},{32,16},{40,24},{48,32},{56,40},{64,11... | collective-permute-start | bytes 2359304 | tf_op jit(solution)/shard_map/ppermute | solution.py:334
  51.7 0.0 copy-done.7
  51.7 3.7 %pick_a.1 = (bf16[3,128,768]{2,1,0:T(8,128)(2,1)}, bf16[3,128,768]{2,1,0:T(8,128)(2,1)}, bf16[3,128,768]{2,1,0:T(8,128)(2,1)}, bf16[3,128,768]{2,1,0:T(8,128)(2,1)}) custom-call(s32[382]{0:T(512)} %plan.1, bf16[8,128,768]{2,1,0:T(8,128)(2,1)} %get-tuple-element.38.cols.after.refs_0_, bf16[8,128,768]{2,1,0:T(8,128)(2,1)} %copy-done.7), custom_call_target="tpu_custom_call" | custom-call | bytes 65536 | tf_op jit(solution)/shard_map/pick_a/pallas_call | solution.py:355
  55.5 1.5 collective-permute-start.6
  57.0 1.7 %collective-permute-start.7 = (bf16[3,128,768]{2,1,0:T(8,128)(2,1)}, bf16[3,128,768]{2,1,0:T(8,128)(2,1)S(1)}, u32[]{:S(2)}, u32[]{:S(2)}) collective-permute-start(bf16[3,128,768]{2,1,0:T(8,128)(2,1)} %get-tuple-element.50), channel_id=1, source_target_pairs={{0,128},{8,136},{16,144},{24,152},{32,160},{40,168},{48,176},{56,1... | collective-permute-start | bytes 1769480 | tf_op jit(solution)/shard_map/ppermute | solution.py:334
  58.7 2.3 %collective-permute-start.8 = (bf16[3,128,768]{2,1,0:T(8,128)(2,1)}, bf16[3,128,768]{2,1,0:T(8,128)(2,1)S(1)}, u32[]{:S(2)}, u32[]{:S(2)}) collective-permute-start(bf16[3,128,768]{2,1,0:T(8,128)(2,1)} %get-tuple-element.51), channel_id=1, source_target_pairs={{0,192},{8,200},{16,208},{24,216},{32,224},{40,232},{48,240},{56,2... | collective-permute-start | bytes 1769480 | tf_op jit(solution)/shard_map/ppermute | solution.py:334
  61.0 23.4 %collective-permute-done.10.refs_4_ = bf16[4,128,768]{2,1,0:T(8,128)(2,1)S(1)} collective-permute-done((bf16[4,128,768]{2,1,0:T(8,128)(2,1)S(1)}, bf16[4,128,768]{2,1,0:T(8,128)(2,1)S(1)}, u32[]{:S(2)}, u32[]{:S(2)}) %collective-permute-start.10) | collective-permute-done | bytes 786464 | tf_op jit(solution)/shard_map/ppermute | solution.py:334
  84.4 0.0 collective-permute-done.9.refs_1_
  84.4 0.0 collective-permute-done.6.refs_3_.refs_1_
  84.4 0.0 copy-start.4
  84.4 0.0 collective-permute-done.7.refs_4_.refs_2_
  84.4 0.0 copy-start.5
  84.4 0.5 collective-permute-done.8.refs_5_.refs_3_
  84.9 0.7 copy-done.8
  85.6 0.2 copy-done.4
  85.8 0.2 copy-done.5
  86.0 0.2 copy-done.6
  86.1 4.1 %pick_b.1 = (bf16[2,128,768]{2,1,0:T(8,128)(2,1)}, bf16[2,128,768]{2,1,0:T(8,128)(2,1)}, bf16[2,128,768]{2,1,0:T(8,128)(2,1)}, bf16[4,2,128,768]{3,2,1,0:T(8,128)(2,1)}) custom-call(s32[382]{0:T(512)} %plan.1, bf16[8,128,768]{2,1,0:T(8,128)(2,1)} %get-tuple-element.38.cols.after.refs_0_, bf16[8,128,768]{2,1,0:T(8,128)(2,1)} %copy-done.8, ...), custom_call_target="tpu_custom_call" | custom-call | bytes 65536 | tf_op jit(solution)/shard_map/pick_b/pallas_call | solution.py:355
  90.2 0.0 copy-start.14
  90.2 4.5 %all-to-all-start = ((bf16[4,2,128,768]{3,2,1,0:T(8,128)(2,1)}), bf16[4,2,128,768]{3,2,1,0:T(8,128)(2,1)S(1)}, u32[]{:S(2)}, u32[]{:S(2)}) async-start(bf16[4,2,128,768]{3,2,1,0:T(8,128)(2,1)} %get-tuple-element.67), calls=%async_computation | async-start | bytes 3145728 | tf_op jit(solution)/shard_map/all_to_all | solution.py:455
  94.8 0.0 copy-done.14
  94.8 1.9 %collective-permute-start.11 = (bf16[2,128,768]{2,1,0:T(8,128)(2,1)S(1)}, bf16[2,128,768]{2,1,0:T(8,128)(2,1)S(1)}, u32[]{:S(2)}, u32[]{:S(2)}) collective-permute-start(bf16[2,128,768]{2,1,0:T(8,128)(2,1)S(1)} %copy-done.14), channel_id=1, source_target_pairs={{0,8},{8,16},{16,24},{24,32},{32,40},{40,48},{48,56},{56,0},{64,72... | collective-permute-start | bytes 1179656 | tf_op jit(solution)/shard_map/ppermute | solution.py:334
  96.7 1.5 collective-permute-start.12
  98.2 3.9 %collective-permute-start.13 = (bf16[2,128,768]{2,1,0:T(8,128)(2,1)}, bf16[2,128,768]{2,1,0:T(8,128)(2,1)S(1)}, u32[]{:S(2)}, u32[]{:S(2)}) collective-permute-start(bf16[2,128,768]{2,1,0:T(8,128)(2,1)} %get-tuple-element.65), channel_id=1, source_target_pairs={{0,200},{8,208},{16,216},{24,224},{32,232},{40,240},{48,248},{56,1... | collective-permute-start | bytes 1179656 | tf_op jit(solution)/shard_map/ppermute | solution.py:334
  102.1 2.8 %collective-permute-start.14 = (bf16[2,128,768]{2,1,0:T(8,128)(2,1)}, bf16[2,128,768]{2,1,0:T(8,128)(2,1)S(1)}, u32[]{:S(2)}, u32[]{:S(2)}) collective-permute-start(bf16[2,128,768]{2,1,0:T(8,128)(2,1)} %get-tuple-element.66), channel_id=1, source_target_pairs={{0,168},{8,176},{16,184},{24,128},{32,136},{40,144},{48,152},{56,1... | collective-permute-start | bytes 1179656 | tf_op jit(solution)/shard_map/ppermute | solution.py:334
  104.9 8.9 %pairs_a.1 = (f32[16,512]{1,0:T(8,128)}, f32[16,128]{1,0:T(8,128)}) custom-call(s32[382]{0:T(512)} %plan.1, bf16[16,512,768]{2,1,0:T(8,128)(2,1)} %get-tuple-element.46.own, bf16[3,128,768]{2,1,0:T(8,128)(2,1)} %get-tuple-element.48.refs_2_.refs_0_, bf16[3,128,768]{2,1,0:T(8,128)(2,1)} %copy-done.4, bf16[3,128,768]{2,1,0:T(8,128)(2,1)} %copy-done.5, ...), custom_call_target="tpu_custom_call" | custom-call | bytes 65536 | tf_op jit(solution)/shard_map/pairs_a/pallas_call | solution.py:375
  113.8 0.0 collective-permute-done.11.refs_0_
  113.9 6.1 %collective-permute-done.12.refs_1_ = bf16[2,128,768]{2,1,0:T(8,128)(2,1)S(1)} collective-permute-done((bf16[2,128,768]{2,1,0:T(8,128)(2,1)}, bf16[2,128,768]{2,1,0:T(8,128)(2,1)S(1)}, u32[]{:S(2)}, u32[]{:S(2)}) %collective-permute-start.12) | collective-permute-done | bytes 393248 | tf_op jit(solution)/shard_map/ppermute | solution.py:334
  119.9 0.8 copy-done.11
  120.7 3.8 %pairs_b.1 = (f32[16,512]{1,0:T(8,128)}, f32[4,128]{1,0:T(4,128)}) custom-call(s32[382]{0:T(512)} %plan.1, bf16[16,512,768]{2,1,0:T(8,128)(2,1)} %get-tuple-element.46.own, bf16[2,128,768]{2,1,0:T(8,128)(2,1)} %copy-done.10, bf16[2,128,768]{2,1,0:T(8,128)(2,1)} %copy-done.11, f32[16,512]{1,0:T(8,128)} %get-tuple-element.60.refs_2_.refs_0_), custom_call_target="tpu_custom_call" | custom-call | bytes 65536 | tf_op jit(solution)/shard_map/pairs_b/pallas_call | solution.py:375
  124.4 2.3 %collective-permute-done.13.refs_4_ = bf16[2,128,768]{2,1,0:T(8,128)(2,1)S(1)} collective-permute-done((bf16[2,128,768]{2,1,0:T(8,128)(2,1)}, bf16[2,128,768]{2,1,0:T(8,128)(2,1)S(1)}, u32[]{:S(2)}, u32[]{:S(2)}) %collective-permute-start.13) | collective-permute-done | bytes 393248 | tf_op jit(solution)/shard_map/ppermute | solution.py:334
  126.8 4.7 %collective-permute-done.14.refs_5_ = bf16[2,128,768]{2,1,0:T(8,128)(2,1)S(1)} collective-permute-done((bf16[2,128,768]{2,1,0:T(8,128)(2,1)}, bf16[2,128,768]{2,1,0:T(8,128)(2,1)S(1)}, u32[]{:S(2)}, u32[]{:S(2)}) %collective-permute-start.14) | collective-permute-done | bytes 393248 | tf_op jit(solution)/shard_map/ppermute | solution.py:334
  131.5 0.1 all-to-all-done.refs_6_
  131.6 0.6 copy-done.13
  132.2 0.5 copy-done.3
  132.8 5.4 %pairs_c.1 = (f32[16,512]{1,0:T(8,128)}, f32[64,128]{1,0:T(8,128)}, f32[8,512]{1,0:T(8,128)}) custom-call(s32[382]{0:T(512)} %plan.1, bf16[16,512,768]{2,1,0:T(8,128)(2,1)} %get-tuple-element.46.own, f32[16,512]{1,0:T(8,128)} %get-tuple-element.60.refs_2_.refs_0_, f32[16,128]{1,0:T(8,128)} %get-tuple-element.61.refs_1_, ...), custom_call_target="tpu_custom_call" | custom-call | bytes 65536 | tf_op jit(solution)/shard_map/pairs_c/pallas_call | solution.py:375
  138.1 10.9 %all-to-all-start.1 = ((f32[32,2,128]{2,1,0:T(2,128)}), f32[32,2,128]{2,1,0:T(2,128)S(1)}, u32[]{:S(2)}, u32[]{:S(2)}) async-start(f32[32,2,128]{2,1,0:T(2,128)} %bitcast.8), calls=%async_computation.1 | async-start | bytes 65536 | tf_op jit(solution)/shard_map/all_to_all | solution.py:483
  149.1 0.1 collective-permute-start.15
  149.2 1.4 collective-permute-done.15.sib_rows
  150.6 0.8 copy-done.1
  151.3 7.6 %all-to-all-done.1 = f32[32,2,128]{2,1,0:T(2,128)S(1)} async-done(((f32[32,2,128]{2,1,0:T(2,128)}), f32[32,2,128]{2,1,0:T(2,128)S(1)}, u32[]{:S(2)}, u32[]{:S(2)}) %all-to-all-start.1) | async-done | bytes 32800 | tf_op jit(solution)/shard_map/all_to_all | solution.py:483
  159.0 0.7 merge.1.one
  159.7 0.8 collective-permute-start.16
  160.5 3.0 %collective-permute-done.16.two = f32[8,512]{1,0:T(8,128)S(1)} collective-permute-done((f32[8,512]{1,0:T(8,128)S(1)}, f32[8,512]{1,0:T(8,128)S(1)}, u32[]{:S(2)}, u32[]{:S(2)}) %collective-permute-start.16) | collective-permute-done | bytes 16416 | tf_op jit(solution)/shard_map/ppermute | solution.py:503
  163.5 1.2 collective-permute-start.17
  164.7 4.0 %collective-permute-done.17.two = f32[8,512]{1,0:T(8,128)S(1)} collective-permute-done((f32[8,512]{1,0:T(8,128)S(1)}, f32[8,512]{1,0:T(8,128)S(1)}, u32[]{:S(2)}, u32[]{:S(2)}) %collective-permute-start.17) | collective-permute-done | bytes 16416 | tf_op jit(solution)/shard_map/ppermute | solution.py:513
  168.8 0.6 finish.1
  (19 shorter events, 0.0 us)
Async XLA Ops:
  0.0 16.9 %collective-permute-start.5 = (bf16[8,512,768]{2,1,0:T(8,128)(2,1)}, bf16[8,512,768]{2,1,0:T(8,128)(2,1)}, u32[]{:S(2)}, u32[]{:S(2)}) collective-permute-start(bf16[8,512,768]{2,1,0:T(8,128)(2,1)} %bitcast.5), channel_id=1, source_target_pairs={{0,4},{4,0},{1,5},{5,1},{2,6},{6,2},{3,7},{7,3},{8,12},{12,8},{9,1... | collective-permute-start | bytes 18874376 | tf_op jit(solution)/shard_map/ppermute | solution.py:413
  4.4 41.7 %collective-permute-start = (bf16[8,128,768]{2,1,0:T(8,128)(2,1)}, bf16[8,128,768]{2,1,0:T(8,128)(2,1)S(1)}, u32[]{:S(2)}, u32[]{:S(2)}) collective-permute-start(bf16[8,128,768]{2,1,0:T(8,128)(2,1)} %get-tuple-element.38.cols.after.refs_0_), channel_id=1, source_target_pairs={{0,8},{8,16},{16,24},{24,32},{32,40},{40,48},{48,56},{56,0},{64,72... | collective-permute-start | bytes 4718600 | tf_op jit(solution)/shard_map/ppermute | solution.py:334
  6.4 37.4 %collective-permute-start.1 = (bf16[1,128,768]{2,1,0:T(8,128)(2,1)}, bf16[1,128,768]{2,1,0:T(8,128)(2,1)S(1)}, u32[]{:S(2)}, u32[]{:S(2)}) collective-permute-start(bf16[1,128,768]{2,1,0:T(8,128)(2,1)} %get-tuple-element.39), channel_id=1, source_target_pairs={{0,48},{8,56},{16,0},{24,8},{32,16},{40,24},{48,32},{56,40},{64,11... | collective-permute-start | bytes 589832 | tf_op jit(solution)/shard_map/ppermute | solution.py:334
  11.8 32.0 %collective-permute-start.2 = (bf16[1,128,768]{2,1,0:T(8,128)(2,1)}, bf16[1,128,768]{2,1,0:T(8,128)(2,1)S(1)}, u32[]{:S(2)}, u32[]{:S(2)}) collective-permute-start(bf16[1,128,768]{2,1,0:T(8,128)(2,1)} %get-tuple-element.40), channel_id=1, source_target_pairs={{0,112},{8,120},{16,64},{24,72},{32,80},{40,88},{48,96},{56,104},{... | collective-permute-start | bytes 589832 | tf_op jit(solution)/shard_map/ppermute | solution.py:334
  14.1 29.6 %collective-permute-start.3 = (bf16[1,128,768]{2,1,0:T(8,128)(2,1)}, bf16[1,128,768]{2,1,0:T(8,128)(2,1)S(1)}, u32[]{:S(2)}, u32[]{:S(2)}) collective-permute-start(bf16[1,128,768]{2,1,0:T(8,128)(2,1)} %get-tuple-element.41), channel_id=1, source_target_pairs={{0,176},{8,184},{16,128},{24,136},{32,144},{40,152},{48,160},{56,1... | collective-permute-start | bytes 589832 | tf_op jit(solution)/shard_map/ppermute | solution.py:334
  16.9 29.2 %collective-permute-start.4 = (bf16[1,128,768]{2,1,0:T(8,128)(2,1)}, bf16[1,128,768]{2,1,0:T(8,128)(2,1)S(1)}, u32[]{:S(2)}, u32[]{:S(2)}) collective-permute-start(bf16[1,128,768]{2,1,0:T(8,128)(2,1)} %get-tuple-element.42), channel_id=1, source_target_pairs={{0,240},{8,248},{16,192},{24,200},{32,208},{40,216},{48,224},{56,2... | collective-permute-start | bytes 589832 | tf_op jit(solution)/shard_map/ppermute | solution.py:334
  46.1 5.6 %copy-start.7 = (bf16[8,128,768]{2,1,0:T(8,128)(2,1)}, bf16[8,128,768]{2,1,0:T(8,128)(2,1)S(1)}, u32[]{:S(2)}) copy-start(bf16[8,128,768]{2,1,0:T(8,128)(2,1)S(1)} %collective-permute-done.refs_1_) | copy-start | bytes 4718596
  46.1 38.3 %collective-permute-start.9 = (bf16[8,128,768]{2,1,0:T(8,128)(2,1)S(1)}, bf16[8,128,768]{2,1,0:T(8,128)(2,1)S(1)}, u32[]{:S(2)}, u32[]{:S(2)}) collective-permute-start(bf16[8,128,768]{2,1,0:T(8,128)(2,1)S(1)} %collective-permute-done.refs_1_), channel_id=1, source_target_pairs={{0,8},{8,16},{16,24},{24,32},{32,40},{40,48},{48,56},{56,0},{64,72... | collective-permute-start | bytes 4718600 | tf_op jit(solution)/shard_map/ppermute | solution.py:334
  48.7 35.6 %collective-permute-start.10 = (bf16[4,128,768]{2,1,0:T(8,128)(2,1)S(1)}, bf16[4,128,768]{2,1,0:T(8,128)(2,1)S(1)}, u32[]{:S(2)}, u32[]{:S(2)}) collective-permute-start(bf16[4,128,768]{2,1,0:T(8,128)(2,1)S(1)} %pad_maximum_fusion), channel_id=1, source_target_pairs={{0,48},{8,56},{16,0},{24,8},{32,16},{40,24},{48,32},{56,40},{64,11... | collective-permute-start | bytes 2359304 | tf_op jit(solution)/shard_map/ppermute | solution.py:334
  55.5 28.9 %collective-permute-start.6 = (bf16[3,128,768]{2,1,0:T(8,128)(2,1)}, bf16[3,128,768]{2,1,0:T(8,128)(2,1)S(1)}, u32[]{:S(2)}, u32[]{:S(2)}) collective-permute-start(bf16[3,128,768]{2,1,0:T(8,128)(2,1)} %get-tuple-element.49), channel_id=1, source_target_pairs={{0,64},{8,72},{16,80},{24,88},{32,96},{40,104},{48,112},{56,120},{... | collective-permute-start | bytes 1769480 | tf_op jit(solution)/shard_map/ppermute | solution.py:334
  57.0 27.4 %collective-permute-start.7 = (bf16[3,128,768]{2,1,0:T(8,128)(2,1)}, bf16[3,128,768]{2,1,0:T(8,128)(2,1)S(1)}, u32[]{:S(2)}, u32[]{:S(2)}) collective-permute-start(bf16[3,128,768]{2,1,0:T(8,128)(2,1)} %get-tuple-element.50), channel_id=1, source_target_pairs={{0,128},{8,136},{16,144},{24,152},{32,160},{40,168},{48,176},{56,1... | collective-permute-start | bytes 1769480 | tf_op jit(solution)/shard_map/ppermute | solution.py:334
  58.7 26.2 %collective-permute-start.8 = (bf16[3,128,768]{2,1,0:T(8,128)(2,1)}, bf16[3,128,768]{2,1,0:T(8,128)(2,1)S(1)}, u32[]{:S(2)}, u32[]{:S(2)}) collective-permute-start(bf16[3,128,768]{2,1,0:T(8,128)(2,1)} %get-tuple-element.51), channel_id=1, source_target_pairs={{0,192},{8,200},{16,208},{24,216},{32,224},{40,232},{48,240},{56,2... | collective-permute-start | bytes 1769480 | tf_op jit(solution)/shard_map/ppermute | solution.py:334
  84.4 20.5 %copy-start.9 = (bf16[4,128,768]{2,1,0:T(8,128)(2,1)}, bf16[4,128,768]{2,1,0:T(8,128)(2,1)S(1)}, u32[]{:S(2)}) copy-start(bf16[4,128,768]{2,1,0:T(8,128)(2,1)S(1)} %collective-permute-done.10.refs_4_) | copy-start | bytes 2359300
  84.4 1.2 copy-start.8
  84.4 1.4 copy-start.4
  84.4 1.5 copy-start.5
  84.9 1.2 copy-start.6
  90.2 4.6 %copy-start.14 = (bf16[2,128,768]{2,1,0:T(8,128)(2,1)S(1)}, bf16[2,128,768]{2,1,0:T(8,128)(2,1)}, u32[]{:S(2)}) copy-start(bf16[2,128,768]{2,1,0:T(8,128)(2,1)} %get-tuple-element.59.refs_5_) | copy-start | bytes 1179652
  90.2 41.3 %all-to-all-start = ((bf16[4,2,128,768]{3,2,1,0:T(8,128)(2,1)}), bf16[4,2,128,768]{3,2,1,0:T(8,128)(2,1)S(1)}, u32[]{:S(2)}, u32[]{:S(2)}) async-start(bf16[4,2,128,768]{3,2,1,0:T(8,128)(2,1)} %get-tuple-element.67), calls=%async_computation | async-start | bytes 3145728 | tf_op jit(solution)/shard_map/all_to_all | solution.py:455
  94.8 19.0 %collective-permute-start.11 = (bf16[2,128,768]{2,1,0:T(8,128)(2,1)S(1)}, bf16[2,128,768]{2,1,0:T(8,128)(2,1)S(1)}, u32[]{:S(2)}, u32[]{:S(2)}) collective-permute-start(bf16[2,128,768]{2,1,0:T(8,128)(2,1)S(1)} %copy-done.14), channel_id=1, source_target_pairs={{0,8},{8,16},{16,24},{24,32},{32,40},{40,48},{48,56},{56,0},{64,72... | collective-permute-start | bytes 1179656 | tf_op jit(solution)/shard_map/ppermute | solution.py:334
  96.7 23.2 %collective-permute-start.12 = (bf16[2,128,768]{2,1,0:T(8,128)(2,1)}, bf16[2,128,768]{2,1,0:T(8,128)(2,1)S(1)}, u32[]{:S(2)}, u32[]{:S(2)}) collective-permute-start(bf16[2,128,768]{2,1,0:T(8,128)(2,1)} %get-tuple-element.62), channel_id=1, source_target_pairs={{0,72},{8,80},{16,88},{24,96},{32,104},{40,112},{48,120},{56,64},{... | collective-permute-start | bytes 1179656 | tf_op jit(solution)/shard_map/ppermute | solution.py:334
  98.2 28.6 %collective-permute-start.13 = (bf16[2,128,768]{2,1,0:T(8,128)(2,1)}, bf16[2,128,768]{2,1,0:T(8,128)(2,1)S(1)}, u32[]{:S(2)}, u32[]{:S(2)}) collective-permute-start(bf16[2,128,768]{2,1,0:T(8,128)(2,1)} %get-tuple-element.65), channel_id=1, source_target_pairs={{0,200},{8,208},{16,216},{24,224},{32,232},{40,240},{48,248},{56,1... | collective-permute-start | bytes 1179656 | tf_op jit(solution)/shard_map/ppermute | solution.py:334
  102.1 29.3 %collective-permute-start.14 = (bf16[2,128,768]{2,1,0:T(8,128)(2,1)}, bf16[2,128,768]{2,1,0:T(8,128)(2,1)S(1)}, u32[]{:S(2)}, u32[]{:S(2)}) collective-permute-start(bf16[2,128,768]{2,1,0:T(8,128)(2,1)} %get-tuple-element.66), channel_id=1, source_target_pairs={{0,168},{8,176},{16,184},{24,128},{32,136},{40,144},{48,152},{56,1... | collective-permute-start | bytes 1179656 | tf_op jit(solution)/shard_map/ppermute | solution.py:334
  113.8 6.1 %copy-start.10 = (bf16[2,128,768]{2,1,0:T(8,128)(2,1)}, bf16[2,128,768]{2,1,0:T(8,128)(2,1)S(1)}, u32[]{:S(2)}) copy-start(bf16[2,128,768]{2,1,0:T(8,128)(2,1)S(1)} %collective-permute-done.11.refs_0_) | copy-start | bytes 1179652
  119.9 0.8 copy-start.11
  126.8 4.8 %copy-start.12 = (bf16[2,128,768]{2,1,0:T(8,128)(2,1)}, bf16[2,128,768]{2,1,0:T(8,128)(2,1)S(1)}, u32[]{:S(2)}) copy-start(bf16[2,128,768]{2,1,0:T(8,128)(2,1)S(1)} %collective-permute-done.13.refs_4_) | copy-start | bytes 1179652
  131.5 0.8 copy-start.13
  131.6 1.2 copy-start.3
  132.7 17.8 %copy-start.2 = (f32[8,512]{1,0:T(8,128)S(1)}, f32[8,512]{1,0:T(8,128)}, u32[]{:S(2)}) copy-start(f32[8,512]{1,0:T(8,128)} %get-tuple-element.45.local) | copy-start | bytes 49156
  132.8 26.2 %copy-start = (s32[382]{0:T(512)S(1)}, s32[382]{0:T(512)}, u32[]{:S(2)}) copy-start(s32[382]{0:T(512)} %plan.1) | copy-start | bytes 4588
  138.1 20.8 %all-to-all-start.1 = ((f32[32,2,128]{2,1,0:T(2,128)}), f32[32,2,128]{2,1,0:T(2,128)S(1)}, u32[]{:S(2)}, u32[]{:S(2)}) async-start(f32[32,2,128]{2,1,0:T(2,128)} %bitcast.8), calls=%async_computation.1 | async-start | bytes 65536 | tf_op jit(solution)/shard_map/all_to_all | solution.py:483
  149.1 1.5 collective-permute-start.15
  150.6 0.8 copy-start.1
  159.7 3.8 %collective-permute-start.16 = (f32[8,512]{1,0:T(8,128)S(1)}, f32[8,512]{1,0:T(8,128)S(1)}, u32[]{:S(2)}, u32[]{:S(2)}) collective-permute-start(f32[8,512]{1,0:T(8,128)S(1)} %merge.1.one), channel_id=1, source_target_pairs={{0,1},{1,0},{2,3},{3,2},{4,5},{5,4},{6,7},{7,6},{8,9},{9,8},{10,11... | collective-permute-start | bytes 49160 | tf_op jit(solution)/shard_map/ppermute | solution.py:503
  163.5 5.2 %collective-permute-start.17 = (f32[8,512]{1,0:T(8,128)S(1)}, f32[8,512]{1,0:T(8,128)S(1)}, u32[]{:S(2)}, u32[]{:S(2)}) collective-permute-start(f32[8,512]{1,0:T(8,128)S(1)} %higher.1.one), channel_id=1, source_target_pairs={{0,2},{1,3},{2,0},{3,1},{4,6},{5,7},{6,4},{7,5},{8,10},{9,11},{10,... | collective-permute-start | bytes 49160 | tf_op jit(solution)/shard_map/ppermute | solution.py:513

commit v5 on v3

--- a/solution.py
+++ b/solution.py
@@ -289,7 +289,11 @@
     return jnp.where(mine, jnp.maximum(running, wide), running)
 
 
-def merge_kernel(plan, local, row_best, sib_rows, back, out, best):
+def blend_kernel(local, row_best, sib_rows, out):
+    out[...] = jnp.maximum(jnp.maximum(local[...], row_best[0:blocks]), sib_rows[...])
+
+
+def merge_kernel(plan, blended, back, out, best):
     rep = lax.axis_index("rep")
     best[...] = jnp.full((blocks, quarter), absent, jnp.float32)
     for number in range(len(every)):
@@ -297,8 +301,7 @@
         best[pl.ds(block, 1), :] = jnp.maximum(
             best[pl.ds(block, 1), :], back[pl.ds(plan[at_back_row + number], 1), :]
         )
-    merged = jnp.maximum(jnp.maximum(local[...], row_best[0:blocks]), sib_rows[...])
-    merged = spread_in(merged, best[...], rep)
+    merged = spread_in(blended[...], best[...], rep)
     lane = lax.broadcasted_iota(jnp.int32, (1, rows), 1)
     for b in range(blocks):
         out[b : b + 1, :] = jnp.where(lane < plan[at_own + b], merged[b : b + 1], -1.0)
@@ -437,8 +440,8 @@
     away = move(jnp.concatenate(away, axis=0), 0, -2)
     picked = pick(numbers(first), False, [cols, hop1], [], "pick_a")
     first_in = [move(a, dx, 0) for dx, a in enumerate(picked)]
-    hop2, away, around = lax.optimization_barrier((hop2, away, around))
-    picked = pick(numbers(third + second), True, [cols, hop2], first_in, "pick_b")
+    hop2, away, around, *first_in = lax.optimization_barrier((hop2, away, around, *first_in))
+    picked = pick(numbers(third + second), True, [cols, hop2], [], "pick_b")
     third_in = [move(a, slots[0][0], 1) for slots, a in zip(third, picked)]
     second_in = lax.all_to_all(picked[-1], "x", split_axis=0, concat_axis=0, tiled=True)
     down_in = move(around, 2, -3)
@@ -469,16 +472,25 @@
     )
     sib_rows = lax.ppermute(sib_best, "core", swap)
     back = lax.all_to_all(col_best, ("x", "z"), split_axis=0, concat_axis=0, tiled=True)
+    blended = pl.pallas_call(
+        blend_kernel,
+        out_shape=jax.ShapeDtypeStruct((blocks, rows), f32),
+        in_specs=[vmem, vmem, vmem],
+        out_specs=vmem,
+        compiler_params=small,
+        cost_estimate=cost,
+        name="blend",
+    )(local_best, row_best, sib_rows)
     combined = pl.pallas_call(
         merge_kernel,
         out_shape=jax.ShapeDtypeStruct((blocks, rows), f32),
-        in_specs=[smem, vmem, vmem, vmem, vmem],
+        in_specs=[smem, vmem, vmem],
         out_specs=vmem,
         scratch_shapes=[pltpu.VMEM((blocks, quarter), f32)],
         compiler_params=small,
         cost_estimate=cost,
         name="merge",
-    )(plan, local_best, row_best, sib_rows, back)
+    )(plan, blended, back)
     others = [
         lax.ppermute(combined, "rep", [(y, (y + d) % n_rep) for y in range(n_rep)])
         for d in range(1, n_rep)

time: 171 us -> 170 us (level)
    unnamed x30 -> x26, local copies, waits for them, and re-layouts: 3.96 us -> 4.68 us
where the time goes in v5:
time: 170 us; the launch traced here: 168 us
  Pallas kernels  60.4 us (36%)
  waiting for transfers between devices  52.7 us (31%)
  starting transfers between devices  50.1 us (29%)
  local copies, waits for them, and re-layouts  4.68 us (3%)
    ppermute x14, waiting for transfers between devices, move(): return lax.ppermute(value, ('x', 'z'), steps)  38.7 us
    ppermute x14, starting transfers between devices, move(): return lax.ppermute(value, ('x', 'z'), steps)  34.9 us
    pallas_call x3, Pallas kernels, compare(): pl.pallas_call(functools.partial(pair_kernel, stage, feeds), out_shape=[j...  22 us
    pallas_call x1, Pallas kernels, on_device(): pl.pallas_call(local_kernel, grid=(2 * blocks,), out_shape=(jax.ShapeDtyp...  21.8 us
    all_to_all x1, starting transfers between devices, on_device(): lax.all_to_all(col_best, ('x', 'z'), split_axis=0, concat_axis=0, tiled=T...  8.64 us
    pallas_call x2, Pallas kernels, pick(): pl.pallas_call(functools.partial(pick_kernel, wanted, spread), out_shape=...  8.13 us
    all_to_all x1, waiting for transfers between devices, on_device(): lax.all_to_all(col_best, ('x', 'z'), split_axis=0, concat_axis=0, tiled=T...  7.62 us
    ppermute x3, waiting for transfers between devices, on_device(): lax.ppermute(combined, 'rep', [(y, (y + d) % n_rep) for y in range(n_rep)])  4.95 us
  transfers between devices with their start and end apart: 21, of which 12 were waited for; matrix products, arithmetic and copies ran while one was open for 0% of the time, Pallas kernels for 27%

profile of v5, /device:TPU:24, one launch (start us, length us, event | category | flops | bytes accessed | tf_op | source)
XLA Modules:
  0.0 168.2 jit_solution(2432856573503399698)
XLA Ops:
  0.0 0.0 collective-permute-start.5
  0.0 4.4 %prep.1 = (bf16[8,128,768]{2,1,0:T(8,128)(2,1)}, bf16[1,128,768]{2,1,0:T(8,128)(2,1)}, bf16[1,128,768]{2,1,0:T(8,128)(2,1)}, bf16[1,128,768]{2,1,0:T(8,128)(2,1)...) custom-call(s32[64,64]{1,0:T(8,128)} %table.3, bf16[8,512,768]{2,1,0:T(8,128)(2,1)} %bitcast.6), custom_call_target="tpu_custom_call" | custom-call | bytes 65536 | tf_op jit(solution)/shard_map/prep/pallas_call | solution.py:386
  4.4 2.0 %collective-permute-start = (bf16[8,128,768]{2,1,0:T(8,128)(2,1)}, bf16[8,128,768]{2,1,0:T(8,128)(2,1)S(1)}, u32[]{:S(2)}, u32[]{:S(2)}) collective-permute-start(bf16[8,128,768]{2,1,0:T(8,128)(2,1)} %get-tuple-element.42.cols.after.refs_0_), channel_id=1, source_target_pairs={{0,8},{8,16},{16,24},{24,32},{32,40},{40,48},{48,56},{56,0},{64,72... | collective-permute-start | bytes 4718600 | tf_op jit(solution)/shard_map/ppermute | solution.py:325
  6.4 5.4 %collective-permute-start.1 = (bf16[1,128,768]{2,1,0:T(8,128)(2,1)}, bf16[1,128,768]{2,1,0:T(8,128)(2,1)S(1)}, u32[]{:S(2)}, u32[]{:S(2)}) collective-permute-start(bf16[1,128,768]{2,1,0:T(8,128)(2,1)} %get-tuple-element.43), channel_id=1, source_target_pairs={{0,48},{8,56},{16,0},{24,8},{32,16},{40,24},{48,32},{56,40},{64,11... | collective-permute-start | bytes 589832 | tf_op jit(solution)/shard_map/ppermute | solution.py:325
  11.8 2.4 %collective-permute-start.2 = (bf16[1,128,768]{2,1,0:T(8,128)(2,1)}, bf16[1,128,768]{2,1,0:T(8,128)(2,1)S(1)}, u32[]{:S(2)}, u32[]{:S(2)}) collective-permute-start(bf16[1,128,768]{2,1,0:T(8,128)(2,1)} %get-tuple-element.44), channel_id=1, source_target_pairs={{0,112},{8,120},{16,64},{24,72},{32,80},{40,88},{48,96},{56,104},{... | collective-permute-start | bytes 589832 | tf_op jit(solution)/shard_map/ppermute | solution.py:325
  14.1 2.7 %collective-permute-start.3 = (bf16[1,128,768]{2,1,0:T(8,128)(2,1)}, bf16[1,128,768]{2,1,0:T(8,128)(2,1)S(1)}, u32[]{:S(2)}, u32[]{:S(2)}) collective-permute-start(bf16[1,128,768]{2,1,0:T(8,128)(2,1)} %get-tuple-element.45), channel_id=1, source_target_pairs={{0,176},{8,184},{16,128},{24,136},{32,144},{40,152},{48,160},{56,1... | collective-permute-start | bytes 589832 | tf_op jit(solution)/shard_map/ppermute | solution.py:325
  16.9 0.0 collective-permute-done.5.sib
  16.9 2.1 %collective-permute-start.4 = (bf16[1,128,768]{2,1,0:T(8,128)(2,1)}, bf16[1,128,768]{2,1,0:T(8,128)(2,1)S(1)}, u32[]{:S(2)}, u32[]{:S(2)}) collective-permute-start(bf16[1,128,768]{2,1,0:T(8,128)(2,1)} %get-tuple-element.46), channel_id=1, source_target_pairs={{0,240},{8,248},{16,192},{24,200},{32,208},{40,216},{48,224},{56,2... | collective-permute-start | bytes 589832 | tf_op jit(solution)/shard_map/ppermute | solution.py:325
  19.0 2.8 %plan.1 = s32[344]{0:T(512)} custom-call(s32[64,64]{1,0:T(8,128)} %table.3, s32[512]{0:T(512)} %valid.3, bf16[8,128,768]{2,1,0:T(8,128)(2,1)} %get-tuple-element.42.cols.after.refs_0_), custom_call_target="tpu_custom_call" | custom-call | bytes 65536 | tf_op jit(solution)/shard_map/plan/pallas_call | solution.py:407
  21.8 21.8 %local.1 = (bf16[16,512,768]{2,1,0:T(8,128)(2,1)}, f32[8,512]{1,0:T(8,128)}) custom-call(s32[512]{0:T(512)} %valid.3, bf16[8,512,768]{2,1,0:T(8,128)(2,1)} %bitcast.7, bf16[8,512,768]{2,1,0:T(8,128)(2,1)} %collective-permute-done.5.sib, bf16[8,128,768]{2,1,0:T(8,128)(2,1)} %get-tuple-element.42.cols.after.refs_0_), custom_call_target="tpu_custom_call" | custom-call | bytes 65536 | tf_op jit(solution)/shard_map/local/pallas_call | solution.py:417
  43.6 0.0 collective-permute-done.1
  43.6 0.0 collective-permute-done.2
  43.6 0.0 collective-permute-done.3
  43.6 2.5 %collective-permute-done.4 = bf16[1,128,768]{2,1,0:T(8,128)(2,1)S(1)} collective-permute-done((bf16[1,128,768]{2,1,0:T(8,128)(2,1)}, bf16[1,128,768]{2,1,0:T(8,128)(2,1)S(1)}, u32[]{:S(2)}, u32[]{:S(2)}) %collective-permute-start.4) | collective-permute-done | bytes 196640 | tf_op jit(solution)/shard_map/ppermute | solution.py:325
  46.1 0.0 collective-permute-done.refs_1_
  46.1 2.5 %collective-permute-start.6 = (bf16[8,128,768]{2,1,0:T(8,128)(2,1)S(1)}, bf16[8,128,768]{2,1,0:T(8,128)(2,1)S(1)}, u32[]{:S(2)}, u32[]{:S(2)}) collective-permute-start(bf16[8,128,768]{2,1,0:T(8,128)(2,1)S(1)} %collective-permute-done.refs_1_), channel_id=1, source_target_pairs={{0,8},{8,16},{16,24},{24,32},{32,40},{40,48},{48,56},{56,0},{64,72... | collective-permute-start | bytes 4718600 | tf_op jit(solution)/shard_map/ppermute | solution.py:325
  48.6 0.1 pad_maximum_fusion
  48.7 3.0 %collective-permute-start.7 = (bf16[4,128,768]{2,1,0:T(8,128)(2,1)S(1)}, bf16[4,128,768]{2,1,0:T(8,128)(2,1)S(1)}, u32[]{:S(2)}, u32[]{:S(2)}) collective-permute-start(bf16[4,128,768]{2,1,0:T(8,128)(2,1)S(1)} %pad_maximum_fusion), channel_id=1, source_target_pairs={{0,48},{8,56},{16,0},{24,8},{32,16},{40,24},{48,32},{56,40},{64,11... | collective-permute-start | bytes 2359304 | tf_op jit(solution)/shard_map/ppermute | solution.py:325
  51.7 0.0 copy-done.4
  51.7 3.8 %pick_a.1 = (bf16[3,128,768]{2,1,0:T(8,128)(2,1)}, bf16[3,128,768]{2,1,0:T(8,128)(2,1)}, bf16[3,128,768]{2,1,0:T(8,128)(2,1)}, bf16[3,128,768]{2,1,0:T(8,128)(2,1)}) custom-call(s32[344]{0:T(512)} %plan.1, bf16[8,128,768]{2,1,0:T(8,128)(2,1)} %get-tuple-element.42.cols.after.refs_0_, bf16[8,128,768]{2,1,0:T(8,128)(2,1)} %copy-done.4), custom_call_target="tpu_custom_call" | custom-call | bytes 65536 | tf_op jit(solution)/shard_map/pick_a/pallas_call | solution.py:346
  55.6 1.7 %collective-permute-start.10 = (bf16[3,128,768]{2,1,0:T(8,128)(2,1)}, bf16[3,128,768]{2,1,0:T(8,128)(2,1)S(1)}, u32[]{:S(2)}, u32[]{:S(2)}) collective-permute-start(bf16[3,128,768]{2,1,0:T(8,128)(2,1)} %get-tuple-element.60), channel_id=1, source_target_pairs={{0,192},{8,200},{16,208},{24,216},{32,224},{40,232},{48,240},{56,2... | collective-permute-start | bytes 1769480 | tf_op jit(solution)/shard_map/ppermute | solution.py:325
  57.2 0.4 collective-permute-start.8
  57.7 2.7 %collective-permute-start.9 = (bf16[3,128,768]{2,1,0:T(8,128)(2,1)}, bf16[3,128,768]{2,1,0:T(8,128)(2,1)S(1)}, u32[]{:S(2)}, u32[]{:S(2)}) collective-permute-start(bf16[3,128,768]{2,1,0:T(8,128)(2,1)} %get-tuple-element.59), channel_id=1, source_target_pairs={{0,128},{8,136},{16,144},{24,152},{32,160},{40,168},{48,176},{56,1... | collective-permute-start | bytes 1769480 | tf_op jit(solution)/shard_map/ppermute | solution.py:325
  60.3 11.8 %collective-permute-done.10.refs_3_ = bf16[3,128,768]{2,1,0:T(8,128)(2,1)S(1)} collective-permute-done((bf16[3,128,768]{2,1,0:T(8,128)(2,1)}, bf16[3,128,768]{2,1,0:T(8,128)(2,1)S(1)}, u32[]{:S(2)}, u32[]{:S(2)}) %collective-permute-start.10) | collective-permute-done | bytes 589856 | tf_op jit(solution)/shard_map/ppermute | solution.py:325
  72.1 13.7 %collective-permute-done.8.refs_1_ = bf16[3,128,768]{2,1,0:T(8,128)(2,1)S(1)} collective-permute-done((bf16[3,128,768]{2,1,0:T(8,128)(2,1)}, bf16[3,128,768]{2,1,0:T(8,128)(2,1)S(1)}, u32[]{:S(2)}, u32[]{:S(2)}) %collective-permute-start.8) | collective-permute-done | bytes 589856 | tf_op jit(solution)/shard_map/ppermute | solution.py:325
  85.8 0.0 collective-permute-done.9.refs_2_
  85.8 0.0 collective-permute-done.7.refs_4_
  85.8 0.0 copy-start.6
  85.8 0.0 collective-permute-done.6.refs_1_
  85.8 0.0 copy-start.5
  85.8 1.2 copy-done.5
  87.0 4.3 %pick_b.1 = (bf16[2,128,768]{2,1,0:T(8,128)(2,1)}, bf16[2,128,768]{2,1,0:T(8,128)(2,1)}, bf16[2,128,768]{2,1,0:T(8,128)(2,1)}, bf16[4,2,128,768]{3,2,1,0:T(8,128)(2,1)}) custom-call(s32[344]{0:T(512)} %plan.1, bf16[8,128,768]{2,1,0:T(8,128)(2,1)} %get-tuple-element.42.cols.after.refs_0_, bf16[8,128,768]{2,1,0:T(8,128)(2,1)} %copy-done.5), custom_call_target="tpu_custom_call" | custom-call | bytes 65536 | tf_op jit(solution)/shard_map/pick_b/pallas_call | solution.py:346
  91.3 0.0 copy-done.9
  91.4 3.6 %all-to-all-start = ((bf16[4,2,128,768]{3,2,1,0:T(8,128)(2,1)}), bf16[4,2,128,768]{3,2,1,0:T(8,128)(2,1)S(1)}, u32[]{:S(2)}, u32[]{:S(2)}) async-start(bf16[4,2,128,768]{3,2,1,0:T(8,128)(2,1)} %get-tuple-element.75), calls=%async_computation | async-start | bytes 3145728 | tf_op jit(solution)/shard_map/all_to_all | solution.py:446
  94.9 1.2 collective-permute-start.11
  96.1 1.5 collective-permute-start.12
  97.6 3.5 %collective-permute-start.13 = (bf16[2,128,768]{2,1,0:T(8,128)(2,1)}, bf16[2,128,768]{2,1,0:T(8,128)(2,1)S(1)}, u32[]{:S(2)}, u32[]{:S(2)}) collective-permute-start(bf16[2,128,768]{2,1,0:T(8,128)(2,1)} %get-tuple-element.73), channel_id=1, source_target_pairs={{0,200},{8,208},{16,216},{24,224},{32,232},{40,240},{48,248},{56,1... | collective-permute-start | bytes 1179656 | tf_op jit(solution)/shard_map/ppermute | solution.py:325
  101.1 3.8 %collective-permute-start.14 = (bf16[2,128,768]{2,1,0:T(8,128)(2,1)}, bf16[2,128,768]{2,1,0:T(8,128)(2,1)}, u32[]{:S(2)}, u32[]{:S(2)}) collective-permute-start(bf16[2,128,768]{2,1,0:T(8,128)(2,1)} %get-tuple-element.74), channel_id=1, source_target_pairs={{0,168},{8,176},{16,184},{24,128},{32,136},{40,144},{48,152},{56,1... | collective-permute-start | bytes 1179656 | tf_op jit(solution)/shard_map/ppermute | solution.py:325
  104.9 0.0 copy-done.7
  104.9 0.0 copy-done.8
  104.9 8.7 %pairs_a.1 = (f32[16,512]{1,0:T(8,128)}, f32[16,128]{1,0:T(8,128)}) custom-call(s32[344]{0:T(512)} %plan.1, bf16[16,512,768]{2,1,0:T(8,128)(2,1)} %get-tuple-element.50.own, bf16[3,128,768]{2,1,0:T(8,128)(2,1)} %get-tuple-element.61.refs_0_, bf16[3,128,768]{2,1,0:T(8,128)(2,1)} %copy-done.8, bf16[3,128,768]{2,1,0:T(8,128)(2,1)} %copy-done.9, ...), custom_call_target="tpu_custom_call" | custom-call | bytes 65536 | tf_op jit(solution)/shard_map/pairs_a/pallas_call | solution.py:366
  113.6 0.0 collective-permute-done.11.refs_0_
  113.6 6.1 %collective-permute-done.12.refs_1_ = bf16[2,128,768]{2,1,0:T(8,128)(2,1)S(1)} collective-permute-done((bf16[2,128,768]{2,1,0:T(8,128)(2,1)}, bf16[2,128,768]{2,1,0:T(8,128)(2,1)S(1)}, u32[]{:S(2)}, u32[]{:S(2)}) %collective-permute-start.12) | collective-permute-done | bytes 393248 | tf_op jit(solution)/shard_map/ppermute | solution.py:325
  119.8 0.8 copy-done.11
  120.5 4.7 %pairs_b.1 = (f32[16,512]{1,0:T(8,128)}, f32[4,128]{1,0:T(4,128)}) custom-call(s32[344]{0:T(512)} %plan.1, bf16[16,512,768]{2,1,0:T(8,128)(2,1)} %get-tuple-element.50.own, bf16[2,128,768]{2,1,0:T(8,128)(2,1)} %copy-done.10, bf16[2,128,768]{2,1,0:T(8,128)(2,1)} %copy-done.11, f32[16,512]{1,0:T(8,128)} %get-tuple-element.68.refs_2_.refs_0_), custom_call_target="tpu_custom_call" | custom-call | bytes 65536 | tf_op jit(solution)/shard_map/pairs_b/pallas_call | solution.py:366
  125.2 1.0 collective-permute-done.13.refs_4_
  126.3 0.8 copy-done.12
  127.0 3.6 %collective-permute-done.14.refs_5_ = bf16[2,128,768]{2,1,0:T(8,128)(2,1)} collective-permute-done((bf16[2,128,768]{2,1,0:T(8,128)(2,1)}, bf16[2,128,768]{2,1,0:T(8,128)(2,1)}, u32[]{:S(2)}, u32[]{:S(2)}) %collective-permute-start.14) | collective-permute-done | bytes 393248 | tf_op jit(solution)/shard_map/ppermute | solution.py:325
  130.6 0.1 all-to-all-done.refs_6_
  130.7 1.2 copy-done.3
  131.9 8.6 %pairs_c.1 = (f32[16,512]{1,0:T(8,128)}, f32[64,128]{1,0:T(8,128)}, f32[8,512]{1,0:T(8,128)}) custom-call(s32[344]{0:T(512)} %plan.1, bf16[16,512,768]{2,1,0:T(8,128)(2,1)} %get-tuple-element.50.own, f32[16,512]{1,0:T(8,128)} %get-tuple-element.68.refs_2_.refs_0_, f32[16,128]{1,0:T(8,128)} %get-tuple-element.69.refs_1_, ...), custom_call_target="tpu_custom_call" | custom-call | bytes 65536 | tf_op jit(solution)/shard_map/pairs_c/pallas_call | solution.py:366
  140.5 8.6 %all-to-all-start.1 = ((f32[32,2,128]{2,1,0:T(2,128)}), f32[32,2,128]{2,1,0:T(2,128)S(1)}, u32[]{:S(2)}, u32[]{:S(2)}) async-start(f32[32,2,128]{2,1,0:T(2,128)} %bitcast.8), calls=%async_computation.1 | async-start | bytes 65536 | tf_op jit(solution)/shard_map/all_to_all | solution.py:474
  149.1 0.1 collective-permute-start.15
  149.2 1.4 collective-permute-done.15.sib_rows
  150.6 0.8 copy-done.1
  151.4 7.6 %all-to-all-done.1 = f32[32,2,128]{2,1,0:T(2,128)S(1)} async-done(((f32[32,2,128]{2,1,0:T(2,128)}), f32[32,2,128]{2,1,0:T(2,128)S(1)}, u32[]{:S(2)}, u32[]{:S(2)}) %all-to-all-start.1) | async-done | bytes 32800 | tf_op jit(solution)/shard_map/all_to_all | solution.py:474
  159.0 0.7 merge.1.one
  159.8 0.3 collective-permute-start.16
  160.1 2.6 %collective-permute-start.17 = (f32[8,512]{1,0:T(8,128)S(1)}, f32[8,512]{1,0:T(8,128)S(1)}, u32[]{:S(2)}, u32[]{:S(2)}) collective-permute-start(f32[8,512]{1,0:T(8,128)S(1)} %merge.1.one), channel_id=1, source_target_pairs={{0,2},{1,3},{2,0},{3,1},{4,6},{5,7},{6,4},{7,5},{8,10},{9,11},{10,... | collective-permute-start | bytes 49160 | tf_op jit(solution)/shard_map/ppermute | solution.py:495
  162.6 0.0 collective-permute-start.18
  162.6 0.9 collective-permute-done.16.two
  163.6 1.7 %collective-permute-done.17.three = f32[8,512]{1,0:T(8,128)S(1)} collective-permute-done((f32[8,512]{1,0:T(8,128)S(1)}, f32[8,512]{1,0:T(8,128)S(1)}, u32[]{:S(2)}, u32[]{:S(2)}) %collective-permute-start.17) | collective-permute-done | bytes 16416 | tf_op jit(solution)/shard_map/ppermute | solution.py:495
  165.3 2.3 %collective-permute-done.18.four = f32[8,512]{1,0:T(8,128)S(1)} collective-permute-done((f32[8,512]{1,0:T(8,128)S(1)}, f32[8,512]{1,0:T(8,128)S(1)}, u32[]{:S(2)}, u32[]{:S(2)}) %collective-permute-start.18) | collective-permute-done | bytes 16416 | tf_op jit(solution)/shard_map/ppermute | solution.py:495
  167.6 0.6 finish.1
  (16 shorter events, 0.0 us)
Async XLA Ops:
  0.0 16.9 %collective-permute-start.5 = (bf16[8,512,768]{2,1,0:T(8,128)(2,1)}, bf16[8,512,768]{2,1,0:T(8,128)(2,1)}, u32[]{:S(2)}, u32[]{:S(2)}) collective-permute-start(bf16[8,512,768]{2,1,0:T(8,128)(2,1)} %bitcast.5), channel_id=1, source_target_pairs={{0,4},{4,0},{1,5},{5,1},{2,6},{6,2},{3,7},{7,3},{8,12},{12,8},{9,1... | collective-permute-start | bytes 18874376 | tf_op jit(solution)/shard_map/ppermute | solution.py:404
  4.4 41.7 %collective-permute-start = (bf16[8,128,768]{2,1,0:T(8,128)(2,1)}, bf16[8,128,768]{2,1,0:T(8,128)(2,1)S(1)}, u32[]{:S(2)}, u32[]{:S(2)}) collective-permute-start(bf16[8,128,768]{2,1,0:T(8,128)(2,1)} %get-tuple-element.42.cols.after.refs_0_), channel_id=1, source_target_pairs={{0,8},{8,16},{16,24},{24,32},{32,40},{40,48},{48,56},{56,0},{64,72... | collective-permute-start | bytes 4718600 | tf_op jit(solution)/shard_map/ppermute | solution.py:325
  6.4 37.3 %collective-permute-start.1 = (bf16[1,128,768]{2,1,0:T(8,128)(2,1)}, bf16[1,128,768]{2,1,0:T(8,128)(2,1)S(1)}, u32[]{:S(2)}, u32[]{:S(2)}) collective-permute-start(bf16[1,128,768]{2,1,0:T(8,128)(2,1)} %get-tuple-element.43), channel_id=1, source_target_pairs={{0,48},{8,56},{16,0},{24,8},{32,16},{40,24},{48,32},{56,40},{64,11... | collective-permute-start | bytes 589832 | tf_op jit(solution)/shard_map/ppermute | solution.py:325
  11.8 31.9 %collective-permute-start.2 = (bf16[1,128,768]{2,1,0:T(8,128)(2,1)}, bf16[1,128,768]{2,1,0:T(8,128)(2,1)S(1)}, u32[]{:S(2)}, u32[]{:S(2)}) collective-permute-start(bf16[1,128,768]{2,1,0:T(8,128)(2,1)} %get-tuple-element.44), channel_id=1, source_target_pairs={{0,112},{8,120},{16,64},{24,72},{32,80},{40,88},{48,96},{56,104},{... | collective-permute-start | bytes 589832 | tf_op jit(solution)/shard_map/ppermute | solution.py:325
  14.1 29.5 %collective-permute-start.3 = (bf16[1,128,768]{2,1,0:T(8,128)(2,1)}, bf16[1,128,768]{2,1,0:T(8,128)(2,1)S(1)}, u32[]{:S(2)}, u32[]{:S(2)}) collective-permute-start(bf16[1,128,768]{2,1,0:T(8,128)(2,1)} %get-tuple-element.45), channel_id=1, source_target_pairs={{0,176},{8,184},{16,128},{24,136},{32,144},{40,152},{48,160},{56,1... | collective-permute-start | bytes 589832 | tf_op jit(solution)/shard_map/ppermute | solution.py:325
  16.9 29.2 %collective-permute-start.4 = (bf16[1,128,768]{2,1,0:T(8,128)(2,1)}, bf16[1,128,768]{2,1,0:T(8,128)(2,1)S(1)}, u32[]{:S(2)}, u32[]{:S(2)}) collective-permute-start(bf16[1,128,768]{2,1,0:T(8,128)(2,1)} %get-tuple-element.46), channel_id=1, source_target_pairs={{0,240},{8,248},{16,192},{24,200},{32,208},{40,216},{48,224},{56,2... | collective-permute-start | bytes 589832 | tf_op jit(solution)/shard_map/ppermute | solution.py:325
  46.1 5.6 %copy-start.4 = (bf16[8,128,768]{2,1,0:T(8,128)(2,1)}, bf16[8,128,768]{2,1,0:T(8,128)(2,1)S(1)}, u32[]{:S(2)}) copy-start(bf16[8,128,768]{2,1,0:T(8,128)(2,1)S(1)} %collective-permute-done.refs_1_) | copy-start | bytes 4718596
  46.1 39.7 %collective-permute-start.6 = (bf16[8,128,768]{2,1,0:T(8,128)(2,1)S(1)}, bf16[8,128,768]{2,1,0:T(8,128)(2,1)S(1)}, u32[]{:S(2)}, u32[]{:S(2)}) collective-permute-start(bf16[8,128,768]{2,1,0:T(8,128)(2,1)S(1)} %collective-permute-done.refs_1_), channel_id=1, source_target_pairs={{0,8},{8,16},{16,24},{24,32},{32,40},{40,48},{48,56},{56,0},{64,72... | collective-permute-start | bytes 4718600 | tf_op jit(solution)/shard_map/ppermute | solution.py:325
  48.7 37.1 %collective-permute-start.7 = (bf16[4,128,768]{2,1,0:T(8,128)(2,1)S(1)}, bf16[4,128,768]{2,1,0:T(8,128)(2,1)S(1)}, u32[]{:S(2)}, u32[]{:S(2)}) collective-permute-start(bf16[4,128,768]{2,1,0:T(8,128)(2,1)S(1)} %pad_maximum_fusion), channel_id=1, source_target_pairs={{0,48},{8,56},{16,0},{24,8},{32,16},{40,24},{48,32},{56,40},{64,11... | collective-permute-start | bytes 2359304 | tf_op jit(solution)/shard_map/ppermute | solution.py:325
  55.6 16.5 %collective-permute-start.10 = (bf16[3,128,768]{2,1,0:T(8,128)(2,1)}, bf16[3,128,768]{2,1,0:T(8,128)(2,1)S(1)}, u32[]{:S(2)}, u32[]{:S(2)}) collective-permute-start(bf16[3,128,768]{2,1,0:T(8,128)(2,1)} %get-tuple-element.60), channel_id=1, source_target_pairs={{0,192},{8,200},{16,208},{24,216},{32,224},{40,232},{48,240},{56,2... | collective-permute-start | bytes 1769480 | tf_op jit(solution)/shard_map/ppermute | solution.py:325
  57.2 28.5 %collective-permute-start.8 = (bf16[3,128,768]{2,1,0:T(8,128)(2,1)}, bf16[3,128,768]{2,1,0:T(8,128)(2,1)S(1)}, u32[]{:S(2)}, u32[]{:S(2)}) collective-permute-start(bf16[3,128,768]{2,1,0:T(8,128)(2,1)} %get-tuple-element.58), channel_id=1, source_target_pairs={{0,64},{8,72},{16,80},{24,88},{32,96},{40,104},{48,112},{56,120},{... | collective-permute-start | bytes 1769480 | tf_op jit(solution)/shard_map/ppermute | solution.py:325
  57.7 28.1 %collective-permute-start.9 = (bf16[3,128,768]{2,1,0:T(8,128)(2,1)}, bf16[3,128,768]{2,1,0:T(8,128)(2,1)S(1)}, u32[]{:S(2)}, u32[]{:S(2)}) collective-permute-start(bf16[3,128,768]{2,1,0:T(8,128)(2,1)} %get-tuple-element.59), channel_id=1, source_target_pairs={{0,128},{8,136},{16,144},{24,152},{32,160},{40,168},{48,176},{56,1... | collective-permute-start | bytes 1769480 | tf_op jit(solution)/shard_map/ppermute | solution.py:325
  72.1 32.8 %copy-start.7 = (bf16[3,128,768]{2,1,0:T(8,128)(2,1)}, bf16[3,128,768]{2,1,0:T(8,128)(2,1)S(1)}, u32[]{:S(2)}) copy-start(bf16[3,128,768]{2,1,0:T(8,128)(2,1)S(1)} %collective-permute-done.10.refs_3_) | copy-start | bytes 1769476
  85.8 19.1 %copy-start.8 = (bf16[3,128,768]{2,1,0:T(8,128)(2,1)}, bf16[3,128,768]{2,1,0:T(8,128)(2,1)S(1)}, u32[]{:S(2)}) copy-start(bf16[3,128,768]{2,1,0:T(8,128)(2,1)S(1)} %collective-permute-done.8.refs_1_) | copy-start | bytes 1769476
  85.8 5.6 %copy-start.9 = (bf16[3,128,768]{2,1,0:T(8,128)(2,1)}, bf16[3,128,768]{2,1,0:T(8,128)(2,1)S(1)}, u32[]{:S(2)}) copy-start(bf16[3,128,768]{2,1,0:T(8,128)(2,1)S(1)} %collective-permute-done.9.refs_2_) | copy-start | bytes 1769476
  85.8 19.1 %copy-start.6 = (bf16[4,128,768]{2,1,0:T(8,128)(2,1)}, bf16[4,128,768]{2,1,0:T(8,128)(2,1)S(1)}, u32[]{:S(2)}) copy-start(bf16[4,128,768]{2,1,0:T(8,128)(2,1)S(1)} %collective-permute-done.7.refs_4_) | copy-start | bytes 2359300
  85.8 1.2 copy-start.5
  91.4 39.4 %all-to-all-start = ((bf16[4,2,128,768]{3,2,1,0:T(8,128)(2,1)}), bf16[4,2,128,768]{3,2,1,0:T(8,128)(2,1)S(1)}, u32[]{:S(2)}, u32[]{:S(2)}) async-start(bf16[4,2,128,768]{3,2,1,0:T(8,128)(2,1)} %get-tuple-element.75), calls=%async_computation | async-start | bytes 3145728 | tf_op jit(solution)/shard_map/all_to_all | solution.py:446
  94.9 18.7 %collective-permute-start.11 = (bf16[2,128,768]{2,1,0:T(8,128)(2,1)}, bf16[2,128,768]{2,1,0:T(8,128)(2,1)S(1)}, u32[]{:S(2)}, u32[]{:S(2)}) collective-permute-start(bf16[2,128,768]{2,1,0:T(8,128)(2,1)} %get-tuple-element.67.refs_5_), channel_id=1, source_target_pairs={{0,8},{8,16},{16,24},{24,32},{32,40},{40,48},{48,56},{56,0},{64,72... | collective-permute-start | bytes 1179656 | tf_op jit(solution)/shard_map/ppermute | solution.py:325
  96.1 23.6 %collective-permute-start.12 = (bf16[2,128,768]{2,1,0:T(8,128)(2,1)}, bf16[2,128,768]{2,1,0:T(8,128)(2,1)S(1)}, u32[]{:S(2)}, u32[]{:S(2)}) collective-permute-start(bf16[2,128,768]{2,1,0:T(8,128)(2,1)} %get-tuple-element.70), channel_id=1, source_target_pairs={{0,72},{8,80},{16,88},{24,96},{32,104},{40,112},{48,120},{56,64},{... | collective-permute-start | bytes 1179656 | tf_op jit(solution)/shard_map/ppermute | solution.py:325
  97.6 28.7 %collective-permute-start.13 = (bf16[2,128,768]{2,1,0:T(8,128)(2,1)}, bf16[2,128,768]{2,1,0:T(8,128)(2,1)S(1)}, u32[]{:S(2)}, u32[]{:S(2)}) collective-permute-start(bf16[2,128,768]{2,1,0:T(8,128)(2,1)} %get-tuple-element.73), channel_id=1, source_target_pairs={{0,200},{8,208},{16,216},{24,224},{32,232},{40,240},{48,248},{56,1... | collective-permute-start | bytes 1179656 | tf_op jit(solution)/shard_map/ppermute | solution.py:325
  101.1 29.5 %collective-permute-start.14 = (bf16[2,128,768]{2,1,0:T(8,128)(2,1)}, bf16[2,128,768]{2,1,0:T(8,128)(2,1)}, u32[]{:S(2)}, u32[]{:S(2)}) collective-permute-start(bf16[2,128,768]{2,1,0:T(8,128)(2,1)} %get-tuple-element.74), channel_id=1, source_target_pairs={{0,168},{8,176},{16,184},{24,128},{32,136},{40,144},{48,152},{56,1... | collective-permute-start | bytes 1179656 | tf_op jit(solution)/shard_map/ppermute | solution.py:325
  113.6 6.2 %copy-start.10 = (bf16[2,128,768]{2,1,0:T(8,128)(2,1)}, bf16[2,128,768]{2,1,0:T(8,128)(2,1)S(1)}, u32[]{:S(2)}) copy-start(bf16[2,128,768]{2,1,0:T(8,128)(2,1)S(1)} %collective-permute-done.11.refs_0_) | copy-start | bytes 1179652
  119.8 0.8 copy-start.11
  126.3 0.8 copy-start.12
  130.7 1.2 copy-start.3
  131.9 18.7 %copy-start.2 = (f32[8,512]{1,0:T(8,128)S(1)}, f32[8,512]{1,0:T(8,128)}, u32[]{:S(2)}) copy-start(f32[8,512]{1,0:T(8,128)} %get-tuple-element.49.local) | copy-start | bytes 49156
  131.9 27.1 %copy-start = (s32[344]{0:T(512)S(1)}, s32[344]{0:T(512)}, u32[]{:S(2)}) copy-start(s32[344]{0:T(512)} %plan.1) | copy-start | bytes 4132
  140.5 18.5 %all-to-all-start.1 = ((f32[32,2,128]{2,1,0:T(2,128)}), f32[32,2,128]{2,1,0:T(2,128)S(1)}, u32[]{:S(2)}, u32[]{:S(2)}) async-start(f32[32,2,128]{2,1,0:T(2,128)} %bitcast.8), calls=%async_computation.1 | async-start | bytes 65536 | tf_op jit(solution)/shard_map/all_to_all | solution.py:474
  149.1 1.5 collective-permute-start.15
  150.6 0.8 copy-start.1
  159.8 3.8 %collective-permute-start.16 = (f32[8,512]{1,0:T(8,128)S(1)}, f32[8,512]{1,0:T(8,128)S(1)}, u32[]{:S(2)}, u32[]{:S(2)}) collective-permute-start(f32[8,512]{1,0:T(8,128)S(1)} %merge.1.one), channel_id=1, source_target_pairs={{0,1},{1,2},{2,3},{3,0},{4,5},{5,6},{6,7},{7,4},{8,9},{9,10},{10,1... | collective-permute-start | bytes 49160 | tf_op jit(solution)/shard_map/ppermute | solution.py:495
  160.1 5.2 %collective-permute-start.17 = (f32[8,512]{1,0:T(8,128)S(1)}, f32[8,512]{1,0:T(8,128)S(1)}, u32[]{:S(2)}, u32[]{:S(2)}) collective-permute-start(f32[8,512]{1,0:T(8,128)S(1)} %merge.1.one), channel_id=1, source_target_pairs={{0,2},{1,3},{2,0},{3,1},{4,6},{5,7},{6,4},{7,5},{8,10},{9,11},{10,... | collective-permute-start | bytes 49160 | tf_op jit(solution)/shard_map/ppermute | solution.py:495
  162.6 4.9 %collective-permute-start.18 = (f32[8,512]{1,0:T(8,128)S(1)}, f32[8,512]{1,0:T(8,128)S(1)}, u32[]{:S(2)}, u32[]{:S(2)}) collective-permute-start(f32[8,512]{1,0:T(8,128)S(1)} %merge.1.one), channel_id=1, source_target_pairs={{0,3},{1,0},{2,1},{3,2},{4,7},{5,4},{6,5},{7,6},{8,11},{9,8},{10,9... | collective-permute-start | bytes 49160 | tf_op jit(solution)/shard_map/ppermute | solution.py:495

commit v6 on v5

--- a/solution.py
+++ b/solution.py
@@ -54,10 +54,10 @@
 second = [[(dx, 2, 2, 0), (dx, 2, 2, 1)] for dx in range(n_x)]
 third = [[(dx, 3, 2, 0), (dx, 3, 2, 1)] for dx in (0, 1, 3)]
 far = [(dx, 4, 1, 0) for dx in range(n_x)]
-down = [(2, 5, 2, 0), (2, 5, 2, 1)]
-stages = [sum(first, []) + far, third[0] + third[1], third[2] + down + sum(second, [])]
+extra, down = [(2, 3, 1, 0)], [(2, 5, 1, 0)]
+stages = [sum(first, []) + far, third[0] + third[1], third[2] + extra + down + sum(second, [])]
 every = sum(stages, [])
-gone_of = {0: 0, 1: 1, 2: 2, 3: 2}
+gone_of = {0: 0, 1: 1, 2: 2, 3: 2, 5: 0}
 at_pick, at_back, at_back_row, at_row, at_own = 0, 32, 64, 96, 128
 at_stage, plan_size = [], 144
 for stage in stages:
@@ -120,7 +120,7 @@
         plan[second_of + count] = slots
 
 
-def prep_kernel(table, emb, units, to0, to1, to2, to3, around, raw, unit, sem_in, sems):
+def prep_kernel(table, emb, units, to0, to1, to2, to3, raw, unit, sem_in, sems):
     x, z, core, rep = place()
     chip = chip_at(x, z, 0, 0)
     loads = [
@@ -135,8 +135,8 @@
         unit[b] = normalise(raw[b])
         copies.append(pltpu.make_async_copy(unit.at[b], units.at[b], sem_in.at[b]))
         copies[-1].start()
-    outs = [to0.at[0], to1.at[0], to2.at[0], to3.at[0], around.at[0], around.at[1]]
-    for a, (dx, dz, many, which) in enumerate(far + down):
+    outs = [to0.at[0], to1.at[0], to2.at[0], to3.at[0]]
+    for a, (dx, dz, many, which) in enumerate(far):
         _, _, block, _ = pair_info(table, chip, chip_at(x, z, dx, dz), core, many, which)
         copies.append(pltpu.make_async_copy(unit.at[block], outs[a], sems.at[a]))
         copies[-1].start()
@@ -157,12 +157,12 @@
     gets, puts = [], []
     for a, numbers in enumerate(wanted):
         for place_in, number in enumerate(numbers):
-            held = near_by if every[number][1] == 0 else hop
+            held = near_by if every[number][1] in (0, 5) else hop
             gets.append(
                 pltpu.make_async_copy(
                     held.at[plan[at_pick + number]],
                     parts.at[a, place_in],
-                    get_sems.at[3 * a + place_in],
+                    get_sems.at[4 * a + place_in],
                 )
             )
             gets[-1].start()
@@ -218,7 +218,9 @@
     x, z, core, rep = place()
     gets = []
     for a, (array, dx, count, first_slot) in enumerate(feeds):
-        came = arrays[array] if dx is None else arrays[array].at[(x - dx + n_x) & (n_x - 1)]
+        came = arrays[array].at[pl.ds(0, count)]
+        if dx is not None:
+            came = arrays[array].at[(x - dx + n_x) & (n_x - 1)]
         gets.append(pltpu.make_async_copy(came, held.at[pl.ds(first_slot, count)], sem_g.at[a]))
         gets[-1].start()
     loads = []
@@ -349,8 +351,8 @@
             in_specs=[smem] + [hbm] * len(held + after),
             out_specs=[hbm] * len(shapes),
             scratch_shapes=[
-                pltpu.VMEM((n, 3) + part, bf16),
-                pltpu.SemaphoreType.DMA((3 * n,)),
+                pltpu.VMEM((n, 4) + part, bf16),
+                pltpu.SemaphoreType.DMA((4 * n,)),
                 pltpu.SemaphoreType.DMA((n,)),
             ],
             compiler_params=middle,
@@ -383,18 +385,17 @@
     def numbers(wanted):
         return [[every.index(slot) for slot in slots] for slots in wanted]
 
-    cols, *away, around = pl.pallas_call(
+    cols, *away = pl.pallas_call(
         prep_kernel,
         out_shape=[jax.ShapeDtypeStruct((blocks,) + part, bf16)]
-        + [jax.ShapeDtypeStruct((1,) + part, bf16)] * n_x
-        + [jax.ShapeDtypeStruct((2,) + part, bf16)],
+        + [jax.ShapeDtypeStruct((1,) + part, bf16)] * n_x,
         in_specs=[smem, hbm],
-        out_specs=[hbm] * (2 + n_x),
+        out_specs=[hbm] * (1 + n_x),
         scratch_shapes=[
             pltpu.VMEM((blocks,) + part, bf16),
             pltpu.VMEM((blocks,) + part, bf16),
             pltpu.SemaphoreType.DMA((blocks,)),
-            pltpu.SemaphoreType.DMA((len(far + down),)),
+            pltpu.SemaphoreType.DMA((n_x,)),
         ],
         compiler_params=params,
         cost_estimate=cost,
@@ -438,13 +439,15 @@
     hop1, away, local_best, plan = lax.optimization_barrier((hop1, away, local_best, plan))
     hop2 = move(hop1, 0, 1)
     away = move(jnp.concatenate(away, axis=0), 0, -2)
-    picked = pick(numbers(first), False, [cols, hop1], [], "pick_a")
+    wanted = [slots + down if slots[0][0] == 2 else slots for slots in first]
+    picked = pick(numbers(wanted), False, [cols, hop1], [], "pick_a")
     first_in = [move(a, dx, 0) for dx, a in enumerate(picked)]
-    hop2, away, around, *first_in = lax.optimization_barrier((hop2, away, around, *first_in))
-    picked = pick(numbers(third + second), True, [cols, hop2], [], "pick_b")
-    third_in = [move(a, slots[0][0], 1) for slots, a in zip(third, picked)]
+    hop2, away, *first_in = lax.optimization_barrier((hop2, away, *first_in))
+    wanted = third + [extra]
+    picked = pick(numbers(wanted + second), True, [cols, hop2], [], "pick_b")
+    third_in = [move(a, slots[0][0], 1) for slots, a in zip(wanted, picked)]
     second_in = lax.all_to_all(picked[-1], "x", split_axis=0, concat_axis=0, tiled=True)
-    down_in = move(around, 2, -3)
+    down_in = move(first_in[2][3:], 0, -3)
 
     past_a = compare(
         0,
@@ -464,8 +467,9 @@
     )
     row_best, col_best, sib_best = compare(
         2,
-        [(0, None, 2, 0), (1, None, 2, 2)] + [(2, dx, 2, 4 + 2 * dx) for dx in range(n_x)],
-        [third_in[2], down_in, second_in],
+        [(0, None, 2, 0), (1, None, 1, 2), (2, None, 1, 3)]
+        + [(3, dx, 2, 4 + 2 * dx) for dx in range(n_x)],
+        [third_in[2], third_in[3], down_in, second_in],
         [*past_a, *past_b],
         [],
         "pairs_c",

time: 170 us -> 174 us (1.024)
  waiting for transfers between devices: 52.7 us -> 55.3 us
    ppermute x14 -> x15, starting transfers between devices: 34.9 us -> 37.7 us  [move(): return lax.ppermute(value, ('x', 'z'), steps)]
    ppermute x14 -> x15, waiting for transfers between devices: 38.7 us -> 41.3 us  [move(): return lax.ppermute(value, ('x', 'z'), steps)]
    unnamed x26 -> x34, local copies, waits for them, and re-layouts: 4.68 us -> 5.33 us
  transfers between devices with their start and end apart: 21 -> 22, of which waited for: 12 -> 11; matrix products, arithmetic and copies ran while one was open for 0% -> 0% of each run, Pallas kernels for 27% -> 27%
where the time goes in v6:
time: 174 us; the launch traced here: 173 us
  Pallas kernels  60.3 us (35%)
  waiting for transfers between devices  55.3 us (32%)
  starting transfers between devices  51.4 us (30%)
  local copies, waits for them, and re-layouts  5.35 us (3%)
    ppermute x15, waiting for transfers between devices, move(): return lax.ppermute(value, ('x', 'z'), steps)  41.3 us
    ppermute x15, starting transfers between devices, move(): return lax.ppermute(value, ('x', 'z'), steps)  37.7 us
    pallas_call x3, Pallas kernels, compare(): pl.pallas_call(functools.partial(pair_kernel, stage, feeds), out_shape=[j...  21.9 us
    pallas_call x1, Pallas kernels, on_device(): pl.pallas_call(local_kernel, grid=(2 * blocks,), out_shape=(jax.ShapeDtyp...  21.8 us
    pallas_call x2, Pallas kernels, pick(): pl.pallas_call(functools.partial(pick_kernel, wanted, spread), out_shape=...  8.2 us
    all_to_all x1, waiting for transfers between devices, on_device(): lax.all_to_all(col_best, ('x', 'z'), split_axis=0, concat_axis=0, tiled=T...  7.65 us
    all_to_all x1, starting transfers between devices, on_device(): lax.all_to_all(col_best, ('x', 'z'), split_axis=0, concat_axis=0, tiled=T...  7.16 us
    unnamed x34, local copies, waits for them, and re-layouts  5.33 us
  transfers between devices with their start and end apart: 22, of which 11 were waited for; matrix products, arithmetic and copies ran while one was open for 0% of the time, Pallas kernels for 27%

profile of v6, /device:TPU:24, one launch (start us, length us, event | category | flops | bytes accessed | tf_op | source)
XLA Modules:
  0.0 172.7 jit_solution(12332180790891474725)
XLA Ops:
  0.0 0.0 collective-permute-start.5
  0.0 4.2 %prep.1 = (bf16[8,128,768]{2,1,0:T(8,128)(2,1)}, bf16[1,128,768]{2,1,0:T(8,128)(2,1)}, bf16[1,128,768]{2,1,0:T(8,128)(2,1)}, bf16[1,128,768]{2,1,0:T(8,128)(2,1)}, bf16[1,128,768]{2,1,0:T(8,128)(2,1)}) custom-call(s32[64,64]{1,0:T(8,128)} %table.3, bf16[8,512,768]{2,1,0:T(8,128)(2,1)} %bitcast.6), custom_call_target="tpu_custom_call" | custom-call | bytes 65536 | tf_op jit(solution)/shard_map/prep/pallas_call | solution.py:388
  4.2 2.0 %collective-permute-start = (bf16[8,128,768]{2,1,0:T(8,128)(2,1)}, bf16[8,128,768]{2,1,0:T(8,128)(2,1)S(1)}, u32[]{:S(2)}, u32[]{:S(2)}) collective-permute-start(bf16[8,128,768]{2,1,0:T(8,128)(2,1)} %get-tuple-element.41.cols.after.refs_0_), channel_id=1, source_target_pairs={{0,8},{8,16},{16,24},{24,32},{32,40},{40,48},{48,56},{56,0},{64,72... | collective-permute-start | bytes 4718600 | tf_op jit(solution)/shard_map/ppermute | solution.py:327
  6.2 5.4 %collective-permute-start.1 = (bf16[1,128,768]{2,1,0:T(8,128)(2,1)}, bf16[1,128,768]{2,1,0:T(8,128)(2,1)S(1)}, u32[]{:S(2)}, u32[]{:S(2)}) collective-permute-start(bf16[1,128,768]{2,1,0:T(8,128)(2,1)} %get-tuple-element.42), channel_id=1, source_target_pairs={{0,48},{8,56},{16,0},{24,8},{32,16},{40,24},{48,32},{56,40},{64,11... | collective-permute-start | bytes 589832 | tf_op jit(solution)/shard_map/ppermute | solution.py:327
  11.6 2.4 %collective-permute-start.2 = (bf16[1,128,768]{2,1,0:T(8,128)(2,1)}, bf16[1,128,768]{2,1,0:T(8,128)(2,1)S(1)}, u32[]{:S(2)}, u32[]{:S(2)}) collective-permute-start(bf16[1,128,768]{2,1,0:T(8,128)(2,1)} %get-tuple-element.43), channel_id=1, source_target_pairs={{0,112},{8,120},{16,64},{24,72},{32,80},{40,88},{48,96},{56,104},{... | collective-permute-start | bytes 589832 | tf_op jit(solution)/shard_map/ppermute | solution.py:327
  14.0 2.7 %collective-permute-start.3 = (bf16[1,128,768]{2,1,0:T(8,128)(2,1)}, bf16[1,128,768]{2,1,0:T(8,128)(2,1)S(1)}, u32[]{:S(2)}, u32[]{:S(2)}) collective-permute-start(bf16[1,128,768]{2,1,0:T(8,128)(2,1)} %get-tuple-element.44), channel_id=1, source_target_pairs={{0,176},{8,184},{16,128},{24,136},{32,144},{40,152},{48,160},{56,1... | collective-permute-start | bytes 589832 | tf_op jit(solution)/shard_map/ppermute | solution.py:327
  16.7 0.0 collective-permute-done.5.sib
  16.7 2.3 %collective-permute-start.4 = (bf16[1,128,768]{2,1,0:T(8,128)(2,1)}, bf16[1,128,768]{2,1,0:T(8,128)(2,1)S(1)}, u32[]{:S(2)}, u32[]{:S(2)}) collective-permute-start(bf16[1,128,768]{2,1,0:T(8,128)(2,1)} %get-tuple-element.45), channel_id=1, source_target_pairs={{0,240},{8,248},{16,192},{24,200},{32,208},{40,216},{48,224},{56,2... | collective-permute-start | bytes 589832 | tf_op jit(solution)/shard_map/ppermute | solution.py:327
  19.0 2.9 %plan.1 = s32[344]{0:T(512)} custom-call(s32[64,64]{1,0:T(8,128)} %table.3, s32[512]{0:T(512)} %valid.3, bf16[8,128,768]{2,1,0:T(8,128)(2,1)} %get-tuple-element.41.cols.after.refs_0_), custom_call_target="tpu_custom_call" | custom-call | bytes 65536 | tf_op jit(solution)/shard_map/plan/pallas_call | solution.py:408
  21.9 21.8 %local.1 = (bf16[16,512,768]{2,1,0:T(8,128)(2,1)}, f32[8,512]{1,0:T(8,128)}) custom-call(s32[512]{0:T(512)} %valid.3, bf16[8,512,768]{2,1,0:T(8,128)(2,1)} %bitcast.7, bf16[8,512,768]{2,1,0:T(8,128)(2,1)} %collective-permute-done.5.sib, bf16[8,128,768]{2,1,0:T(8,128)(2,1)} %get-tuple-element.41.cols.after.refs_0_), custom_call_target="tpu_custom_call" | custom-call | bytes 65536 | tf_op jit(solution)/shard_map/local/pallas_call | solution.py:418
  43.6 0.0 collective-permute-done.1
  43.6 0.0 collective-permute-done.2
  43.6 0.0 collective-permute-done.3
  43.7 2.3 %collective-permute-done.4 = bf16[1,128,768]{2,1,0:T(8,128)(2,1)S(1)} collective-permute-done((bf16[1,128,768]{2,1,0:T(8,128)(2,1)}, bf16[1,128,768]{2,1,0:T(8,128)(2,1)S(1)}, u32[]{:S(2)}, u32[]{:S(2)}) %collective-permute-start.4) | collective-permute-done | bytes 196640 | tf_op jit(solution)/shard_map/ppermute | solution.py:327
  46.0 0.0 collective-permute-done.refs_1_
  46.0 2.5 %collective-permute-start.6 = (bf16[8,128,768]{2,1,0:T(8,128)(2,1)S(1)}, bf16[8,128,768]{2,1,0:T(8,128)(2,1)S(1)}, u32[]{:S(2)}, u32[]{:S(2)}) collective-permute-start(bf16[8,128,768]{2,1,0:T(8,128)(2,1)S(1)} %collective-permute-done.refs_1_), channel_id=1, source_target_pairs={{0,8},{8,16},{16,24},{24,32},{32,40},{40,48},{48,56},{56,0},{64,72... | collective-permute-start | bytes 4718600 | tf_op jit(solution)/shard_map/ppermute | solution.py:327
  48.5 3.9 %pick_a.1 = (bf16[3,128,768]{2,1,0:T(8,128)(2,1)}, bf16[3,128,768]{2,1,0:T(8,128)(2,1)}, bf16[4,128,768]{2,1,0:T(8,128)(2,1)}, bf16[3,128,768]{2,1,0:T(8,128)(2,1)}) custom-call(s32[344]{0:T(512)} %plan.1, bf16[8,128,768]{2,1,0:T(8,128)(2,1)} %get-tuple-element.41.cols.after.refs_0_, bf16[8,128,768]{2,1,0:T(8,128)(2,1)} %copy-done.4), custom_call_target="tpu_custom_call" | custom-call | bytes 65536 | tf_op jit(solution)/shard_map/pick_a/pallas_call | solution.py:348
  52.4 0.0 copy-start.16
  52.4 0.0 copy-start.15
  52.4 3.0 %collective-permute-start.9 = (bf16[4,128,768]{2,1,0:T(8,128)(2,1)}, bf16[4,128,768]{2,1,0:T(8,128)(2,1)S(1)}, u32[]{:S(2)}, u32[]{:S(2)}) collective-permute-start(bf16[4,128,768]{2,1,0:T(8,128)(2,1)} %get-tuple-element.57), channel_id=1, source_target_pairs={{0,128},{8,136},{16,144},{24,152},{32,160},{40,168},{48,176},{56,1... | collective-permute-start | bytes 2359304 | tf_op jit(solution)/shard_map/ppermute | solution.py:327
  55.4 0.1 pad_maximum_fusion
  55.5 3.6 %collective-permute-start.7 = (bf16[4,128,768]{2,1,0:T(8,128)(2,1)S(1)}, bf16[4,128,768]{2,1,0:T(8,128)(2,1)S(1)}, u32[]{:S(2)}, u32[]{:S(2)}) collective-permute-start(bf16[4,128,768]{2,1,0:T(8,128)(2,1)S(1)} %pad_maximum_fusion), channel_id=1, source_target_pairs={{0,48},{8,56},{16,0},{24,8},{32,16},{40,24},{48,32},{56,40},{64,11... | collective-permute-start | bytes 2359304 | tf_op jit(solution)/shard_map/ppermute | solution.py:327
  59.1 1.8 %collective-permute-start.10 = (bf16[3,128,768]{2,1,0:T(8,128)(2,1)S(1)}, bf16[3,128,768]{2,1,0:T(8,128)(2,1)S(1)}, u32[]{:S(2)}, u32[]{:S(2)}) collective-permute-start(bf16[3,128,768]{2,1,0:T(8,128)(2,1)S(1)} %copy-done.16), channel_id=1, source_target_pairs={{0,192},{8,200},{16,208},{24,216},{32,224},{40,232},{48,240},{56,2... | collective-permute-start | bytes 1769480 | tf_op jit(solution)/shard_map/ppermute | solution.py:327
  61.0 0.2 collective-permute-start.8
  61.2 23.4 %collective-permute-done.10.refs_3_ = bf16[3,128,768]{2,1,0:T(8,128)(2,1)S(1)} collective-permute-done((bf16[3,128,768]{2,1,0:T(8,128)(2,1)S(1)}, bf16[3,128,768]{2,1,0:T(8,128)(2,1)S(1)}, u32[]{:S(2)}, u32[]{:S(2)}) %collective-permute-start.10) | collective-permute-done | bytes 589856 | tf_op jit(solution)/shard_map/ppermute | solution.py:327
  84.5 1.3 collective-permute-done.8.refs_1_
  85.8 0.0 collective-permute-done.9.refs_2_
  85.8 6.0 %collective-permute-done.7.refs_4_ = bf16[4,128,768]{2,1,0:T(8,128)(2,1)S(1)} collective-permute-done((bf16[4,128,768]{2,1,0:T(8,128)(2,1)S(1)}, bf16[4,128,768]{2,1,0:T(8,128)(2,1)S(1)}, u32[]{:S(2)}, u32[]{:S(2)}) %collective-permute-start.7) | collective-permute-done | bytes 786464 | tf_op jit(solution)/shard_map/ppermute | solution.py:327
  91.8 0.0 collective-permute-done.6.refs_1_
  91.8 1.2 copy-done.5
  93.0 4.3 %pick_b.1 = (bf16[2,128,768]{2,1,0:T(8,128)(2,1)}, bf16[2,128,768]{2,1,0:T(8,128)(2,1)}, bf16[2,128,768]{2,1,0:T(8,128)(2,1)}, bf16[1,128,768]{2,1,0:T(8,128)(2,1)}, bf16[4,2,128,768]{3,2,1,0:T(8,128)(2,1)}) custom-call(s32[344]{0:T(512)} %plan.1, bf16[8,128,768]{2,1,0:T(8,128)(2,1)} %get-tuple-element.41.cols.after.refs_0_, bf16[8,128,768]{2,1,0:T(8,128)(2,1)} %copy-done.5), custom_call_target="tpu_custom_call" | custom-call | bytes 65536 | tf_op jit(solution)/shard_map/pick_b/pallas_call | solution.py:348
  97.3 3.6 %all-to-all-start = ((bf16[4,2,128,768]{3,2,1,0:T(8,128)(2,1)}), bf16[4,2,128,768]{3,2,1,0:T(8,128)(2,1)S(1)}, u32[]{:S(2)}, u32[]{:S(2)}) async-start(bf16[4,2,128,768]{3,2,1,0:T(8,128)(2,1)} %get-tuple-element.73), calls=%async_computation | async-start | bytes 3145728 | tf_op jit(solution)/shard_map/all_to_all | solution.py:449
  100.9 2.0 %collective-permute-start.11 = (bf16[2,128,768]{2,1,0:T(8,128)(2,1)}, bf16[2,128,768]{2,1,0:T(8,128)(2,1)S(1)}, u32[]{:S(2)}, u32[]{:S(2)}) collective-permute-start(bf16[2,128,768]{2,1,0:T(8,128)(2,1)} %get-tuple-element.65.refs_5_), channel_id=1, source_target_pairs={{0,8},{8,16},{16,24},{24,32},{32,40},{40,48},{48,56},{56,0},{64,72... | collective-permute-start | bytes 1179656 | tf_op jit(solution)/shard_map/ppermute | solution.py:327
  102.8 1.2 collective-permute-start.12
  104.0 4.9 %collective-permute-start.13 = (bf16[2,128,768]{2,1,0:T(8,128)(2,1)}, bf16[2,128,768]{2,1,0:T(8,128)(2,1)S(1)}, u32[]{:S(2)}, u32[]{:S(2)}) collective-permute-start(bf16[2,128,768]{2,1,0:T(8,128)(2,1)} %get-tuple-element.71), channel_id=1, source_target_pairs={{0,200},{8,208},{16,216},{24,224},{32,232},{40,240},{48,248},{56,1... | collective-permute-start | bytes 1179656 | tf_op jit(solution)/shard_map/ppermute | solution.py:327
  108.9 1.5 collective-permute-start.14
  110.4 2.3 %collective-permute-start.15 = (bf16[1,128,768]{2,1,0:T(8,128)(2,1)S(1)}, bf16[1,128,768]{2,1,0:T(8,128)(2,1)S(1)}, u32[]{:S(2)}, u32[]{:S(2)}) collective-permute-start(bf16[1,128,768]{2,1,0:T(8,128)(2,1)S(1)} %slice.3), channel_id=1, source_target_pairs={{0,40},{8,48},{16,56},{24,0},{32,8},{40,16},{48,24},{56,32},{64,10... | collective-permute-start | bytes 589832 | tf_op jit(solution)/shard_map/ppermute | solution.py:327
  112.7 9.6 %pairs_a.1 = (f32[16,512]{1,0:T(8,128)}, f32[16,128]{1,0:T(8,128)}) custom-call(s32[344]{0:T(512)} %plan.1, bf16[16,512,768]{2,1,0:T(8,128)(2,1)} %get-tuple-element.49.own, bf16[3,128,768]{2,1,0:T(8,128)(2,1)} %get-tuple-element.59.refs_0_, bf16[3,128,768]{2,1,0:T(8,128)(2,1)} %copy-done.9, bf16[4,128,768]{2,1,0:T(8,128)(2,1)} %copy-done.6, ...), custom_call_target="tpu_custom_call" | custom-call | bytes 65536 | tf_op jit(solution)/shard_map/pairs_a/pallas_call | solution.py:368
  122.2 0.0 collective-permute-done.11.refs_0_
  122.3 3.4 %collective-permute-done.12.refs_1_ = bf16[2,128,768]{2,1,0:T(8,128)(2,1)S(1)} collective-permute-done((bf16[2,128,768]{2,1,0:T(8,128)(2,1)}, bf16[2,128,768]{2,1,0:T(8,128)(2,1)S(1)}, u32[]{:S(2)}, u32[]{:S(2)}) %collective-permute-start.12) | collective-permute-done | bytes 393248 | tf_op jit(solution)/shard_map/ppermute | solution.py:327
  125.7 0.7 copy-done.11
  126.5 4.7 %pairs_b.1 = (f32[16,512]{1,0:T(8,128)}, f32[4,128]{1,0:T(4,128)}) custom-call(s32[344]{0:T(512)} %plan.1, bf16[16,512,768]{2,1,0:T(8,128)(2,1)} %get-tuple-element.49.own, bf16[2,128,768]{2,1,0:T(8,128)(2,1)} %copy-done.10, bf16[2,128,768]{2,1,0:T(8,128)(2,1)} %copy-done.11, f32[16,512]{1,0:T(8,128)} %get-tuple-element.66.refs_2_.refs_0_), custom_call_target="tpu_custom_call" | custom-call | bytes 65536 | tf_op jit(solution)/shard_map/pairs_b/pallas_call | solution.py:368
  131.1 4.9 %collective-permute-done.14.refs_5_ = bf16[1,128,768]{2,1,0:T(8,128)(2,1)S(1)} collective-permute-done((bf16[1,128,768]{2,1,0:T(8,128)(2,1)}, bf16[1,128,768]{2,1,0:T(8,128)(2,1)S(1)}, u32[]{:S(2)}, u32[]{:S(2)}) %collective-permute-start.14) | collective-permute-done | bytes 196640 | tf_op jit(solution)/shard_map/ppermute | solution.py:327
  136.1 0.0 collective-permute-done.15.refs_6_
  136.1 0.7 copy-done.13
  136.7 0.7 copy-done.14
  137.4 0.0 collective-permute-done.13.refs_4_
  137.4 0.0 all-to-all-done.refs_7_
  137.4 0.7 copy-done.12
  138.2 0.5 copy-done.3
  138.7 7.7 %pairs_c.1 = (f32[16,512]{1,0:T(8,128)}, f32[64,128]{1,0:T(8,128)}, f32[8,512]{1,0:T(8,128)}) custom-call(s32[344]{0:T(512)} %plan.1, bf16[16,512,768]{2,1,0:T(8,128)(2,1)} %get-tuple-element.49.own, f32[16,512]{1,0:T(8,128)} %get-tuple-element.66.refs_2_.refs_0_, f32[16,128]{1,0:T(8,128)} %get-tuple-element.67.refs_1_, ...), custom_call_target="tpu_custom_call" | custom-call | bytes 65536 | tf_op jit(solution)/shard_map/pairs_c/pallas_call | solution.py:368
  146.4 7.2 %all-to-all-start.1 = ((f32[32,2,128]{2,1,0:T(2,128)}), f32[32,2,128]{2,1,0:T(2,128)S(1)}, u32[]{:S(2)}, u32[]{:S(2)}) async-start(f32[32,2,128]{2,1,0:T(2,128)} %bitcast.8), calls=%async_computation.1 | async-start | bytes 65536 | tf_op jit(solution)/shard_map/all_to_all | solution.py:478
  153.6 0.1 collective-permute-start.16
  153.7 1.4 collective-permute-done.16.sib_rows
  155.1 0.8 copy-done.1
  155.8 7.6 %all-to-all-done.1 = f32[32,2,128]{2,1,0:T(2,128)S(1)} async-done(((f32[32,2,128]{2,1,0:T(2,128)}), f32[32,2,128]{2,1,0:T(2,128)S(1)}, u32[]{:S(2)}, u32[]{:S(2)}) %all-to-all-start.1) | async-done | bytes 32800 | tf_op jit(solution)/shard_map/all_to_all | solution.py:478
  163.5 0.7 merge.1.one
  164.2 0.3 collective-permute-start.17
  164.5 2.6 %collective-permute-start.18 = (f32[8,512]{1,0:T(8,128)S(1)}, f32[8,512]{1,0:T(8,128)S(1)}, u32[]{:S(2)}, u32[]{:S(2)}) collective-permute-start(f32[8,512]{1,0:T(8,128)S(1)} %merge.1.one), channel_id=1, source_target_pairs={{0,2},{1,3},{2,0},{3,1},{4,6},{5,7},{6,4},{7,5},{8,10},{9,11},{10,... | collective-permute-start | bytes 49160 | tf_op jit(solution)/shard_map/ppermute | solution.py:499
  167.1 0.0 collective-permute-start.19
  167.1 0.9 collective-permute-done.17.two
  168.0 1.7 %collective-permute-done.18.three = f32[8,512]{1,0:T(8,128)S(1)} collective-permute-done((f32[8,512]{1,0:T(8,128)S(1)}, f32[8,512]{1,0:T(8,128)S(1)}, u32[]{:S(2)}, u32[]{:S(2)}) %collective-permute-start.18) | collective-permute-done | bytes 16416 | tf_op jit(solution)/shard_map/ppermute | solution.py:499
  169.8 2.3 %collective-permute-done.19.four = f32[8,512]{1,0:T(8,128)S(1)} collective-permute-done((f32[8,512]{1,0:T(8,128)S(1)}, f32[8,512]{1,0:T(8,128)S(1)}, u32[]{:S(2)}, u32[]{:S(2)}) %collective-permute-start.19) | collective-permute-done | bytes 16416 | tf_op jit(solution)/shard_map/ppermute | solution.py:499
  172.1 0.6 finish.1
  (27 shorter events, 0.1 us)
Async XLA Ops:
  0.0 16.7 %collective-permute-start.5 = (bf16[8,512,768]{2,1,0:T(8,128)(2,1)}, bf16[8,512,768]{2,1,0:T(8,128)(2,1)}, u32[]{:S(2)}, u32[]{:S(2)}) collective-permute-start(bf16[8,512,768]{2,1,0:T(8,128)(2,1)} %bitcast.5), channel_id=1, source_target_pairs={{0,4},{4,0},{1,5},{5,1},{2,6},{6,2},{3,7},{7,3},{8,12},{12,8},{9,1... | collective-permute-start | bytes 18874376 | tf_op jit(solution)/shard_map/ppermute | solution.py:405
  4.2 41.7 %collective-permute-start = (bf16[8,128,768]{2,1,0:T(8,128)(2,1)}, bf16[8,128,768]{2,1,0:T(8,128)(2,1)S(1)}, u32[]{:S(2)}, u32[]{:S(2)}) collective-permute-start(bf16[8,128,768]{2,1,0:T(8,128)(2,1)} %get-tuple-element.41.cols.after.refs_0_), channel_id=1, source_target_pairs={{0,8},{8,16},{16,24},{24,32},{32,40},{40,48},{48,56},{56,0},{64,72... | collective-permute-start | bytes 4718600 | tf_op jit(solution)/shard_map/ppermute | solution.py:327
  6.2 37.4 %collective-permute-start.1 = (bf16[1,128,768]{2,1,0:T(8,128)(2,1)}, bf16[1,128,768]{2,1,0:T(8,128)(2,1)S(1)}, u32[]{:S(2)}, u32[]{:S(2)}) collective-permute-start(bf16[1,128,768]{2,1,0:T(8,128)(2,1)} %get-tuple-element.42), channel_id=1, source_target_pairs={{0,48},{8,56},{16,0},{24,8},{32,16},{40,24},{48,32},{56,40},{64,11... | collective-permute-start | bytes 589832 | tf_op jit(solution)/shard_map/ppermute | solution.py:327
  11.6 32.0 %collective-permute-start.2 = (bf16[1,128,768]{2,1,0:T(8,128)(2,1)}, bf16[1,128,768]{2,1,0:T(8,128)(2,1)S(1)}, u32[]{:S(2)}, u32[]{:S(2)}) collective-permute-start(bf16[1,128,768]{2,1,0:T(8,128)(2,1)} %get-tuple-element.43), channel_id=1, source_target_pairs={{0,112},{8,120},{16,64},{24,72},{32,80},{40,88},{48,96},{56,104},{... | collective-permute-start | bytes 589832 | tf_op jit(solution)/shard_map/ppermute | solution.py:327
  14.0 29.6 %collective-permute-start.3 = (bf16[1,128,768]{2,1,0:T(8,128)(2,1)}, bf16[1,128,768]{2,1,0:T(8,128)(2,1)S(1)}, u32[]{:S(2)}, u32[]{:S(2)}) collective-permute-start(bf16[1,128,768]{2,1,0:T(8,128)(2,1)} %get-tuple-element.44), channel_id=1, source_target_pairs={{0,176},{8,184},{16,128},{24,136},{32,144},{40,152},{48,160},{56,1... | collective-permute-start | bytes 589832 | tf_op jit(solution)/shard_map/ppermute | solution.py:327
  16.7 29.2 %collective-permute-start.4 = (bf16[1,128,768]{2,1,0:T(8,128)(2,1)}, bf16[1,128,768]{2,1,0:T(8,128)(2,1)S(1)}, u32[]{:S(2)}, u32[]{:S(2)}) collective-permute-start(bf16[1,128,768]{2,1,0:T(8,128)(2,1)} %get-tuple-element.45), channel_id=1, source_target_pairs={{0,240},{8,248},{16,192},{24,200},{32,208},{40,216},{48,224},{56,2... | collective-permute-start | bytes 589832 | tf_op jit(solution)/shard_map/ppermute | solution.py:327
  46.0 2.5 %copy-start.4 = (bf16[8,128,768]{2,1,0:T(8,128)(2,1)}, bf16[8,128,768]{2,1,0:T(8,128)(2,1)S(1)}, u32[]{:S(2)}) copy-start(bf16[8,128,768]{2,1,0:T(8,128)(2,1)S(1)} %collective-permute-done.refs_1_) | copy-start | bytes 4718596
  46.0 45.8 %collective-permute-start.6 = (bf16[8,128,768]{2,1,0:T(8,128)(2,1)S(1)}, bf16[8,128,768]{2,1,0:T(8,128)(2,1)S(1)}, u32[]{:S(2)}, u32[]{:S(2)}) collective-permute-start(bf16[8,128,768]{2,1,0:T(8,128)(2,1)S(1)} %collective-permute-done.refs_1_), channel_id=1, source_target_pairs={{0,8},{8,16},{16,24},{24,32},{32,40},{40,48},{48,56},{56,0},{64,72... | collective-permute-start | bytes 4718600 | tf_op jit(solution)/shard_map/ppermute | solution.py:327
  52.4 6.7 %copy-start.16 = (bf16[3,128,768]{2,1,0:T(8,128)(2,1)S(1)}, bf16[3,128,768]{2,1,0:T(8,128)(2,1)}, u32[]{:S(2)}) copy-start(bf16[3,128,768]{2,1,0:T(8,128)(2,1)} %get-tuple-element.58) | copy-start | bytes 1769476
  52.4 8.5 %copy-start.15 = (bf16[3,128,768]{2,1,0:T(8,128)(2,1)S(1)}, bf16[3,128,768]{2,1,0:T(8,128)(2,1)}, u32[]{:S(2)}) copy-start(bf16[3,128,768]{2,1,0:T(8,128)(2,1)} %get-tuple-element.56) | copy-start | bytes 1769476
  52.4 33.4 %collective-permute-start.9 = (bf16[4,128,768]{2,1,0:T(8,128)(2,1)}, bf16[4,128,768]{2,1,0:T(8,128)(2,1)S(1)}, u32[]{:S(2)}, u32[]{:S(2)}) collective-permute-start(bf16[4,128,768]{2,1,0:T(8,128)(2,1)} %get-tuple-element.57), channel_id=1, source_target_pairs={{0,128},{8,136},{16,144},{24,152},{32,160},{40,168},{48,176},{56,1... | collective-permute-start | bytes 2359304 | tf_op jit(solution)/shard_map/ppermute | solution.py:327
  55.5 36.2 %collective-permute-start.7 = (bf16[4,128,768]{2,1,0:T(8,128)(2,1)S(1)}, bf16[4,128,768]{2,1,0:T(8,128)(2,1)S(1)}, u32[]{:S(2)}, u32[]{:S(2)}) collective-permute-start(bf16[4,128,768]{2,1,0:T(8,128)(2,1)S(1)} %pad_maximum_fusion), channel_id=1, source_target_pairs={{0,48},{8,56},{16,0},{24,8},{32,16},{40,24},{48,32},{56,40},{64,11... | collective-permute-start | bytes 2359304 | tf_op jit(solution)/shard_map/ppermute | solution.py:327
  59.1 25.4 %collective-permute-start.10 = (bf16[3,128,768]{2,1,0:T(8,128)(2,1)S(1)}, bf16[3,128,768]{2,1,0:T(8,128)(2,1)S(1)}, u32[]{:S(2)}, u32[]{:S(2)}) collective-permute-start(bf16[3,128,768]{2,1,0:T(8,128)(2,1)S(1)} %copy-done.16), channel_id=1, source_target_pairs={{0,192},{8,200},{16,208},{24,216},{32,224},{40,232},{48,240},{56,2... | collective-permute-start | bytes 1769480 | tf_op jit(solution)/shard_map/ppermute | solution.py:327
  61.0 24.8 %collective-permute-start.8 = (bf16[3,128,768]{2,1,0:T(8,128)(2,1)S(1)}, bf16[3,128,768]{2,1,0:T(8,128)(2,1)S(1)}, u32[]{:S(2)}, u32[]{:S(2)}) collective-permute-start(bf16[3,128,768]{2,1,0:T(8,128)(2,1)S(1)} %copy-done.15), channel_id=1, source_target_pairs={{0,64},{8,72},{16,80},{24,88},{32,96},{40,104},{48,112},{56,120},{... | collective-permute-start | bytes 1769480 | tf_op jit(solution)/shard_map/ppermute | solution.py:327
  84.5 12.7 %copy-start.8 = (bf16[3,128,768]{2,1,0:T(8,128)(2,1)}, bf16[3,128,768]{2,1,0:T(8,128)(2,1)S(1)}, u32[]{:S(2)}) copy-start(bf16[3,128,768]{2,1,0:T(8,128)(2,1)S(1)} %collective-permute-done.10.refs_3_) | copy-start | bytes 1769476
  85.8 11.5 %copy-start.9 = (bf16[3,128,768]{2,1,0:T(8,128)(2,1)}, bf16[3,128,768]{2,1,0:T(8,128)(2,1)S(1)}, u32[]{:S(2)}) copy-start(bf16[3,128,768]{2,1,0:T(8,128)(2,1)S(1)} %collective-permute-done.8.refs_1_) | copy-start | bytes 1769476
  85.8 26.9 %copy-start.6 = (bf16[4,128,768]{2,1,0:T(8,128)(2,1)}, bf16[4,128,768]{2,1,0:T(8,128)(2,1)S(1)}, u32[]{:S(2)}) copy-start(bf16[4,128,768]{2,1,0:T(8,128)(2,1)S(1)} %collective-permute-done.9.refs_2_) | copy-start | bytes 2359300
  91.8 20.9 %copy-start.7 = (bf16[4,128,768]{2,1,0:T(8,128)(2,1)}, bf16[4,128,768]{2,1,0:T(8,128)(2,1)S(1)}, u32[]{:S(2)}) copy-start(bf16[4,128,768]{2,1,0:T(8,128)(2,1)S(1)} %collective-permute-done.7.refs_4_) | copy-start | bytes 2359300
  91.8 1.2 copy-start.5
  97.3 40.1 %all-to-all-start = ((bf16[4,2,128,768]{3,2,1,0:T(8,128)(2,1)}), bf16[4,2,128,768]{3,2,1,0:T(8,128)(2,1)S(1)}, u32[]{:S(2)}, u32[]{:S(2)}) async-start(bf16[4,2,128,768]{3,2,1,0:T(8,128)(2,1)} %get-tuple-element.73), calls=%async_computation | async-start | bytes 3145728 | tf_op jit(solution)/shard_map/all_to_all | solution.py:449
  100.9 21.4 %collective-permute-start.11 = (bf16[2,128,768]{2,1,0:T(8,128)(2,1)}, bf16[2,128,768]{2,1,0:T(8,128)(2,1)S(1)}, u32[]{:S(2)}, u32[]{:S(2)}) collective-permute-start(bf16[2,128,768]{2,1,0:T(8,128)(2,1)} %get-tuple-element.65.refs_5_), channel_id=1, source_target_pairs={{0,8},{8,16},{16,24},{24,32},{32,40},{40,48},{48,56},{56,0},{64,72... | collective-permute-start | bytes 1179656 | tf_op jit(solution)/shard_map/ppermute | solution.py:327
  102.8 22.9 %collective-permute-start.12 = (bf16[2,128,768]{2,1,0:T(8,128)(2,1)}, bf16[2,128,768]{2,1,0:T(8,128)(2,1)S(1)}, u32[]{:S(2)}, u32[]{:S(2)}) collective-permute-start(bf16[2,128,768]{2,1,0:T(8,128)(2,1)} %get-tuple-element.68), channel_id=1, source_target_pairs={{0,72},{8,80},{16,88},{24,96},{32,104},{40,112},{48,120},{56,64},{... | collective-permute-start | bytes 1179656 | tf_op jit(solution)/shard_map/ppermute | solution.py:327
  104.0 33.4 %collective-permute-start.13 = (bf16[2,128,768]{2,1,0:T(8,128)(2,1)}, bf16[2,128,768]{2,1,0:T(8,128)(2,1)S(1)}, u32[]{:S(2)}, u32[]{:S(2)}) collective-permute-start(bf16[2,128,768]{2,1,0:T(8,128)(2,1)} %get-tuple-element.71), channel_id=1, source_target_pairs={{0,200},{8,208},{16,216},{24,224},{32,232},{40,240},{48,248},{56,1... | collective-permute-start | bytes 1179656 | tf_op jit(solution)/shard_map/ppermute | solution.py:327
  108.9 27.2 %collective-permute-start.14 = (bf16[1,128,768]{2,1,0:T(8,128)(2,1)}, bf16[1,128,768]{2,1,0:T(8,128)(2,1)S(1)}, u32[]{:S(2)}, u32[]{:S(2)}) collective-permute-start(bf16[1,128,768]{2,1,0:T(8,128)(2,1)} %get-tuple-element.72), channel_id=1, source_target_pairs={{0,136},{8,144},{16,152},{24,160},{32,168},{40,176},{48,184},{56,1... | collective-permute-start | bytes 589832 | tf_op jit(solution)/shard_map/ppermute | solution.py:327
  110.4 25.7 %collective-permute-start.15 = (bf16[1,128,768]{2,1,0:T(8,128)(2,1)S(1)}, bf16[1,128,768]{2,1,0:T(8,128)(2,1)S(1)}, u32[]{:S(2)}, u32[]{:S(2)}) collective-permute-start(bf16[1,128,768]{2,1,0:T(8,128)(2,1)S(1)} %slice.3), channel_id=1, source_target_pairs={{0,40},{8,48},{16,56},{24,0},{32,8},{40,16},{48,24},{56,32},{64,10... | collective-permute-start | bytes 589832 | tf_op jit(solution)/shard_map/ppermute | solution.py:327
  122.3 3.5 %copy-start.10 = (bf16[2,128,768]{2,1,0:T(8,128)(2,1)}, bf16[2,128,768]{2,1,0:T(8,128)(2,1)S(1)}, u32[]{:S(2)}) copy-start(bf16[2,128,768]{2,1,0:T(8,128)(2,1)S(1)} %collective-permute-done.11.refs_0_) | copy-start | bytes 1179652
  125.7 0.7 copy-start.11
  136.1 0.7 copy-start.13
  136.7 0.7 copy-start.14
  137.4 0.7 copy-start.12
  137.4 1.3 copy-start.3
  138.7 16.4 %copy-start.2 = (f32[8,512]{1,0:T(8,128)S(1)}, f32[8,512]{1,0:T(8,128)}, u32[]{:S(2)}) copy-start(f32[8,512]{1,0:T(8,128)} %get-tuple-element.48.local) | copy-start | bytes 49156
  138.7 24.8 %copy-start = (s32[344]{0:T(512)S(1)}, s32[344]{0:T(512)}, u32[]{:S(2)}) copy-start(s32[344]{0:T(512)} %plan.1) | copy-start | bytes 4132
  146.4 17.1 %all-to-all-start.1 = ((f32[32,2,128]{2,1,0:T(2,128)}), f32[32,2,128]{2,1,0:T(2,128)S(1)}, u32[]{:S(2)}, u32[]{:S(2)}) async-start(f32[32,2,128]{2,1,0:T(2,128)} %bitcast.8), calls=%async_computation.1 | async-start | bytes 65536 | tf_op jit(solution)/shard_map/all_to_all | solution.py:478
  153.6 1.5 collective-permute-start.16
  155.1 0.8 copy-start.1
  164.2 3.8 %collective-permute-start.17 = (f32[8,512]{1,0:T(8,128)S(1)}, f32[8,512]{1,0:T(8,128)S(1)}, u32[]{:S(2)}, u32[]{:S(2)}) collective-permute-start(f32[8,512]{1,0:T(8,128)S(1)} %merge.1.one), channel_id=1, source_target_pairs={{0,1},{1,2},{2,3},{3,0},{4,5},{5,6},{6,7},{7,4},{8,9},{9,10},{10,1... | collective-permute-start | bytes 49160 | tf_op jit(solution)/shard_map/ppermute | solution.py:499
  164.5 5.2 %collective-permute-start.18 = (f32[8,512]{1,0:T(8,128)S(1)}, f32[8,512]{1,0:T(8,128)S(1)}, u32[]{:S(2)}, u32[]{:S(2)}) collective-permute-start(f32[8,512]{1,0:T(8,128)S(1)} %merge.1.one), channel_id=1, source_target_pairs={{0,2},{1,3},{2,0},{3,1},{4,6},{5,7},{6,4},{7,5},{8,10},{9,11},{10,... | collective-permute-start | bytes 49160 | tf_op jit(solution)/shard_map/ppermute | solution.py:499
  167.1 4.9 %collective-permute-start.19 = (f32[8,512]{1,0:T(8,128)S(1)}, f32[8,512]{1,0:T(8,128)S(1)}, u32[]{:S(2)}, u32[]{:S(2)}) collective-permute-start(f32[8,512]{1,0:T(8,128)S(1)} %merge.1.one), channel_id=1, source_target_pairs={{0,3},{1,0},{2,1},{3,2},{4,7},{5,4},{6,5},{7,6},{8,11},{9,8},{10,9... | collective-permute-start | bytes 49160 | tf_op jit(solution)/shard_map/ppermute | solution.py:499

commit v7 on v5

--- a/solution.py
+++ b/solution.py
@@ -55,7 +55,7 @@
 third = [[(dx, 3, 2, 0), (dx, 3, 2, 1)] for dx in (0, 1, 3)]
 far = [(dx, 4, 1, 0) for dx in range(n_x)]
 down = [(2, 5, 2, 0), (2, 5, 2, 1)]
-stages = [sum(first, []) + far, third[0] + third[1], third[2] + down + sum(second, [])]
+stages = [sum(first, []) + far, down + third[0] + third[1], third[2] + sum(second, [])]
 every = sum(stages, [])
 gone_of = {0: 0, 1: 1, 2: 2, 3: 2}
 at_pick, at_back, at_back_row, at_row, at_own = 0, 32, 64, 96, 128
@@ -441,10 +441,10 @@
     picked = pick(numbers(first), False, [cols, hop1], [], "pick_a")
     first_in = [move(a, dx, 0) for dx, a in enumerate(picked)]
     hop2, away, around, *first_in = lax.optimization_barrier((hop2, away, around, *first_in))
+    down_in = move(around, 2, -3)
     picked = pick(numbers(third + second), True, [cols, hop2], [], "pick_b")
     third_in = [move(a, slots[0][0], 1) for slots, a in zip(third, picked)]
     second_in = lax.all_to_all(picked[-1], "x", split_axis=0, concat_axis=0, tiled=True)
-    down_in = move(around, 2, -3)
 
     past_a = compare(
         0,
@@ -456,16 +456,16 @@
     )
     past_b = compare(
         1,
-        [(0, None, 2, 0), (1, None, 2, 2)],
-        third_in[:2],
+        [(0, None, 2, 0), (1, None, 2, 2), (2, None, 2, 4)],
+        [down_in] + third_in[:2],
         [],
         [past_a[0]],
         "pairs_b",
     )
     row_best, col_best, sib_best = compare(
         2,
-        [(0, None, 2, 0), (1, None, 2, 2)] + [(2, dx, 2, 4 + 2 * dx) for dx in range(n_x)],
-        [third_in[2], down_in, second_in],
+        [(0, None, 2, 0)] + [(1, dx, 2, 2 + 2 * dx) for dx in range(n_x)],
+        [third_in[2], second_in],
         [*past_a, *past_b],
         [],
         "pairs_c",

time: 170 us -> 174 us (1.024)
  waiting for transfers between devices: 52.7 us -> 54.9 us
    ppermute x14, waiting for transfers between devices: 38.7 us -> 41 us  [move(): return lax.ppermute(value, ('x', 'z'), steps)]
  transfers between devices with their start and end apart: 21 -> 21, of which waited for: 12 -> 10; matrix products, arithmetic and copies ran while one was open for 0% -> 0% of each run, Pallas kernels for 27% -> 28%
where the time goes in v7:
time: 174 us; the launch traced here: 172 us
  Pallas kernels  62 us (36%)
  waiting for transfers between devices  54.9 us (32%)
  starting transfers between devices  51.2 us (29%)
  local copies, waits for them, and re-layouts  3.9 us (2%)
    ppermute x14, waiting for transfers between devices, move(): return lax.ppermute(value, ('x', 'z'), steps)  41 us
    ppermute x14, starting transfers between devices, move(): return lax.ppermute(value, ('x', 'z'), steps)  35.6 us
    pallas_call x3, Pallas kernels, compare(): pl.pallas_call(functools.partial(pair_kernel, stage, feeds), out_shape=[j...  23.6 us
    pallas_call x1, Pallas kernels, on_device(): pl.pallas_call(local_kernel, grid=(2 * blocks,), out_shape=(jax.ShapeDtyp...  21.8 us
    all_to_all x1, starting transfers between devices, on_device(): lax.all_to_all(col_best, ('x', 'z'), split_axis=0, concat_axis=0, tiled=T...  9.06 us
    pallas_call x2, Pallas kernels, pick(): pl.pallas_call(functools.partial(pick_kernel, wanted, spread), out_shape=...  8.16 us
    all_to_all x1, waiting for transfers between devices, on_device(): lax.all_to_all(col_best, ('x', 'z'), split_axis=0, concat_axis=0, tiled=T...  7.59 us
    ppermute x3, waiting for transfers between devices, on_device(): lax.ppermute(combined, 'rep', [(y, (y + d) % n_rep) for y in range(n_rep)])  4.95 us
  transfers between devices with their start and end apart: 21, of which 10 were waited for; matrix products, arithmetic and copies ran while one was open for 0% of the time, Pallas kernels for 28%

profile of v7, /device:TPU:24, one launch (start us, length us, event | category | flops | bytes accessed | tf_op | source)
XLA Modules:
  0.0 172.4 jit_solution(586188058762148442)
XLA Ops:
  0.0 0.0 collective-permute-start.5
  0.0 4.4 %prep.1 = (bf16[8,128,768]{2,1,0:T(8,128)(2,1)}, bf16[1,128,768]{2,1,0:T(8,128)(2,1)}, bf16[1,128,768]{2,1,0:T(8,128)(2,1)}, bf16[1,128,768]{2,1,0:T(8,128)(2,1)...) custom-call(s32[64,64]{1,0:T(8,128)} %table.3, bf16[8,512,768]{2,1,0:T(8,128)(2,1)} %bitcast.6), custom_call_target="tpu_custom_call" | custom-call | bytes 65536 | tf_op jit(solution)/shard_map/prep/pallas_call | solution.py:386
  4.4 2.0 %collective-permute-start = (bf16[8,128,768]{2,1,0:T(8,128)(2,1)}, bf16[8,128,768]{2,1,0:T(8,128)(2,1)S(1)}, u32[]{:S(2)}, u32[]{:S(2)}) collective-permute-start(bf16[8,128,768]{2,1,0:T(8,128)(2,1)} %get-tuple-element.42.cols.after.refs_0_), channel_id=1, source_target_pairs={{0,8},{8,16},{16,24},{24,32},{32,40},{40,48},{48,56},{56,0},{64,72... | collective-permute-start | bytes 4718600 | tf_op jit(solution)/shard_map/ppermute | solution.py:325
  6.4 5.4 %collective-permute-start.1 = (bf16[1,128,768]{2,1,0:T(8,128)(2,1)}, bf16[1,128,768]{2,1,0:T(8,128)(2,1)S(1)}, u32[]{:S(2)}, u32[]{:S(2)}) collective-permute-start(bf16[1,128,768]{2,1,0:T(8,128)(2,1)} %get-tuple-element.43), channel_id=1, source_target_pairs={{0,48},{8,56},{16,0},{24,8},{32,16},{40,24},{48,32},{56,40},{64,11... | collective-permute-start | bytes 589832 | tf_op jit(solution)/shard_map/ppermute | solution.py:325
  11.8 2.4 %collective-permute-start.2 = (bf16[1,128,768]{2,1,0:T(8,128)(2,1)}, bf16[1,128,768]{2,1,0:T(8,128)(2,1)S(1)}, u32[]{:S(2)}, u32[]{:S(2)}) collective-permute-start(bf16[1,128,768]{2,1,0:T(8,128)(2,1)} %get-tuple-element.44), channel_id=1, source_target_pairs={{0,112},{8,120},{16,64},{24,72},{32,80},{40,88},{48,96},{56,104},{... | collective-permute-start | bytes 589832 | tf_op jit(solution)/shard_map/ppermute | solution.py:325
  14.1 2.7 %collective-permute-start.3 = (bf16[1,128,768]{2,1,0:T(8,128)(2,1)}, bf16[1,128,768]{2,1,0:T(8,128)(2,1)S(1)}, u32[]{:S(2)}, u32[]{:S(2)}) collective-permute-start(bf16[1,128,768]{2,1,0:T(8,128)(2,1)} %get-tuple-element.45), channel_id=1, source_target_pairs={{0,176},{8,184},{16,128},{24,136},{32,144},{40,152},{48,160},{56,1... | collective-permute-start | bytes 589832 | tf_op jit(solution)/shard_map/ppermute | solution.py:325
  16.9 0.0 collective-permute-done.5.sib
  16.9 2.1 %collective-permute-start.4 = (bf16[1,128,768]{2,1,0:T(8,128)(2,1)}, bf16[1,128,768]{2,1,0:T(8,128)(2,1)S(1)}, u32[]{:S(2)}, u32[]{:S(2)}) collective-permute-start(bf16[1,128,768]{2,1,0:T(8,128)(2,1)} %get-tuple-element.46), channel_id=1, source_target_pairs={{0,240},{8,248},{16,192},{24,200},{32,208},{40,216},{48,224},{56,2... | collective-permute-start | bytes 589832 | tf_op jit(solution)/shard_map/ppermute | solution.py:325
  19.0 2.8 %plan.1 = s32[344]{0:T(512)} custom-call(s32[64,64]{1,0:T(8,128)} %table.3, s32[512]{0:T(512)} %valid.3, bf16[8,128,768]{2,1,0:T(8,128)(2,1)} %get-tuple-element.42.cols.after.refs_0_), custom_call_target="tpu_custom_call" | custom-call | bytes 65536 | tf_op jit(solution)/shard_map/plan/pallas_call | solution.py:407
  21.8 21.8 %local.1 = (bf16[16,512,768]{2,1,0:T(8,128)(2,1)}, f32[8,512]{1,0:T(8,128)}) custom-call(s32[512]{0:T(512)} %valid.3, bf16[8,512,768]{2,1,0:T(8,128)(2,1)} %bitcast.7, bf16[8,512,768]{2,1,0:T(8,128)(2,1)} %collective-permute-done.5.sib, bf16[8,128,768]{2,1,0:T(8,128)(2,1)} %get-tuple-element.42.cols.after.refs_0_), custom_call_target="tpu_custom_call" | custom-call | bytes 65536 | tf_op jit(solution)/shard_map/local/pallas_call | solution.py:417
  43.6 0.0 collective-permute-done.1
  43.6 0.0 collective-permute-done.2
  43.6 0.0 collective-permute-done.3
  43.6 2.5 %collective-permute-done.4 = bf16[1,128,768]{2,1,0:T(8,128)(2,1)S(1)} collective-permute-done((bf16[1,128,768]{2,1,0:T(8,128)(2,1)}, bf16[1,128,768]{2,1,0:T(8,128)(2,1)S(1)}, u32[]{:S(2)}, u32[]{:S(2)}) %collective-permute-start.4) | collective-permute-done | bytes 196640 | tf_op jit(solution)/shard_map/ppermute | solution.py:325
  46.1 0.0 collective-permute-done.refs_1_
  46.1 2.5 %collective-permute-start.6 = (bf16[8,128,768]{2,1,0:T(8,128)(2,1)S(1)}, bf16[8,128,768]{2,1,0:T(8,128)(2,1)S(1)}, u32[]{:S(2)}, u32[]{:S(2)}) collective-permute-start(bf16[8,128,768]{2,1,0:T(8,128)(2,1)S(1)} %collective-permute-done.refs_1_), channel_id=1, source_target_pairs={{0,8},{8,16},{16,24},{24,32},{32,40},{40,48},{48,56},{56,0},{64,72... | collective-permute-start | bytes 4718600 | tf_op jit(solution)/shard_map/ppermute | solution.py:325
  48.6 0.1 pad_maximum_fusion
  48.7 3.0 %collective-permute-start.7 = (bf16[4,128,768]{2,1,0:T(8,128)(2,1)S(1)}, bf16[4,128,768]{2,1,0:T(8,128)(2,1)S(1)}, u32[]{:S(2)}, u32[]{:S(2)}) collective-permute-start(bf16[4,128,768]{2,1,0:T(8,128)(2,1)S(1)} %pad_maximum_fusion), channel_id=1, source_target_pairs={{0,48},{8,56},{16,0},{24,8},{32,16},{40,24},{48,32},{56,40},{64,11... | collective-permute-start | bytes 2359304 | tf_op jit(solution)/shard_map/ppermute | solution.py:325
  51.7 0.0 copy-done.4
  51.7 3.9 %pick_a.1 = (bf16[3,128,768]{2,1,0:T(8,128)(2,1)}, bf16[3,128,768]{2,1,0:T(8,128)(2,1)}, bf16[3,128,768]{2,1,0:T(8,128)(2,1)}, bf16[3,128,768]{2,1,0:T(8,128)(2,1)}) custom-call(s32[344]{0:T(512)} %plan.1, bf16[8,128,768]{2,1,0:T(8,128)(2,1)} %get-tuple-element.42.cols.after.refs_0_, bf16[8,128,768]{2,1,0:T(8,128)(2,1)} %copy-done.4), custom_call_target="tpu_custom_call" | custom-call | bytes 65536 | tf_op jit(solution)/shard_map/pick_a/pallas_call | solution.py:346
  55.6 1.6 collective-permute-start.10
  57.2 0.5 collective-permute-start.8
  57.7 2.8 %collective-permute-start.9 = (bf16[3,128,768]{2,1,0:T(8,128)(2,1)}, bf16[3,128,768]{2,1,0:T(8,128)(2,1)S(1)}, u32[]{:S(2)}, u32[]{:S(2)}) collective-permute-start(bf16[3,128,768]{2,1,0:T(8,128)(2,1)} %get-tuple-element.59), channel_id=1, source_target_pairs={{0,128},{8,136},{16,144},{24,152},{32,160},{40,168},{48,176},{56,1... | collective-permute-start | bytes 1769480 | tf_op jit(solution)/shard_map/ppermute | solution.py:325
  60.5 22.0 %collective-permute-done.10.refs_3_ = bf16[3,128,768]{2,1,0:T(8,128)(2,1)S(1)} collective-permute-done((bf16[3,128,768]{2,1,0:T(8,128)(2,1)}, bf16[3,128,768]{2,1,0:T(8,128)(2,1)S(1)}, u32[]{:S(2)}, u32[]{:S(2)}) %collective-permute-start.10) | collective-permute-done | bytes 589856 | tf_op jit(solution)/shard_map/ppermute | solution.py:325
  82.5 0.0 collective-permute-done.8.refs_1_
  82.5 3.3 %collective-permute-done.9.refs_2_ = bf16[3,128,768]{2,1,0:T(8,128)(2,1)S(1)} collective-permute-done((bf16[3,128,768]{2,1,0:T(8,128)(2,1)}, bf16[3,128,768]{2,1,0:T(8,128)(2,1)S(1)}, u32[]{:S(2)}, u32[]{:S(2)}) %collective-permute-start.9) | collective-permute-done | bytes 589856 | tf_op jit(solution)/shard_map/ppermute | solution.py:325
  85.8 0.0 collective-permute-done.7.refs_4_
  85.8 0.0 collective-permute-done.6.refs_1_
  85.8 0.0 copy-start.5
  85.8 1.2 copy-done.5
  87.0 4.3 %pick_b.1 = (bf16[2,128,768]{2,1,0:T(8,128)(2,1)}, bf16[2,128,768]{2,1,0:T(8,128)(2,1)}, bf16[2,128,768]{2,1,0:T(8,128)(2,1)}, bf16[4,2,128,768]{3,2,1,0:T(8,128)(2,1)}) custom-call(s32[344]{0:T(512)} %plan.1, bf16[8,128,768]{2,1,0:T(8,128)(2,1)} %get-tuple-element.42.cols.after.refs_0_, bf16[8,128,768]{2,1,0:T(8,128)(2,1)} %copy-done.5), custom_call_target="tpu_custom_call" | custom-call | bytes 65536 | tf_op jit(solution)/shard_map/pick_b/pallas_call | solution.py:346
  91.3 0.0 copy-done.9
  91.3 3.6 %all-to-all-start = ((bf16[4,2,128,768]{3,2,1,0:T(8,128)(2,1)}), bf16[4,2,128,768]{3,2,1,0:T(8,128)(2,1)S(1)}, u32[]{:S(2)}, u32[]{:S(2)}) async-start(bf16[4,2,128,768]{3,2,1,0:T(8,128)(2,1)} %get-tuple-element.75), calls=%async_computation | async-start | bytes 3145728 | tf_op jit(solution)/shard_map/all_to_all | solution.py:447
  94.9 1.1 collective-permute-start.12
  96.0 1.5 collective-permute-start.13
  97.4 6.6 %collective-permute-start.11 = (bf16[2,128,768]{2,1,0:T(8,128)(2,1)}, bf16[2,128,768]{2,1,0:T(8,128)(2,1)S(1)}, u32[]{:S(2)}, u32[]{:S(2)}) collective-permute-start(bf16[2,128,768]{2,1,0:T(8,128)(2,1)} %get-tuple-element.70), channel_id=1, source_target_pairs={{0,168},{8,176},{16,184},{24,128},{32,136},{40,144},{48,152},{56,1... | collective-permute-start | bytes 1179656 | tf_op jit(solution)/shard_map/ppermute | solution.py:325
  104.0 1.5 collective-permute-start.14
  105.5 0.0 copy-done.7
  105.5 0.0 copy-done.8
  105.5 0.0 copy-done.6
  105.5 9.8 %pairs_a.1 = (f32[16,512]{1,0:T(8,128)}, f32[16,128]{1,0:T(8,128)}) custom-call(s32[344]{0:T(512)} %plan.1, bf16[16,512,768]{2,1,0:T(8,128)(2,1)} %get-tuple-element.50.own, bf16[3,128,768]{2,1,0:T(8,128)(2,1)} %get-tuple-element.61.refs_0_, bf16[3,128,768]{2,1,0:T(8,128)(2,1)} %copy-done.8, bf16[3,128,768]{2,1,0:T(8,128)(2,1)} %copy-done.9, ...), custom_call_target="tpu_custom_call" | custom-call | bytes 65536 | tf_op jit(solution)/shard_map/pairs_a/pallas_call | solution.py:366
  115.3 0.0 collective-permute-done.12.refs_1_
  115.3 0.0 copy-start.10
  115.3 4.3 %collective-permute-done.13.refs_2_ = bf16[2,128,768]{2,1,0:T(8,128)(2,1)S(1)} collective-permute-done((bf16[2,128,768]{2,1,0:T(8,128)(2,1)}, bf16[2,128,768]{2,1,0:T(8,128)(2,1)S(1)}, u32[]{:S(2)}, u32[]{:S(2)}) %collective-permute-start.13) | collective-permute-done | bytes 393248 | tf_op jit(solution)/shard_map/ppermute | solution.py:325
  119.6 8.9 %collective-permute-done.11.refs_0_ = bf16[2,128,768]{2,1,0:T(8,128)(2,1)S(1)} collective-permute-done((bf16[2,128,768]{2,1,0:T(8,128)(2,1)}, bf16[2,128,768]{2,1,0:T(8,128)(2,1)S(1)}, u32[]{:S(2)}, u32[]{:S(2)}) %collective-permute-start.11) | collective-permute-done | bytes 393248 | tf_op jit(solution)/shard_map/ppermute | solution.py:325
  128.5 0.8 copy-done.12
  129.3 6.2 %pairs_b.1 = (f32[16,512]{1,0:T(8,128)}, f32[6,128]{1,0:T(8,128)}) custom-call(s32[344]{0:T(512)} %plan.1, bf16[16,512,768]{2,1,0:T(8,128)(2,1)} %get-tuple-element.50.own, bf16[2,128,768]{2,1,0:T(8,128)(2,1)} %copy-done.12, bf16[2,128,768]{2,1,0:T(8,128)(2,1)} %copy-done.10, bf16[2,128,768]{2,1,0:T(8,128)(2,1)} %copy-done.11, ...), custom_call_target="tpu_custom_call" | custom-call | bytes 65536 | tf_op jit(solution)/shard_map/pairs_b/pallas_call | solution.py:366
  135.5 0.0 collective-permute-done.14.refs_4_
  135.5 0.0 all-to-all-done.refs_5_
  135.5 1.2 copy-done.3
  136.7 7.6 %pairs_c.1 = (f32[16,512]{1,0:T(8,128)}, f32[64,128]{1,0:T(8,128)}, f32[8,512]{1,0:T(8,128)}) custom-call(s32[344]{0:T(512)} %plan.1, bf16[16,512,768]{2,1,0:T(8,128)(2,1)} %get-tuple-element.50.own, f32[16,512]{1,0:T(8,128)} %get-tuple-element.68.refs_3_.refs_0_, f32[16,128]{1,0:T(8,128)} %get-tuple-element.69.refs_1_, ...), custom_call_target="tpu_custom_call" | custom-call | bytes 65536 | tf_op jit(solution)/shard_map/pairs_c/pallas_call | solution.py:366
  144.3 9.1 %all-to-all-start.1 = ((f32[32,2,128]{2,1,0:T(2,128)}), f32[32,2,128]{2,1,0:T(2,128)S(1)}, u32[]{:S(2)}, u32[]{:S(2)}) async-start(f32[32,2,128]{2,1,0:T(2,128)} %bitcast.8), calls=%async_computation.1 | async-start | bytes 65536 | tf_op jit(solution)/shard_map/all_to_all | solution.py:474
  153.3 0.1 collective-permute-start.15
  153.4 1.4 collective-permute-done.15.sib_rows
  154.8 0.8 copy-done.1
  155.6 7.6 %all-to-all-done.1 = f32[32,2,128]{2,1,0:T(2,128)S(1)} async-done(((f32[32,2,128]{2,1,0:T(2,128)}), f32[32,2,128]{2,1,0:T(2,128)S(1)}, u32[]{:S(2)}, u32[]{:S(2)}) %all-to-all-start.1) | async-done | bytes 32800 | tf_op jit(solution)/shard_map/all_to_all | solution.py:474
  163.2 0.7 merge.1.one
  163.9 0.3 collective-permute-start.16
  164.2 2.6 %collective-permute-start.17 = (f32[8,512]{1,0:T(8,128)S(1)}, f32[8,512]{1,0:T(8,128)S(1)}, u32[]{:S(2)}, u32[]{:S(2)}) collective-permute-start(f32[8,512]{1,0:T(8,128)S(1)} %merge.1.one), channel_id=1, source_target_pairs={{0,2},{1,3},{2,0},{3,1},{4,6},{5,7},{6,4},{7,5},{8,10},{9,11},{10,... | collective-permute-start | bytes 49160 | tf_op jit(solution)/shard_map/ppermute | solution.py:495
  166.8 0.0 collective-permute-start.18
  166.8 0.9 collective-permute-done.16.two
  167.7 1.7 %collective-permute-done.17.three = f32[8,512]{1,0:T(8,128)S(1)} collective-permute-done((f32[8,512]{1,0:T(8,128)S(1)}, f32[8,512]{1,0:T(8,128)S(1)}, u32[]{:S(2)}, u32[]{:S(2)}) %collective-permute-start.17) | collective-permute-done | bytes 16416 | tf_op jit(solution)/shard_map/ppermute | solution.py:495
  169.5 2.3 %collective-permute-done.18.four = f32[8,512]{1,0:T(8,128)S(1)} collective-permute-done((f32[8,512]{1,0:T(8,128)S(1)}, f32[8,512]{1,0:T(8,128)S(1)}, u32[]{:S(2)}, u32[]{:S(2)}) %collective-permute-start.18) | collective-permute-done | bytes 16416 | tf_op jit(solution)/shard_map/ppermute | solution.py:495
  171.7 0.6 finish.1
  (16 shorter events, 0.0 us)
Async XLA Ops:
  0.0 16.9 %collective-permute-start.5 = (bf16[8,512,768]{2,1,0:T(8,128)(2,1)}, bf16[8,512,768]{2,1,0:T(8,128)(2,1)}, u32[]{:S(2)}, u32[]{:S(2)}) collective-permute-start(bf16[8,512,768]{2,1,0:T(8,128)(2,1)} %bitcast.5), channel_id=1, source_target_pairs={{0,4},{4,0},{1,5},{5,1},{2,6},{6,2},{3,7},{7,3},{8,12},{12,8},{9,1... | collective-permute-start | bytes 18874376 | tf_op jit(solution)/shard_map/ppermute | solution.py:404
  4.4 41.7 %collective-permute-start = (bf16[8,128,768]{2,1,0:T(8,128)(2,1)}, bf16[8,128,768]{2,1,0:T(8,128)(2,1)S(1)}, u32[]{:S(2)}, u32[]{:S(2)}) collective-permute-start(bf16[8,128,768]{2,1,0:T(8,128)(2,1)} %get-tuple-element.42.cols.after.refs_0_), channel_id=1, source_target_pairs={{0,8},{8,16},{16,24},{24,32},{32,40},{40,48},{48,56},{56,0},{64,72... | collective-permute-start | bytes 4718600 | tf_op jit(solution)/shard_map/ppermute | solution.py:325
  6.4 37.3 %collective-permute-start.1 = (bf16[1,128,768]{2,1,0:T(8,128)(2,1)}, bf16[1,128,768]{2,1,0:T(8,128)(2,1)S(1)}, u32[]{:S(2)}, u32[]{:S(2)}) collective-permute-start(bf16[1,128,768]{2,1,0:T(8,128)(2,1)} %get-tuple-element.43), channel_id=1, source_target_pairs={{0,48},{8,56},{16,0},{24,8},{32,16},{40,24},{48,32},{56,40},{64,11... | collective-permute-start | bytes 589832 | tf_op jit(solution)/shard_map/ppermute | solution.py:325
  11.8 31.9 %collective-permute-start.2 = (bf16[1,128,768]{2,1,0:T(8,128)(2,1)}, bf16[1,128,768]{2,1,0:T(8,128)(2,1)S(1)}, u32[]{:S(2)}, u32[]{:S(2)}) collective-permute-start(bf16[1,128,768]{2,1,0:T(8,128)(2,1)} %get-tuple-element.44), channel_id=1, source_target_pairs={{0,112},{8,120},{16,64},{24,72},{32,80},{40,88},{48,96},{56,104},{... | collective-permute-start | bytes 589832 | tf_op jit(solution)/shard_map/ppermute | solution.py:325
  14.1 29.5 %collective-permute-start.3 = (bf16[1,128,768]{2,1,0:T(8,128)(2,1)}, bf16[1,128,768]{2,1,0:T(8,128)(2,1)S(1)}, u32[]{:S(2)}, u32[]{:S(2)}) collective-permute-start(bf16[1,128,768]{2,1,0:T(8,128)(2,1)} %get-tuple-element.45), channel_id=1, source_target_pairs={{0,176},{8,184},{16,128},{24,136},{32,144},{40,152},{48,160},{56,1... | collective-permute-start | bytes 589832 | tf_op jit(solution)/shard_map/ppermute | solution.py:325
  16.9 29.2 %collective-permute-start.4 = (bf16[1,128,768]{2,1,0:T(8,128)(2,1)}, bf16[1,128,768]{2,1,0:T(8,128)(2,1)S(1)}, u32[]{:S(2)}, u32[]{:S(2)}) collective-permute-start(bf16[1,128,768]{2,1,0:T(8,128)(2,1)} %get-tuple-element.46), channel_id=1, source_target_pairs={{0,240},{8,248},{16,192},{24,200},{32,208},{40,216},{48,224},{56,2... | collective-permute-start | bytes 589832 | tf_op jit(solution)/shard_map/ppermute | solution.py:325
  46.1 5.6 %copy-start.4 = (bf16[8,128,768]{2,1,0:T(8,128)(2,1)}, bf16[8,128,768]{2,1,0:T(8,128)(2,1)S(1)}, u32[]{:S(2)}) copy-start(bf16[8,128,768]{2,1,0:T(8,128)(2,1)S(1)} %collective-permute-done.refs_1_) | copy-start | bytes 4718596
  46.1 39.7 %collective-permute-start.6 = (bf16[8,128,768]{2,1,0:T(8,128)(2,1)S(1)}, bf16[8,128,768]{2,1,0:T(8,128)(2,1)S(1)}, u32[]{:S(2)}, u32[]{:S(2)}) collective-permute-start(bf16[8,128,768]{2,1,0:T(8,128)(2,1)S(1)} %collective-permute-done.refs_1_), channel_id=1, source_target_pairs={{0,8},{8,16},{16,24},{24,32},{32,40},{40,48},{48,56},{56,0},{64,72... | collective-permute-start | bytes 4718600 | tf_op jit(solution)/shard_map/ppermute | solution.py:325
  48.7 37.0 %collective-permute-start.7 = (bf16[4,128,768]{2,1,0:T(8,128)(2,1)S(1)}, bf16[4,128,768]{2,1,0:T(8,128)(2,1)S(1)}, u32[]{:S(2)}, u32[]{:S(2)}) collective-permute-start(bf16[4,128,768]{2,1,0:T(8,128)(2,1)S(1)} %pad_maximum_fusion), channel_id=1, source_target_pairs={{0,48},{8,56},{16,0},{24,8},{32,16},{40,24},{48,32},{56,40},{64,11... | collective-permute-start | bytes 2359304 | tf_op jit(solution)/shard_map/ppermute | solution.py:325
  55.6 26.9 %collective-permute-start.10 = (bf16[3,128,768]{2,1,0:T(8,128)(2,1)}, bf16[3,128,768]{2,1,0:T(8,128)(2,1)S(1)}, u32[]{:S(2)}, u32[]{:S(2)}) collective-permute-start(bf16[3,128,768]{2,1,0:T(8,128)(2,1)} %get-tuple-element.60), channel_id=1, source_target_pairs={{0,192},{8,200},{16,208},{24,216},{32,224},{40,232},{48,240},{56,2... | collective-permute-start | bytes 1769480 | tf_op jit(solution)/shard_map/ppermute | solution.py:325
  57.2 25.3 %collective-permute-start.8 = (bf16[3,128,768]{2,1,0:T(8,128)(2,1)}, bf16[3,128,768]{2,1,0:T(8,128)(2,1)S(1)}, u32[]{:S(2)}, u32[]{:S(2)}) collective-permute-start(bf16[3,128,768]{2,1,0:T(8,128)(2,1)} %get-tuple-element.58), channel_id=1, source_target_pairs={{0,64},{8,72},{16,80},{24,88},{32,96},{40,104},{48,112},{56,120},{... | collective-permute-start | bytes 1769480 | tf_op jit(solution)/shard_map/ppermute | solution.py:325
  57.7 28.1 %collective-permute-start.9 = (bf16[3,128,768]{2,1,0:T(8,128)(2,1)}, bf16[3,128,768]{2,1,0:T(8,128)(2,1)S(1)}, u32[]{:S(2)}, u32[]{:S(2)}) collective-permute-start(bf16[3,128,768]{2,1,0:T(8,128)(2,1)} %get-tuple-element.59), channel_id=1, source_target_pairs={{0,128},{8,136},{16,144},{24,152},{32,160},{40,168},{48,176},{56,1... | collective-permute-start | bytes 1769480 | tf_op jit(solution)/shard_map/ppermute | solution.py:325
  82.5 23.0 %copy-start.7 = (bf16[3,128,768]{2,1,0:T(8,128)(2,1)}, bf16[3,128,768]{2,1,0:T(8,128)(2,1)S(1)}, u32[]{:S(2)}) copy-start(bf16[3,128,768]{2,1,0:T(8,128)(2,1)S(1)} %collective-permute-done.10.refs_3_) | copy-start | bytes 1769476
  82.5 23.0 %copy-start.8 = (bf16[3,128,768]{2,1,0:T(8,128)(2,1)}, bf16[3,128,768]{2,1,0:T(8,128)(2,1)S(1)}, u32[]{:S(2)}) copy-start(bf16[3,128,768]{2,1,0:T(8,128)(2,1)S(1)} %collective-permute-done.8.refs_1_) | copy-start | bytes 1769476
  85.8 5.5 %copy-start.9 = (bf16[3,128,768]{2,1,0:T(8,128)(2,1)}, bf16[3,128,768]{2,1,0:T(8,128)(2,1)S(1)}, u32[]{:S(2)}) copy-start(bf16[3,128,768]{2,1,0:T(8,128)(2,1)S(1)} %collective-permute-done.9.refs_2_) | copy-start | bytes 1769476
  85.8 19.7 %copy-start.6 = (bf16[4,128,768]{2,1,0:T(8,128)(2,1)}, bf16[4,128,768]{2,1,0:T(8,128)(2,1)S(1)}, u32[]{:S(2)}) copy-start(bf16[4,128,768]{2,1,0:T(8,128)(2,1)S(1)} %collective-permute-done.7.refs_4_) | copy-start | bytes 2359300
  85.8 1.2 copy-start.5
  91.3 44.2 %all-to-all-start = ((bf16[4,2,128,768]{3,2,1,0:T(8,128)(2,1)}), bf16[4,2,128,768]{3,2,1,0:T(8,128)(2,1)S(1)}, u32[]{:S(2)}, u32[]{:S(2)}) async-start(bf16[4,2,128,768]{3,2,1,0:T(8,128)(2,1)} %get-tuple-element.75), calls=%async_computation | async-start | bytes 3145728 | tf_op jit(solution)/shard_map/all_to_all | solution.py:447
  94.9 20.4 %collective-permute-start.12 = (bf16[2,128,768]{2,1,0:T(8,128)(2,1)}, bf16[2,128,768]{2,1,0:T(8,128)(2,1)S(1)}, u32[]{:S(2)}, u32[]{:S(2)}) collective-permute-start(bf16[2,128,768]{2,1,0:T(8,128)(2,1)} %get-tuple-element.67.refs_5_), channel_id=1, source_target_pairs={{0,8},{8,16},{16,24},{24,32},{32,40},{40,48},{48,56},{56,0},{64,72... | collective-permute-start | bytes 1179656 | tf_op jit(solution)/shard_map/ppermute | solution.py:325
  96.0 23.6 %collective-permute-start.13 = (bf16[2,128,768]{2,1,0:T(8,128)(2,1)}, bf16[2,128,768]{2,1,0:T(8,128)(2,1)S(1)}, u32[]{:S(2)}, u32[]{:S(2)}) collective-permute-start(bf16[2,128,768]{2,1,0:T(8,128)(2,1)} %get-tuple-element.71), channel_id=1, source_target_pairs={{0,72},{8,80},{16,88},{24,96},{32,104},{40,112},{48,120},{56,64},{... | collective-permute-start | bytes 1179656 | tf_op jit(solution)/shard_map/ppermute | solution.py:325
  97.4 31.1 %collective-permute-start.11 = (bf16[2,128,768]{2,1,0:T(8,128)(2,1)}, bf16[2,128,768]{2,1,0:T(8,128)(2,1)S(1)}, u32[]{:S(2)}, u32[]{:S(2)}) collective-permute-start(bf16[2,128,768]{2,1,0:T(8,128)(2,1)} %get-tuple-element.70), channel_id=1, source_target_pairs={{0,168},{8,176},{16,184},{24,128},{32,136},{40,144},{48,152},{56,1... | collective-permute-start | bytes 1179656 | tf_op jit(solution)/shard_map/ppermute | solution.py:325
  104.0 31.5 %collective-permute-start.14 = (bf16[2,128,768]{2,1,0:T(8,128)(2,1)}, bf16[2,128,768]{2,1,0:T(8,128)(2,1)}, u32[]{:S(2)}, u32[]{:S(2)}) collective-permute-start(bf16[2,128,768]{2,1,0:T(8,128)(2,1)} %get-tuple-element.74), channel_id=1, source_target_pairs={{0,200},{8,208},{16,216},{24,224},{32,232},{40,240},{48,248},{56,1... | collective-permute-start | bytes 1179656 | tf_op jit(solution)/shard_map/ppermute | solution.py:325
  115.3 13.2 %copy-start.10 = (bf16[2,128,768]{2,1,0:T(8,128)(2,1)}, bf16[2,128,768]{2,1,0:T(8,128)(2,1)S(1)}, u32[]{:S(2)}) copy-start(bf16[2,128,768]{2,1,0:T(8,128)(2,1)S(1)} %collective-permute-done.12.refs_1_) | copy-start | bytes 1179652
  119.6 8.9 %copy-start.11 = (bf16[2,128,768]{2,1,0:T(8,128)(2,1)}, bf16[2,128,768]{2,1,0:T(8,128)(2,1)S(1)}, u32[]{:S(2)}) copy-start(bf16[2,128,768]{2,1,0:T(8,128)(2,1)S(1)} %collective-permute-done.13.refs_2_) | copy-start | bytes 1179652
  128.5 0.8 copy-start.12
  135.5 1.2 copy-start.3
  136.7 18.1 %copy-start.2 = (f32[8,512]{1,0:T(8,128)S(1)}, f32[8,512]{1,0:T(8,128)}, u32[]{:S(2)}) copy-start(f32[8,512]{1,0:T(8,128)} %get-tuple-element.49.local) | copy-start | bytes 49156
  136.7 26.5 %copy-start = (s32[344]{0:T(512)S(1)}, s32[344]{0:T(512)}, u32[]{:S(2)}) copy-start(s32[344]{0:T(512)} %plan.1) | copy-start | bytes 4132
  144.3 18.9 %all-to-all-start.1 = ((f32[32,2,128]{2,1,0:T(2,128)}), f32[32,2,128]{2,1,0:T(2,128)S(1)}, u32[]{:S(2)}, u32[]{:S(2)}) async-start(f32[32,2,128]{2,1,0:T(2,128)} %bitcast.8), calls=%async_computation.1 | async-start | bytes 65536 | tf_op jit(solution)/shard_map/all_to_all | solution.py:474
  153.3 1.5 collective-permute-start.15
  154.8 0.8 copy-start.1
  163.9 3.8 %collective-permute-start.16 = (f32[8,512]{1,0:T(8,128)S(1)}, f32[8,512]{1,0:T(8,128)S(1)}, u32[]{:S(2)}, u32[]{:S(2)}) collective-permute-start(f32[8,512]{1,0:T(8,128)S(1)} %merge.1.one), channel_id=1, source_target_pairs={{0,1},{1,2},{2,3},{3,0},{4,5},{5,6},{6,7},{7,4},{8,9},{9,10},{10,1... | collective-permute-start | bytes 49160 | tf_op jit(solution)/shard_map/ppermute | solution.py:495
  164.2 5.2 %collective-permute-start.17 = (f32[8,512]{1,0:T(8,128)S(1)}, f32[8,512]{1,0:T(8,128)S(1)}, u32[]{:S(2)}, u32[]{:S(2)}) collective-permute-start(f32[8,512]{1,0:T(8,128)S(1)} %merge.1.one), channel_id=1, source_target_pairs={{0,2},{1,3},{2,0},{3,1},{4,6},{5,7},{6,4},{7,5},{8,10},{9,11},{10,... | collective-permute-start | bytes 49160 | tf_op jit(solution)/shard_map/ppermute | solution.py:495
  166.8 4.9 %collective-permute-start.18 = (f32[8,512]{1,0:T(8,128)S(1)}, f32[8,512]{1,0:T(8,128)S(1)}, u32[]{:S(2)}, u32[]{:S(2)}) collective-permute-start(f32[8,512]{1,0:T(8,128)S(1)} %merge.1.one), channel_id=1, source_target_pairs={{0,3},{1,0},{2,1},{3,2},{4,7},{5,4},{6,5},{7,6},{8,11},{9,8},{10,9... | collective-permute-start | bytes 49160 | tf_op jit(solution)/shard_map/ppermute | solution.py:495

commit v8 on v5

--- a/solution.py
+++ b/solution.py
@@ -241,8 +241,8 @@
             for slot in range(len(done)):
                 col_out[pl.ds(plan[at_row + number], 1), :] = ref[slot : slot + 1, :]
                 number += 1
-    part = lax.broadcasted_iota(jnp.int32, (quarter, rows), 0)
-    lane = lax.broadcasted_iota(jnp.int32, (2 * quarter, rows), 1)
+    row = lax.broadcasted_iota(jnp.int32, (rows, quarter), 0)
+    lane = lax.broadcasted_iota(jnp.int32, (rows, quarter), 1)
     for copy in gets:
         copy.wait()
     for o in range(2 * blocks):
@@ -257,18 +257,22 @@
             pair = [plan[first_of + group], plan[second_of + group]]
             here_slot = [jnp.minimum(slot, slots - 1) for slot in pair]
             scores = dot_t(
-                jnp.concatenate([held[here_slot[0]], held[here_slot[1]]], axis=0), units[o]
+                units[o], jnp.concatenate([held[here_slot[0]], held[here_slot[1]]], axis=0)
             )
-            ok = jnp.where(lane < plan[at_own + o], scores, absent)
-            folded = jnp.maximum(
-                jnp.maximum(ok[:, 0:128], ok[:, 128:256]), jnp.maximum(ok[:, 256:384], ok[:, 384:512])
+            folded = jnp.full((rows, quarter), absent, jnp.float32)
+            for half in range(2):
+                here = scores[:, half * quarter : (half + 1) * quarter]
+                ok = jnp.where(row < plan[at_own + o], here, absent)
+                cols[pl.ds(pair[half], 1), :] = jnp.max(ok, axis=0, keepdims=True)
+                ok = jnp.where(lane < plan[counts + pair[half]], here, absent)
+                folded = jnp.maximum(folded, ok)
+            top = jnp.concatenate(
+                [
+                    jnp.max(folded[k : k + quarter].T, axis=0, keepdims=True)
+                    for k in range(0, rows, quarter)
+                ],
+                axis=1,
             )
-            top = jnp.full((1, rows), absent, jnp.float32)
-            for half in range(2):
-                span = slice(half * quarter, (half + 1) * quarter)
-                here = jnp.where(part < plan[counts + pair[half]], scores[span], absent)
-                top = jnp.maximum(top, jnp.max(here, axis=0, keepdims=True))
-                cols[pl.ds(pair[half], 1), :] = jnp.max(folded[span].T, axis=0, keepdims=True)
             row_out[pl.ds(o, 1), :] = jnp.maximum(row_out[pl.ds(o, 1), :], top)
         return carry
 

time: 170 us -> 169 us (level)
    all_to_all x1, starting transfers between devices: 8.64 us -> 6.88 us  [on_device(): lax.all_to_all(col_best, ('x', 'z'), split_axis=0, concat_axis=0, tiled=T...]
  transfers between devices with their start and end apart: 21 -> 21, of which waited for: 12 -> 12; matrix products, arithmetic and copies ran while one was open for 0% -> 0% of each run, Pallas kernels for 27% -> 28%
where the time goes in v8:
time: 169 us; the launch traced here: 167 us
  Pallas kernels  61.3 us (36%)
  waiting for transfers between devices  51.9 us (31%)
  starting transfers between devices  49.1 us (29%)
  local copies, waits for them, and re-layouts  4.68 us (3%)
    ppermute x14, waiting for transfers between devices, move(): return lax.ppermute(value, ('x', 'z'), steps)  37.7 us
    ppermute x14, starting transfers between devices, move(): return lax.ppermute(value, ('x', 'z'), steps)  35.6 us
    pallas_call x3, Pallas kernels, compare(): pl.pallas_call(functools.partial(pair_kernel, stage, feeds), out_shape=[j...  23.6 us
    pallas_call x1, Pallas kernels, on_device(): pl.pallas_call(local_kernel, grid=(2 * blocks,), out_shape=(jax.ShapeDtyp...  21.8 us
    all_to_all x1, waiting for transfers between devices, on_device(): lax.all_to_all(col_best, ('x', 'z'), split_axis=0, concat_axis=0, tiled=T...  7.59 us
    pallas_call x2, Pallas kernels, pick(): pl.pallas_call(functools.partial(pick_kernel, wanted, spread), out_shape=...  7.36 us
    all_to_all x1, starting transfers between devices, on_device(): lax.all_to_all(col_best, ('x', 'z'), split_axis=0, concat_axis=0, tiled=T...  6.88 us
    ppermute x3, waiting for transfers between devices, on_device(): lax.ppermute(combined, 'rep', [(y, (y + d) % n_rep) for y in range(n_rep)])  4.95 us
  transfers between devices with their start and end apart: 21, of which 12 were waited for; matrix products, arithmetic and copies ran while one was open for 0% of the time, Pallas kernels for 28%

profile of v8, /device:TPU:24, one launch (start us, length us, event | category | flops | bytes accessed | tf_op | source)
XLA Modules:
  0.0 167.2 jit_solution(7700923236890501295)
XLA Ops:
  0.0 0.0 collective-permute-start.5
  0.0 4.4 %prep.1 = (bf16[8,128,768]{2,1,0:T(8,128)(2,1)}, bf16[1,128,768]{2,1,0:T(8,128)(2,1)}, bf16[1,128,768]{2,1,0:T(8,128)(2,1)}, bf16[1,128,768]{2,1,0:T(8,128)(2,1)...) custom-call(s32[64,64]{1,0:T(8,128)} %table.3, bf16[8,512,768]{2,1,0:T(8,128)(2,1)} %bitcast.6), custom_call_target="tpu_custom_call" | custom-call | bytes 65536 | tf_op jit(solution)/shard_map/prep/pallas_call | solution.py:390
  4.4 2.0 %collective-permute-start = (bf16[8,128,768]{2,1,0:T(8,128)(2,1)}, bf16[8,128,768]{2,1,0:T(8,128)(2,1)S(1)}, u32[]{:S(2)}, u32[]{:S(2)}) collective-permute-start(bf16[8,128,768]{2,1,0:T(8,128)(2,1)} %get-tuple-element.42.cols.after.refs_0_), channel_id=1, source_target_pairs={{0,8},{8,16},{16,24},{24,32},{32,40},{40,48},{48,56},{56,0},{64,72... | collective-permute-start | bytes 4718600 | tf_op jit(solution)/shard_map/ppermute | solution.py:329
  6.4 5.4 %collective-permute-start.1 = (bf16[1,128,768]{2,1,0:T(8,128)(2,1)}, bf16[1,128,768]{2,1,0:T(8,128)(2,1)S(1)}, u32[]{:S(2)}, u32[]{:S(2)}) collective-permute-start(bf16[1,128,768]{2,1,0:T(8,128)(2,1)} %get-tuple-element.43), channel_id=1, source_target_pairs={{0,48},{8,56},{16,0},{24,8},{32,16},{40,24},{48,32},{56,40},{64,11... | collective-permute-start | bytes 589832 | tf_op jit(solution)/shard_map/ppermute | solution.py:329
  11.8 2.4 %collective-permute-start.2 = (bf16[1,128,768]{2,1,0:T(8,128)(2,1)}, bf16[1,128,768]{2,1,0:T(8,128)(2,1)S(1)}, u32[]{:S(2)}, u32[]{:S(2)}) collective-permute-start(bf16[1,128,768]{2,1,0:T(8,128)(2,1)} %get-tuple-element.44), channel_id=1, source_target_pairs={{0,112},{8,120},{16,64},{24,72},{32,80},{40,88},{48,96},{56,104},{... | collective-permute-start | bytes 589832 | tf_op jit(solution)/shard_map/ppermute | solution.py:329
  14.1 2.7 %collective-permute-start.3 = (bf16[1,128,768]{2,1,0:T(8,128)(2,1)}, bf16[1,128,768]{2,1,0:T(8,128)(2,1)S(1)}, u32[]{:S(2)}, u32[]{:S(2)}) collective-permute-start(bf16[1,128,768]{2,1,0:T(8,128)(2,1)} %get-tuple-element.45), channel_id=1, source_target_pairs={{0,176},{8,184},{16,128},{24,136},{32,144},{40,152},{48,160},{56,1... | collective-permute-start | bytes 589832 | tf_op jit(solution)/shard_map/ppermute | solution.py:329
  16.9 0.0 collective-permute-done.5.sib
  16.9 2.1 %collective-permute-start.4 = (bf16[1,128,768]{2,1,0:T(8,128)(2,1)}, bf16[1,128,768]{2,1,0:T(8,128)(2,1)S(1)}, u32[]{:S(2)}, u32[]{:S(2)}) collective-permute-start(bf16[1,128,768]{2,1,0:T(8,128)(2,1)} %get-tuple-element.46), channel_id=1, source_target_pairs={{0,240},{8,248},{16,192},{24,200},{32,208},{40,216},{48,224},{56,2... | collective-permute-start | bytes 589832 | tf_op jit(solution)/shard_map/ppermute | solution.py:329
  19.0 2.8 %plan.1 = s32[344]{0:T(512)} custom-call(s32[64,64]{1,0:T(8,128)} %table.3, s32[512]{0:T(512)} %valid.3, bf16[8,128,768]{2,1,0:T(8,128)(2,1)} %get-tuple-element.42.cols.after.refs_0_), custom_call_target="tpu_custom_call" | custom-call | bytes 65536 | tf_op jit(solution)/shard_map/plan/pallas_call | solution.py:411
  21.8 21.8 %local.1 = (bf16[16,512,768]{2,1,0:T(8,128)(2,1)}, f32[8,512]{1,0:T(8,128)}) custom-call(s32[512]{0:T(512)} %valid.3, bf16[8,512,768]{2,1,0:T(8,128)(2,1)} %bitcast.7, bf16[8,512,768]{2,1,0:T(8,128)(2,1)} %collective-permute-done.5.sib, bf16[8,128,768]{2,1,0:T(8,128)(2,1)} %get-tuple-element.42.cols.after.refs_0_), custom_call_target="tpu_custom_call" | custom-call | bytes 65536 | tf_op jit(solution)/shard_map/local/pallas_call | solution.py:421
  43.6 0.0 collective-permute-done.1
  43.6 0.0 collective-permute-done.2
  43.6 0.0 collective-permute-done.3
  43.6 2.5 %collective-permute-done.4 = bf16[1,128,768]{2,1,0:T(8,128)(2,1)S(1)} collective-permute-done((bf16[1,128,768]{2,1,0:T(8,128)(2,1)}, bf16[1,128,768]{2,1,0:T(8,128)(2,1)S(1)}, u32[]{:S(2)}, u32[]{:S(2)}) %collective-permute-start.4) | collective-permute-done | bytes 196640 | tf_op jit(solution)/shard_map/ppermute | solution.py:329
  46.1 0.0 collective-permute-done.refs_1_
  46.1 2.5 %collective-permute-start.6 = (bf16[8,128,768]{2,1,0:T(8,128)(2,1)S(1)}, bf16[8,128,768]{2,1,0:T(8,128)(2,1)S(1)}, u32[]{:S(2)}, u32[]{:S(2)}) collective-permute-start(bf16[8,128,768]{2,1,0:T(8,128)(2,1)S(1)} %collective-permute-done.refs_1_), channel_id=1, source_target_pairs={{0,8},{8,16},{16,24},{24,32},{32,40},{40,48},{48,56},{56,0},{64,72... | collective-permute-start | bytes 4718600 | tf_op jit(solution)/shard_map/ppermute | solution.py:329
  48.6 0.1 pad_maximum_fusion
  48.7 3.0 %collective-permute-start.7 = (bf16[4,128,768]{2,1,0:T(8,128)(2,1)S(1)}, bf16[4,128,768]{2,1,0:T(8,128)(2,1)S(1)}, u32[]{:S(2)}, u32[]{:S(2)}) collective-permute-start(bf16[4,128,768]{2,1,0:T(8,128)(2,1)S(1)} %pad_maximum_fusion), channel_id=1, source_target_pairs={{0,48},{8,56},{16,0},{24,8},{32,16},{40,24},{48,32},{56,40},{64,11... | collective-permute-start | bytes 2359304 | tf_op jit(solution)/shard_map/ppermute | solution.py:329
  51.7 0.0 copy-done.4
  51.7 3.4 %pick_a.1 = (bf16[3,128,768]{2,1,0:T(8,128)(2,1)}, bf16[3,128,768]{2,1,0:T(8,128)(2,1)}, bf16[3,128,768]{2,1,0:T(8,128)(2,1)}, bf16[3,128,768]{2,1,0:T(8,128)(2,1)}) custom-call(s32[344]{0:T(512)} %plan.1, bf16[8,128,768]{2,1,0:T(8,128)(2,1)} %get-tuple-element.42.cols.after.refs_0_, bf16[8,128,768]{2,1,0:T(8,128)(2,1)} %copy-done.4), custom_call_target="tpu_custom_call" | custom-call | bytes 65536 | tf_op jit(solution)/shard_map/pick_a/pallas_call | solution.py:350
  55.1 2.1 %collective-permute-start.10 = (bf16[3,128,768]{2,1,0:T(8,128)(2,1)}, bf16[3,128,768]{2,1,0:T(8,128)(2,1)S(1)}, u32[]{:S(2)}, u32[]{:S(2)}) collective-permute-start(bf16[3,128,768]{2,1,0:T(8,128)(2,1)} %get-tuple-element.60), channel_id=1, source_target_pairs={{0,192},{8,200},{16,208},{24,216},{32,224},{40,232},{48,240},{56,2... | collective-permute-start | bytes 1769480 | tf_op jit(solution)/shard_map/ppermute | solution.py:329
  57.2 0.0 collective-permute-start.8
  57.2 3.4 %collective-permute-start.9 = (bf16[3,128,768]{2,1,0:T(8,128)(2,1)}, bf16[3,128,768]{2,1,0:T(8,128)(2,1)S(1)}, u32[]{:S(2)}, u32[]{:S(2)}) collective-permute-start(bf16[3,128,768]{2,1,0:T(8,128)(2,1)} %get-tuple-element.59), channel_id=1, source_target_pairs={{0,128},{8,136},{16,144},{24,152},{32,160},{40,168},{48,176},{56,1... | collective-permute-start | bytes 1769480 | tf_op jit(solution)/shard_map/ppermute | solution.py:329
  60.6 11.0 %collective-permute-done.10.refs_3_ = bf16[3,128,768]{2,1,0:T(8,128)(2,1)S(1)} collective-permute-done((bf16[3,128,768]{2,1,0:T(8,128)(2,1)}, bf16[3,128,768]{2,1,0:T(8,128)(2,1)S(1)}, u32[]{:S(2)}, u32[]{:S(2)}) %collective-permute-start.10) | collective-permute-done | bytes 589856 | tf_op jit(solution)/shard_map/ppermute | solution.py:329
  71.6 14.2 %collective-permute-done.8.refs_1_ = bf16[3,128,768]{2,1,0:T(8,128)(2,1)S(1)} collective-permute-done((bf16[3,128,768]{2,1,0:T(8,128)(2,1)}, bf16[3,128,768]{2,1,0:T(8,128)(2,1)S(1)}, u32[]{:S(2)}, u32[]{:S(2)}) %collective-permute-start.8) | collective-permute-done | bytes 589856 | tf_op jit(solution)/shard_map/ppermute | solution.py:329
  85.8 0.0 collective-permute-done.9.refs_2_
  85.8 0.0 collective-permute-done.7.refs_4_
  85.8 0.0 copy-start.6
  85.8 0.0 collective-permute-done.6.refs_1_
  85.9 1.2 copy-done.5
  87.1 4.0 %pick_b.1 = (bf16[2,128,768]{2,1,0:T(8,128)(2,1)}, bf16[2,128,768]{2,1,0:T(8,128)(2,1)}, bf16[2,128,768]{2,1,0:T(8,128)(2,1)}, bf16[4,2,128,768]{3,2,1,0:T(8,128)(2,1)}) custom-call(s32[344]{0:T(512)} %plan.1, bf16[8,128,768]{2,1,0:T(8,128)(2,1)} %get-tuple-element.42.cols.after.refs_0_, bf16[8,128,768]{2,1,0:T(8,128)(2,1)} %copy-done.5), custom_call_target="tpu_custom_call" | custom-call | bytes 65536 | tf_op jit(solution)/shard_map/pick_b/pallas_call | solution.py:350
  91.0 0.0 copy-done.9
  91.0 3.6 %all-to-all-start = ((bf16[4,2,128,768]{3,2,1,0:T(8,128)(2,1)}), bf16[4,2,128,768]{3,2,1,0:T(8,128)(2,1)S(1)}, u32[]{:S(2)}, u32[]{:S(2)}) async-start(bf16[4,2,128,768]{3,2,1,0:T(8,128)(2,1)} %get-tuple-element.75), calls=%async_computation | async-start | bytes 3145728 | tf_op jit(solution)/shard_map/all_to_all | solution.py:450
  94.6 1.4 collective-permute-start.11
  96.1 1.5 collective-permute-start.12
  97.5 3.9 %collective-permute-start.13 = (bf16[2,128,768]{2,1,0:T(8,128)(2,1)}, bf16[2,128,768]{2,1,0:T(8,128)(2,1)S(1)}, u32[]{:S(2)}, u32[]{:S(2)}) collective-permute-start(bf16[2,128,768]{2,1,0:T(8,128)(2,1)} %get-tuple-element.73), channel_id=1, source_target_pairs={{0,200},{8,208},{16,216},{24,224},{32,232},{40,240},{48,248},{56,1... | collective-permute-start | bytes 1179656 | tf_op jit(solution)/shard_map/ppermute | solution.py:329
  101.4 3.2 %collective-permute-start.14 = (bf16[2,128,768]{2,1,0:T(8,128)(2,1)}, bf16[2,128,768]{2,1,0:T(8,128)(2,1)}, u32[]{:S(2)}, u32[]{:S(2)}) collective-permute-start(bf16[2,128,768]{2,1,0:T(8,128)(2,1)} %get-tuple-element.74), channel_id=1, source_target_pairs={{0,168},{8,176},{16,184},{24,128},{32,136},{40,144},{48,152},{56,1... | collective-permute-start | bytes 1179656 | tf_op jit(solution)/shard_map/ppermute | solution.py:329
  104.6 0.0 copy-done.7
  104.6 9.2 %pairs_a.1 = (f32[16,512]{1,0:T(8,128)}, f32[16,128]{1,0:T(8,128)}) custom-call(s32[344]{0:T(512)} %plan.1, bf16[16,512,768]{2,1,0:T(8,128)(2,1)} %get-tuple-element.50.own, bf16[3,128,768]{2,1,0:T(8,128)(2,1)} %get-tuple-element.61.refs_0_, bf16[3,128,768]{2,1,0:T(8,128)(2,1)} %copy-done.8, bf16[3,128,768]{2,1,0:T(8,128)(2,1)} %copy-done.9, ...), custom_call_target="tpu_custom_call" | custom-call | bytes 65536 | tf_op jit(solution)/shard_map/pairs_a/pallas_call | solution.py:370
  113.8 0.0 collective-permute-done.11.refs_0_
  113.8 0.0 copy-start.10
  113.9 5.6 %collective-permute-done.12.refs_1_ = bf16[2,128,768]{2,1,0:T(8,128)(2,1)S(1)} collective-permute-done((bf16[2,128,768]{2,1,0:T(8,128)(2,1)}, bf16[2,128,768]{2,1,0:T(8,128)(2,1)S(1)}, u32[]{:S(2)}, u32[]{:S(2)}) %collective-permute-start.12) | collective-permute-done | bytes 393248 | tf_op jit(solution)/shard_map/ppermute | solution.py:329
  119.5 0.0 copy-done.10
  119.5 0.8 copy-done.11
  120.2 5.1 %pairs_b.1 = (f32[16,512]{1,0:T(8,128)}, f32[4,128]{1,0:T(4,128)}) custom-call(s32[344]{0:T(512)} %plan.1, bf16[16,512,768]{2,1,0:T(8,128)(2,1)} %get-tuple-element.50.own, bf16[2,128,768]{2,1,0:T(8,128)(2,1)} %copy-done.10, bf16[2,128,768]{2,1,0:T(8,128)(2,1)} %copy-done.11, f32[16,512]{1,0:T(8,128)} %get-tuple-element.68.refs_2_.refs_0_), custom_call_target="tpu_custom_call" | custom-call | bytes 65536 | tf_op jit(solution)/shard_map/pairs_b/pallas_call | solution.py:370
  125.4 0.8 collective-permute-done.13.refs_4_
  126.2 0.8 copy-done.12
  126.9 3.6 %collective-permute-done.14.refs_5_ = bf16[2,128,768]{2,1,0:T(8,128)(2,1)} collective-permute-done((bf16[2,128,768]{2,1,0:T(8,128)(2,1)}, bf16[2,128,768]{2,1,0:T(8,128)(2,1)}, u32[]{:S(2)}, u32[]{:S(2)}) %collective-permute-start.14) | collective-permute-done | bytes 393248 | tf_op jit(solution)/shard_map/ppermute | solution.py:329
  130.6 0.2 all-to-all-done.refs_6_
  130.8 1.2 copy-done.3
  132.0 9.3 %pairs_c.1 = (f32[16,512]{1,0:T(8,128)}, f32[64,128]{1,0:T(8,128)}, f32[8,512]{1,0:T(8,128)}) custom-call(s32[344]{0:T(512)} %plan.1, bf16[16,512,768]{2,1,0:T(8,128)(2,1)} %get-tuple-element.50.own, f32[16,512]{1,0:T(8,128)} %get-tuple-element.68.refs_2_.refs_0_, f32[16,128]{1,0:T(8,128)} %get-tuple-element.69.refs_1_, ...), custom_call_target="tpu_custom_call" | custom-call | bytes 65536 | tf_op jit(solution)/shard_map/pairs_c/pallas_call | solution.py:370
  141.3 6.9 %all-to-all-start.1 = ((f32[32,2,128]{2,1,0:T(2,128)}), f32[32,2,128]{2,1,0:T(2,128)S(1)}, u32[]{:S(2)}, u32[]{:S(2)}) async-start(f32[32,2,128]{2,1,0:T(2,128)} %bitcast.8), calls=%async_computation.1 | async-start | bytes 65536 | tf_op jit(solution)/shard_map/all_to_all | solution.py:478
  148.2 0.1 collective-permute-start.15
  148.3 1.4 collective-permute-done.15.sib_rows
  149.7 0.8 copy-done.1
  150.4 7.6 %all-to-all-done.1 = f32[32,2,128]{2,1,0:T(2,128)S(1)} async-done(((f32[32,2,128]{2,1,0:T(2,128)}), f32[32,2,128]{2,1,0:T(2,128)S(1)}, u32[]{:S(2)}, u32[]{:S(2)}) %all-to-all-start.1) | async-done | bytes 32800 | tf_op jit(solution)/shard_map/all_to_all | solution.py:478
  158.0 0.7 merge.1.one
  158.7 0.3 collective-permute-start.16
  159.0 2.6 %collective-permute-start.17 = (f32[8,512]{1,0:T(8,128)S(1)}, f32[8,512]{1,0:T(8,128)S(1)}, u32[]{:S(2)}, u32[]{:S(2)}) collective-permute-start(f32[8,512]{1,0:T(8,128)S(1)} %merge.1.one), channel_id=1, source_target_pairs={{0,2},{1,3},{2,0},{3,1},{4,6},{5,7},{6,4},{7,5},{8,10},{9,11},{10,... | collective-permute-start | bytes 49160 | tf_op jit(solution)/shard_map/ppermute | solution.py:499
  161.6 0.0 collective-permute-start.18
  161.6 0.9 collective-permute-done.16.two
  162.6 1.7 %collective-permute-done.17.three = f32[8,512]{1,0:T(8,128)S(1)} collective-permute-done((f32[8,512]{1,0:T(8,128)S(1)}, f32[8,512]{1,0:T(8,128)S(1)}, u32[]{:S(2)}, u32[]{:S(2)}) %collective-permute-start.17) | collective-permute-done | bytes 16416 | tf_op jit(solution)/shard_map/ppermute | solution.py:499
  164.3 2.3 %collective-permute-done.18.four = f32[8,512]{1,0:T(8,128)S(1)} collective-permute-done((f32[8,512]{1,0:T(8,128)S(1)}, f32[8,512]{1,0:T(8,128)S(1)}, u32[]{:S(2)}, u32[]{:S(2)}) %collective-permute-start.18) | collective-permute-done | bytes 16416 | tf_op jit(solution)/shard_map/ppermute | solution.py:499
  166.6 0.6 finish.1
  (16 shorter events, 0.0 us)
Async XLA Ops:
  0.0 16.9 %collective-permute-start.5 = (bf16[8,512,768]{2,1,0:T(8,128)(2,1)}, bf16[8,512,768]{2,1,0:T(8,128)(2,1)}, u32[]{:S(2)}, u32[]{:S(2)}) collective-permute-start(bf16[8,512,768]{2,1,0:T(8,128)(2,1)} %bitcast.5), channel_id=1, source_target_pairs={{0,4},{4,0},{1,5},{5,1},{2,6},{6,2},{3,7},{7,3},{8,12},{12,8},{9,1... | collective-permute-start | bytes 18874376 | tf_op jit(solution)/shard_map/ppermute | solution.py:408
  4.4 41.7 %collective-permute-start = (bf16[8,128,768]{2,1,0:T(8,128)(2,1)}, bf16[8,128,768]{2,1,0:T(8,128)(2,1)S(1)}, u32[]{:S(2)}, u32[]{:S(2)}) collective-permute-start(bf16[8,128,768]{2,1,0:T(8,128)(2,1)} %get-tuple-element.42.cols.after.refs_0_), channel_id=1, source_target_pairs={{0,8},{8,16},{16,24},{24,32},{32,40},{40,48},{48,56},{56,0},{64,72... | collective-permute-start | bytes 4718600 | tf_op jit(solution)/shard_map/ppermute | solution.py:329
  6.4 37.3 %collective-permute-start.1 = (bf16[1,128,768]{2,1,0:T(8,128)(2,1)}, bf16[1,128,768]{2,1,0:T(8,128)(2,1)S(1)}, u32[]{:S(2)}, u32[]{:S(2)}) collective-permute-start(bf16[1,128,768]{2,1,0:T(8,128)(2,1)} %get-tuple-element.43), channel_id=1, source_target_pairs={{0,48},{8,56},{16,0},{24,8},{32,16},{40,24},{48,32},{56,40},{64,11... | collective-permute-start | bytes 589832 | tf_op jit(solution)/shard_map/ppermute | solution.py:329
  11.8 31.9 %collective-permute-start.2 = (bf16[1,128,768]{2,1,0:T(8,128)(2,1)}, bf16[1,128,768]{2,1,0:T(8,128)(2,1)S(1)}, u32[]{:S(2)}, u32[]{:S(2)}) collective-permute-start(bf16[1,128,768]{2,1,0:T(8,128)(2,1)} %get-tuple-element.44), channel_id=1, source_target_pairs={{0,112},{8,120},{16,64},{24,72},{32,80},{40,88},{48,96},{56,104},{... | collective-permute-start | bytes 589832 | tf_op jit(solution)/shard_map/ppermute | solution.py:329
  14.1 29.5 %collective-permute-start.3 = (bf16[1,128,768]{2,1,0:T(8,128)(2,1)}, bf16[1,128,768]{2,1,0:T(8,128)(2,1)S(1)}, u32[]{:S(2)}, u32[]{:S(2)}) collective-permute-start(bf16[1,128,768]{2,1,0:T(8,128)(2,1)} %get-tuple-element.45), channel_id=1, source_target_pairs={{0,176},{8,184},{16,128},{24,136},{32,144},{40,152},{48,160},{56,1... | collective-permute-start | bytes 589832 | tf_op jit(solution)/shard_map/ppermute | solution.py:329
  16.9 29.2 %collective-permute-start.4 = (bf16[1,128,768]{2,1,0:T(8,128)(2,1)}, bf16[1,128,768]{2,1,0:T(8,128)(2,1)S(1)}, u32[]{:S(2)}, u32[]{:S(2)}) collective-permute-start(bf16[1,128,768]{2,1,0:T(8,128)(2,1)} %get-tuple-element.46), channel_id=1, source_target_pairs={{0,240},{8,248},{16,192},{24,200},{32,208},{40,216},{48,224},{56,2... | collective-permute-start | bytes 589832 | tf_op jit(solution)/shard_map/ppermute | solution.py:329
  46.1 5.6 %copy-start.4 = (bf16[8,128,768]{2,1,0:T(8,128)(2,1)}, bf16[8,128,768]{2,1,0:T(8,128)(2,1)S(1)}, u32[]{:S(2)}) copy-start(bf16[8,128,768]{2,1,0:T(8,128)(2,1)S(1)} %collective-permute-done.refs_1_) | copy-start | bytes 4718596
  46.1 39.7 %collective-permute-start.6 = (bf16[8,128,768]{2,1,0:T(8,128)(2,1)S(1)}, bf16[8,128,768]{2,1,0:T(8,128)(2,1)S(1)}, u32[]{:S(2)}, u32[]{:S(2)}) collective-permute-start(bf16[8,128,768]{2,1,0:T(8,128)(2,1)S(1)} %collective-permute-done.refs_1_), channel_id=1, source_target_pairs={{0,8},{8,16},{16,24},{24,32},{32,40},{40,48},{48,56},{56,0},{64,72... | collective-permute-start | bytes 4718600 | tf_op jit(solution)/shard_map/ppermute | solution.py:329
  48.7 37.1 %collective-permute-start.7 = (bf16[4,128,768]{2,1,0:T(8,128)(2,1)S(1)}, bf16[4,128,768]{2,1,0:T(8,128)(2,1)S(1)}, u32[]{:S(2)}, u32[]{:S(2)}) collective-permute-start(bf16[4,128,768]{2,1,0:T(8,128)(2,1)S(1)} %pad_maximum_fusion), channel_id=1, source_target_pairs={{0,48},{8,56},{16,0},{24,8},{32,16},{40,24},{48,32},{56,40},{64,11... | collective-permute-start | bytes 2359304 | tf_op jit(solution)/shard_map/ppermute | solution.py:329
  55.1 16.5 %collective-permute-start.10 = (bf16[3,128,768]{2,1,0:T(8,128)(2,1)}, bf16[3,128,768]{2,1,0:T(8,128)(2,1)S(1)}, u32[]{:S(2)}, u32[]{:S(2)}) collective-permute-start(bf16[3,128,768]{2,1,0:T(8,128)(2,1)} %get-tuple-element.60), channel_id=1, source_target_pairs={{0,192},{8,200},{16,208},{24,216},{32,224},{40,232},{48,240},{56,2... | collective-permute-start | bytes 1769480 | tf_op jit(solution)/shard_map/ppermute | solution.py:329
  57.2 28.6 %collective-permute-start.8 = (bf16[3,128,768]{2,1,0:T(8,128)(2,1)}, bf16[3,128,768]{2,1,0:T(8,128)(2,1)S(1)}, u32[]{:S(2)}, u32[]{:S(2)}) collective-permute-start(bf16[3,128,768]{2,1,0:T(8,128)(2,1)} %get-tuple-element.58), channel_id=1, source_target_pairs={{0,64},{8,72},{16,80},{24,88},{32,96},{40,104},{48,112},{56,120},{... | collective-permute-start | bytes 1769480 | tf_op jit(solution)/shard_map/ppermute | solution.py:329
  57.2 28.6 %collective-permute-start.9 = (bf16[3,128,768]{2,1,0:T(8,128)(2,1)}, bf16[3,128,768]{2,1,0:T(8,128)(2,1)S(1)}, u32[]{:S(2)}, u32[]{:S(2)}) collective-permute-start(bf16[3,128,768]{2,1,0:T(8,128)(2,1)} %get-tuple-element.59), channel_id=1, source_target_pairs={{0,128},{8,136},{16,144},{24,152},{32,160},{40,168},{48,176},{56,1... | collective-permute-start | bytes 1769480 | tf_op jit(solution)/shard_map/ppermute | solution.py:329
  71.6 33.0 %copy-start.7 = (bf16[3,128,768]{2,1,0:T(8,128)(2,1)}, bf16[3,128,768]{2,1,0:T(8,128)(2,1)S(1)}, u32[]{:S(2)}) copy-start(bf16[3,128,768]{2,1,0:T(8,128)(2,1)S(1)} %collective-permute-done.10.refs_3_) | copy-start | bytes 1769476
  85.8 18.8 %copy-start.8 = (bf16[3,128,768]{2,1,0:T(8,128)(2,1)}, bf16[3,128,768]{2,1,0:T(8,128)(2,1)S(1)}, u32[]{:S(2)}) copy-start(bf16[3,128,768]{2,1,0:T(8,128)(2,1)S(1)} %collective-permute-done.8.refs_1_) | copy-start | bytes 1769476
  85.8 5.2 %copy-start.9 = (bf16[3,128,768]{2,1,0:T(8,128)(2,1)}, bf16[3,128,768]{2,1,0:T(8,128)(2,1)S(1)}, u32[]{:S(2)}) copy-start(bf16[3,128,768]{2,1,0:T(8,128)(2,1)S(1)} %collective-permute-done.9.refs_2_) | copy-start | bytes 1769476
  85.8 18.8 %copy-start.6 = (bf16[4,128,768]{2,1,0:T(8,128)(2,1)}, bf16[4,128,768]{2,1,0:T(8,128)(2,1)S(1)}, u32[]{:S(2)}) copy-start(bf16[4,128,768]{2,1,0:T(8,128)(2,1)S(1)} %collective-permute-done.7.refs_4_) | copy-start | bytes 2359300
  85.8 1.2 copy-start.5
  91.0 39.8 %all-to-all-start = ((bf16[4,2,128,768]{3,2,1,0:T(8,128)(2,1)}), bf16[4,2,128,768]{3,2,1,0:T(8,128)(2,1)S(1)}, u32[]{:S(2)}, u32[]{:S(2)}) async-start(bf16[4,2,128,768]{3,2,1,0:T(8,128)(2,1)} %get-tuple-element.75), calls=%async_computation | async-start | bytes 3145728 | tf_op jit(solution)/shard_map/all_to_all | solution.py:450
  94.6 19.2 %collective-permute-start.11 = (bf16[2,128,768]{2,1,0:T(8,128)(2,1)}, bf16[2,128,768]{2,1,0:T(8,128)(2,1)S(1)}, u32[]{:S(2)}, u32[]{:S(2)}) collective-permute-start(bf16[2,128,768]{2,1,0:T(8,128)(2,1)} %get-tuple-element.67.refs_5_), channel_id=1, source_target_pairs={{0,8},{8,16},{16,24},{24,32},{32,40},{40,48},{48,56},{56,0},{64,72... | collective-permute-start | bytes 1179656 | tf_op jit(solution)/shard_map/ppermute | solution.py:329
  96.1 23.4 %collective-permute-start.12 = (bf16[2,128,768]{2,1,0:T(8,128)(2,1)}, bf16[2,128,768]{2,1,0:T(8,128)(2,1)S(1)}, u32[]{:S(2)}, u32[]{:S(2)}) collective-permute-start(bf16[2,128,768]{2,1,0:T(8,128)(2,1)} %get-tuple-element.70), channel_id=1, source_target_pairs={{0,72},{8,80},{16,88},{24,96},{32,104},{40,112},{48,120},{56,64},{... | collective-permute-start | bytes 1179656 | tf_op jit(solution)/shard_map/ppermute | solution.py:329
  97.5 28.6 %collective-permute-start.13 = (bf16[2,128,768]{2,1,0:T(8,128)(2,1)}, bf16[2,128,768]{2,1,0:T(8,128)(2,1)S(1)}, u32[]{:S(2)}, u32[]{:S(2)}) collective-permute-start(bf16[2,128,768]{2,1,0:T(8,128)(2,1)} %get-tuple-element.73), channel_id=1, source_target_pairs={{0,200},{8,208},{16,216},{24,224},{32,232},{40,240},{48,248},{56,1... | collective-permute-start | bytes 1179656 | tf_op jit(solution)/shard_map/ppermute | solution.py:329
  101.4 29.1 %collective-permute-start.14 = (bf16[2,128,768]{2,1,0:T(8,128)(2,1)}, bf16[2,128,768]{2,1,0:T(8,128)(2,1)}, u32[]{:S(2)}, u32[]{:S(2)}) collective-permute-start(bf16[2,128,768]{2,1,0:T(8,128)(2,1)} %get-tuple-element.74), channel_id=1, source_target_pairs={{0,168},{8,176},{16,184},{24,128},{32,136},{40,144},{48,152},{56,1... | collective-permute-start | bytes 1179656 | tf_op jit(solution)/shard_map/ppermute | solution.py:329
  113.8 5.6 %copy-start.10 = (bf16[2,128,768]{2,1,0:T(8,128)(2,1)}, bf16[2,128,768]{2,1,0:T(8,128)(2,1)S(1)}, u32[]{:S(2)}) copy-start(bf16[2,128,768]{2,1,0:T(8,128)(2,1)S(1)} %collective-permute-done.11.refs_0_) | copy-start | bytes 1179652
  119.5 0.8 copy-start.11
  126.2 0.8 copy-start.12
  130.8 1.2 copy-start.3
  132.0 17.7 %copy-start.2 = (f32[8,512]{1,0:T(8,128)S(1)}, f32[8,512]{1,0:T(8,128)}, u32[]{:S(2)}) copy-start(f32[8,512]{1,0:T(8,128)} %get-tuple-element.49.local) | copy-start | bytes 49156
  132.0 26.0 %copy-start = (s32[344]{0:T(512)S(1)}, s32[344]{0:T(512)}, u32[]{:S(2)}) copy-start(s32[344]{0:T(512)} %plan.1) | copy-start | bytes 4132
  141.3 16.7 %all-to-all-start.1 = ((f32[32,2,128]{2,1,0:T(2,128)}), f32[32,2,128]{2,1,0:T(2,128)S(1)}, u32[]{:S(2)}, u32[]{:S(2)}) async-start(f32[32,2,128]{2,1,0:T(2,128)} %bitcast.8), calls=%async_computation.1 | async-start | bytes 65536 | tf_op jit(solution)/shard_map/all_to_all | solution.py:478
  148.2 1.5 collective-permute-start.15
  149.7 0.8 copy-start.1
  158.7 3.8 %collective-permute-start.16 = (f32[8,512]{1,0:T(8,128)S(1)}, f32[8,512]{1,0:T(8,128)S(1)}, u32[]{:S(2)}, u32[]{:S(2)}) collective-permute-start(f32[8,512]{1,0:T(8,128)S(1)} %merge.1.one), channel_id=1, source_target_pairs={{0,1},{1,2},{2,3},{3,0},{4,5},{5,6},{6,7},{7,4},{8,9},{9,10},{10,1... | collective-permute-start | bytes 49160 | tf_op jit(solution)/shard_map/ppermute | solution.py:499
  159.0 5.2 %collective-permute-start.17 = (f32[8,512]{1,0:T(8,128)S(1)}, f32[8,512]{1,0:T(8,128)S(1)}, u32[]{:S(2)}, u32[]{:S(2)}) collective-permute-start(f32[8,512]{1,0:T(8,128)S(1)} %merge.1.one), channel_id=1, source_target_pairs={{0,2},{1,3},{2,0},{3,1},{4,6},{5,7},{6,4},{7,5},{8,10},{9,11},{10,... | collective-permute-start | bytes 49160 | tf_op jit(solution)/shard_map/ppermute | solution.py:499
  161.6 4.9 %collective-permute-start.18 = (f32[8,512]{1,0:T(8,128)S(1)}, f32[8,512]{1,0:T(8,128)S(1)}, u32[]{:S(2)}, u32[]{:S(2)}) collective-permute-start(f32[8,512]{1,0:T(8,128)S(1)} %merge.1.one), channel_id=1, source_target_pairs={{0,3},{1,0},{2,1},{3,2},{4,7},{5,4},{6,5},{7,6},{8,11},{9,8},{10,9... | collective-permute-start | bytes 49160 | tf_op jit(solution)/shard_map/ppermute | solution.py:499
